TPU v7x, 32 devices: a whole 2x2x4 slice. The times are simulated.
32 devices in a mesh: dp: 4 (over y, x), tp: 8 (over z, core).
Axes of the slice: x: 2, y: 2, z: 4, core: 2. Of those that a mesh axis runs over, the one named last changes fastest.
Arguments:
- tokens: bfloat16 [8, 2048, 2048], P('dp', 'tp'), may hold values from -6 to 6
- segments: int32 [8, 2048], P('dp'), may hold values from 0 to 3, as said below
- first_gain: float32 [2048], replicated, may hold values from 0.5 to 1.5
- first_shift: float32 [2048], replicated, may hold values from -1.25 to 1.25
- in_weight: bfloat16 [2048, 3, 2048], P('dp', None, 'tp'), may hold values from -0.125 to 0.125
- in_bias: float32 [2, 2048], P(None, 'tp'), may hold values from -1.75 to 1.75
- out_weight: bfloat16 [2048, 2048], P('tp', 'dp'), may hold values from -0.5 to 0.5
- out_bias: float32 [2048], replicated, may hold values from -1.25 to 1.25
- second_gain: float32 [2048], replicated, may hold values from 0.5 to 1.5
- second_shift: float32 [2048], replicated, may hold values from -1.25 to 1.25
- up_weight: bfloat16 [2048, 8192], P('dp', 'tp'), may hold values from -0.125 to 0.125
- up_bias: float32 [8192], P('tp'), may hold values from -1.75 to 1.75
- down_weight: bfloat16 [8192, 2048], P('tp', 'dp'), may hold values from -0.0625 to 0.0625
- down_bias: float32 [2048], replicated, may hold values from -1.25 to 1.25
- cotangent: bfloat16 [8, 2048, 2048], P('dp', 'tp'), may hold values from -8 to 8
Outputs:
- mixed: bfloat16 [8, 2048, 2048], P('dp', 'tp')
- tokens_grad: bfloat16 [8, 2048, 2048], P('dp', 'tp')
- first_gain_grad: float32 [2048], replicated
- first_shift_grad: float32 [2048], replicated
- in_weight_grad: float32 [2048, 3, 2048], P('dp', None, 'tp')
- in_bias_grad: float32 [2, 2048], P(None, 'tp')
- out_weight_grad: float32 [2048, 2048], P('tp', 'dp')
- out_bias_grad: float32 [2048], replicated
- second_gain_grad: float32 [2048], replicated
- second_shift_grad: float32 [2048], replicated
- up_weight_grad: float32 [2048, 8192], P('dp', 'tp')
- up_bias_grad: float32 [8192], P('tp')
- down_weight_grad: float32 [8192, 2048], P('tp', 'dp')
- down_bias_grad: float32 [2048], replicated
Inputs may be any that keep to these rules, and one draw needn't show every extreme that they name: `segments`: within a row the numbers start at 0 and never fall. A row is either one sequence of 2048 positions (all 0) or four sequences of 512 positions (0 to 3). Among the 2 rows of one index of dp exactly one is a single sequence.
All inputs are finite; a program needn't handle non-finite values.
Results may differ from a plain program's by a relative error of at most 0.02.
Values may be sent and summed in bfloat16 or wider, within the bound.
A program may use at most 256 MiB of HBM per device.

v0:
```python
import jax
import jax.numpy as jnp
from jax import lax
from jax.sharding import PartitionSpec as P

HDIM = 128


EPSILON = 1e-05
MASKED = -1e30


def normalize(rows, gain, shift):
    center = rows - jnp.mean(rows, axis=-1, keepdims=True)
    inverse = lax.rsqrt(jnp.mean(center * center, axis=-1, keepdims=True) + EPSILON)
    scaled = center * inverse
    return (scaled * gain + shift, scaled, inverse)


def normalize_back(grad_normed, scaled, inverse, gain):
    weighted = grad_normed * gain
    return inverse * (
        weighted
        - jnp.mean(weighted, axis=-1, keepdims=True)
        - scaled * jnp.mean(weighted * scaled, axis=-1, keepdims=True)
    )


def to_heads(matrix, head_size):
    return matrix.reshape(matrix.shape[0], -1, head_size).transpose(1, 0, 2)


def from_heads(stacked):
    return stacked.transpose(1, 0, 2).reshape(stacked.shape[1], -1)


def block_scores(query, keys, seg, offset, block, factor):
    part = query[:, offset : offset + block]
    scores = factor * jnp.einsum("hqd,hkd->hqk", part, keys, preferred_element_type=jnp.float32)
    positions = jnp.arange(keys.shape[1])
    allowed = (seg[offset : offset + block, None] == seg[None, :]) & (
        positions[None, :] <= positions[offset : offset + block, None]
    )
    return (jnp.where(allowed[None], scores, MASKED), part)


def attend(query, keys, values, seg, factor):
    length = keys.shape[1]
    block = min(512, length)
    pieces = []
    totals = []
    for offset in range(0, length, block):
        scores, part = block_scores(query, keys, seg, offset, block, factor)
        top = jnp.max(scores, axis=-1, keepdims=True)
        expo = jnp.exp(scores - top)
        total = jnp.sum(expo, axis=-1, keepdims=True)
        probs = (expo / total).astype(jnp.bfloat16)
        pieces.append(jnp.einsum("hqk,hkd->hqd", probs, values, preferred_element_type=jnp.float32))
        totals.append(top + jnp.log(total))
    return (jnp.concatenate(pieces, 1), jnp.concatenate(totals, 1))


def attend_back(query, keys, values, seg, log_total, grad_out, factor):
    length = keys.shape[1]
    block = min(512, length)
    grad_keys = jnp.zeros(keys.shape, jnp.float32)
    grad_values = jnp.zeros(values.shape, jnp.float32)
    grad_query = []
    for offset in range(0, length, block):
        scores, part = block_scores(query, keys, seg, offset, block, factor)
        probs = jnp.exp(scores - log_total[:, offset : offset + block])
        probs_low = probs.astype(jnp.bfloat16)
        grad_part = grad_out[:, offset : offset + block]
        grad_probs = jnp.einsum(
            "hqd,hkd->hqk", grad_part, values, preferred_element_type=jnp.float32
        )
        grad_scores = probs * (grad_probs - jnp.sum(probs * grad_probs, axis=-1, keepdims=True))
        scores_low = grad_scores.astype(jnp.bfloat16)
        grad_query.append(
            factor
            * jnp.einsum("hqk,hkd->hqd", scores_low, keys, preferred_element_type=jnp.float32)
        )
        grad_keys = grad_keys + factor * jnp.einsum(
            "hqk,hqd->hkd", scores_low, part, preferred_element_type=jnp.float32
        )
        grad_values = grad_values + jnp.einsum(
            "hqk,hqd->hkd", probs_low, grad_part, preferred_element_type=jnp.float32
        )
    return (
        jnp.concatenate(grad_query, 1).astype(jnp.bfloat16),
        grad_keys.astype(jnp.bfloat16),
        grad_values.astype(jnp.bfloat16),
    )


def local(
    tokens,
    segments,
    first_gain,
    first_shift,
    in_weight,
    in_bias,
    out_weight,
    out_bias,
    second_gain,
    second_shift,
    up_weight,
    up_bias,
    down_weight,
    down_bias,
    cotangent,
):
    local_len = tokens.shape[1]
    width = tokens.shape[2]
    local_cols = in_weight.shape[2]
    local_hidden = up_weight.shape[1]
    factor = HDIM ** (-0.5)
    in_all, out_all, up_all, down_all = (
        lax.all_gather(in_weight, "dp", axis=0, tiled=True),
        lax.all_gather(out_weight, "dp", axis=1, tiled=True),
        lax.all_gather(up_weight, "dp", axis=0, tiled=True),
        lax.all_gather(down_weight, "dp", axis=1, tiled=True),
    )
    in_flat = in_all.reshape(width, 3 * local_cols)

    def one_batch(carry, item):
        accumulated, wide_sums, bias_in, bias_up = carry
        rows, seg, cot = item
        rows_f = rows.astype(jnp.float32)
        normed1, scaled1, inverse1 = normalize(rows_f, first_gain, first_shift)
        full1 = lax.all_gather(normed1.astype(jnp.bfloat16), "tp", axis=0, tiled=True)
        proj = jnp.dot(full1, in_flat, preferred_element_type=jnp.float32)
        query = to_heads((proj[:, :local_cols] + in_bias[0]).astype(jnp.bfloat16), HDIM)
        keys = to_heads(proj[:, local_cols : 2 * local_cols].astype(jnp.bfloat16), HDIM)
        values = to_heads((proj[:, 2 * local_cols :] + in_bias[1]).astype(jnp.bfloat16), HDIM)
        attended, log_total = attend(query, keys, values, seg, factor)
        attended_low = from_heads(attended).astype(jnp.bfloat16)
        piece = lax.slice_in_dim(attended_low, 0, local_len * lax.axis_size("tp"), axis=0)
        attn_part = lax.psum_scatter(
            jnp.dot(piece, out_all, preferred_element_type=jnp.float32).astype(jnp.bfloat16),
            "tp",
            scatter_dimension=0,
            tiled=True,
        ).astype(jnp.float32)
        resid = rows_f + attn_part + out_bias
        normed2, scaled2, inverse2 = normalize(resid, second_gain, second_shift)
        full2 = lax.all_gather(normed2.astype(jnp.bfloat16), "tp", axis=0, tiled=True)
        upward = jnp.dot(full2, up_all, preferred_element_type=jnp.float32) + up_bias
        active, gelu_pull = jax.vjp(jax.nn.gelu, upward)
        active_low = active.astype(jnp.bfloat16)
        piece = active_low
        mixed = (
            resid
            + lax.psum_scatter(
                jnp.dot(piece, down_all, preferred_element_type=jnp.float32).astype(jnp.bfloat16),
                "tp",
                scatter_dimension=0,
                tiled=True,
            ).astype(jnp.float32)
            + down_bias
        ).astype(jnp.bfloat16)
        cot_f = cot.astype(jnp.float32)
        cot_full = lax.all_gather(cot, "tp", axis=0, tiled=True)
        grad_down = jnp.einsum(
            "sf,sd->fd", active_low, cot_full, preferred_element_type=jnp.float32
        )
        grad_active = jnp.einsum(
            "sd,fd->sf", cot_full, down_all, preferred_element_type=jnp.float32
        )
        grad_upward = gelu_pull(grad_active)[0].astype(jnp.bfloat16)
        grad_up = jnp.einsum("sd,sf->df", full2, grad_upward, preferred_element_type=jnp.float32)
        piece = grad_upward
        grad_normed2 = lax.psum_scatter(
            jnp.einsum("sf,df->sd", piece, up_all, preferred_element_type=jnp.float32).astype(
                jnp.bfloat16
            ),
            "tp",
            scatter_dimension=0,
            tiled=True,
        ).astype(jnp.float32)
        grad_resid = cot_f + normalize_back(grad_normed2, scaled2, inverse2, second_gain)
        resid_full = lax.all_gather(grad_resid.astype(jnp.bfloat16), "tp", axis=0, tiled=True)
        grad_out = jnp.einsum(
            "sc,sd->cd", attended_low, resid_full, preferred_element_type=jnp.float32
        )
        grad_attended = to_heads(
            jnp.einsum("sd,cd->sc", resid_full, out_all, preferred_element_type=jnp.float32).astype(
                jnp.bfloat16
            ),
            HDIM,
        )
        grad_query, grad_keys, grad_values = attend_back(
            query, keys, values, seg, log_total, grad_attended, factor
        )
        grad_proj = jnp.concatenate(
            [from_heads(grad_query), from_heads(grad_keys), from_heads(grad_values)], 1
        )
        grad_in = jnp.einsum(
            "sd,sc->dc", full1, grad_proj, preferred_element_type=jnp.float32
        ).reshape(width, 3, local_cols)
        piece = lax.slice_in_dim(grad_proj, 0, local_len * lax.axis_size("tp"), axis=0)
        grad_normed1 = lax.psum_scatter(
            jnp.einsum("sc,dc->sd", piece, in_flat, preferred_element_type=jnp.float32).astype(
                jnp.bfloat16
            ),
            "tp",
            scatter_dimension=0,
            tiled=True,
        ).astype(jnp.float32)
        tokens_grad = (
            grad_resid + normalize_back(grad_normed1, scaled1, inverse1, first_gain)
        ).astype(jnp.bfloat16)
        wide_terms = jnp.stack(
            [
                jnp.sum(grad_normed1 * scaled1, 0),
                jnp.sum(grad_normed1, 0),
                jnp.sum(grad_resid, 0),
                jnp.sum(grad_normed2 * scaled2, 0),
                jnp.sum(grad_normed2, 0),
                jnp.sum(cot_f, 0),
            ]
        )
        in_terms = jnp.stack(
            [
                jnp.sum(grad_proj[:, :local_cols], 0, dtype=jnp.float32),
                jnp.sum(grad_proj[:, 2 * local_cols :], 0, dtype=jnp.float32),
            ]
        )
        up_terms = jnp.sum(grad_upward, 0, dtype=jnp.float32)
        matrix_terms = (grad_in, grad_out, grad_up, grad_down)
        matrix_terms = (
            lax.psum_scatter(
                matrix_terms[0].astype(jnp.bfloat16), "dp", scatter_dimension=0, tiled=True
            ).astype(jnp.float32),
            lax.psum_scatter(
                matrix_terms[1].astype(jnp.bfloat16), "dp", scatter_dimension=1, tiled=True
            ).astype(jnp.float32),
            lax.psum_scatter(
                matrix_terms[2].astype(jnp.bfloat16), "dp", scatter_dimension=0, tiled=True
            ).astype(jnp.float32),
            lax.psum_scatter(
                matrix_terms[3].astype(jnp.bfloat16), "dp", scatter_dimension=1, tiled=True
            ).astype(jnp.float32),
        )
        accumulated = tuple((a + b for a, b in zip(accumulated, matrix_terms)))
        return (
            (accumulated, wide_sums + wide_terms, bias_in + in_terms, bias_up + up_terms),
            (mixed, tokens_grad),
        )

    starting = tuple(
        (jnp.zeros(w.shape, jnp.float32) for w in (in_weight, out_weight, up_weight, down_weight))
    )
    initial = (
        starting,
        jnp.zeros((6, width), jnp.float32),
        jnp.zeros((2, local_cols), jnp.float32),
        jnp.zeros((local_hidden,), jnp.float32),
    )
    final, (mixed, tokens_grad) = lax.scan(one_batch, initial, (tokens, segments, cotangent))
    accumulated, wide_sums, bias_in, bias_up = final
    grad_in, grad_out, grad_up, grad_down = accumulated
    tp_at = lax.axis_index("tp")
    spread_in = lax.dynamic_update_slice(
        jnp.zeros((2, width), jnp.float32), bias_in, (0, tp_at * local_cols)
    )
    spread_up = lax.dynamic_update_slice(
        jnp.zeros((local_hidden * lax.axis_size("tp"),), jnp.float32),
        bias_up,
        (tp_at * local_hidden,),
    )
    summed_wide, summed_in, summed_up = lax.psum((wide_sums, spread_in, spread_up), ("dp", "tp"))
    in_bias_grad = lax.dynamic_slice_in_dim(summed_in, tp_at * local_cols, local_cols, 1)
    up_bias_grad = lax.dynamic_slice_in_dim(summed_up, tp_at * local_hidden, local_hidden, 0)
    return (
        mixed,
        tokens_grad,
        summed_wide[0],
        summed_wide[1],
        grad_in,
        in_bias_grad,
        grad_out,
        summed_wide[2],
        summed_wide[3],
        summed_wide[4],
        grad_up,
        up_bias_grad,
        grad_down,
        summed_wide[5],
    )


def solution(mesh):
    in_specs = (
        P("dp", "tp", None),
        P("dp", None),
        P(),
        P(),
        P("dp", None, "tp"),
        P(None, "tp"),
        P("tp", "dp"),
        P(),
        P(),
        P(),
        P("dp", "tp"),
        P("tp"),
        P("tp", "dp"),
        P(),
        P("dp", "tp", None),
    )
    out_specs = (
        P("dp", "tp", None),
        P("dp", "tp", None),
        P(),
        P(),
        P("dp", None, "tp"),
        P(None, "tp"),
        P("tp", "dp"),
        P(),
        P(),
        P(),
        P("dp", "tp"),
        P("tp"),
        P("tp", "dp"),
        P(),
    )
    return jax.shard_map(local, mesh=mesh, in_specs=in_specs, out_specs=out_specs, check_vma=False)
```

profile of v0, /device:TPU:0, one launch (start us, length us, event | category | flops | bytes accessed | tf_op | source)
XLA Modules:
  0.0 2300.1 jit_solution(10767682092705980549)
XLA Ops:
  11.8 45.2 %all-gather.13.cloned.1.call-done = bf16[2048,3,256]{0,2,1:T(8,128)(2,1)} async-done(((bf16[512,3,256]{0,2,1:T(8,128)(2,1)}), bf16[2048,3,256]{0,2,1:T(8,128)(2,1)}) %all-gather.13.cloned.1.call-update) | async-done | bytes 3145744 | tf_op jit(solution)/shard_map/all_gather | solution.py:119
  57.0 4.6 copy.58
  61.6 23.7 %all-gather.15.cloned.1.call-done = bf16[256,2048]{1,0:T(8,128)(2,1)} async-done(((bf16[256,512]{1,0:T(8,128)(2,1)}), bf16[256,2048]{1,0:T(8,128)(2,1)}) %all-gather.15.cloned.1.call-update) | async-done | bytes 1048592 | tf_op jit(solution)/shard_map/all_gather | solution.py:120
  85.3 54.6 %all-gather.19.cloned.1.call-done = bf16[2048,1024]{1,0:T(8,128)(2,1)} async-done(((bf16[512,1024]{1,0:T(8,128)(2,1)}), bf16[2048,1024]{1,0:T(8,128)(2,1)}) %all-gather.19.cloned.1.call-update) | async-done | bytes 4194320 | tf_op jit(solution)/shard_map/all_gather | solution.py:121
  139.9 54.3 %all-gather.17.cloned.1.call-done = bf16[1024,2048]{1,0:T(8,128)(2,1)} async-done(((bf16[1024,512]{1,0:T(8,128)(2,1)}), bf16[1024,2048]{1,0:T(8,128)(2,1)}) %all-gather.17.cloned.1.call-update) | async-done | bytes 4194320 | tf_op jit(solution)/shard_map/all_gather | solution.py:122
  194.2 1967.9 %while.29 = (s32[]{:T(128)}, f32[512,3,256]{0,2,1:T(8,128)}, f32[256,512]{1,0:T(8,128)}, f32[512,1024]{1,0:T(8,128)}, f32[1024,512]{1,0:T(8,128)}, /*index=5*/f3...) while((s32[]{:T(128)}, f32[512,3,256]{0,2,1:T(8,128)}, ...), condition=%wide.region_38.39_spmd.clone, body=%wide.region_0.38_spmd.clone.sunk | while | flops 90555023360 | bytes 1361523712 | solution.py:260
  200.4 5.5 fusion.304
  205.9 74.3 %all-gather.21.cloned.1.call-done = bf16[2048,2048]{1,0:T(8,128)(2,1)} async-done(((bf16[256,2048]{1,0:T(8,128)(2,1)}), bf16[2048,2048]{1,0:T(8,128)(2,1)}) %all-gather.21.cloned.1.call-update) | async-done | bytes 8388624 | tf_op jit(solution)/shard_map/while/body/eval_jaxpr/all_gather | solution.py:131
  280.2 10.4 fusion.301
  328.1 7.2 convolution_convert_fusion.16
  335.4 88.3 %reduce-scatter.9.cloned.1.call-done = bf16[256,2048]{1,0:T(8,128)(2,1)} async-done(((bf16[2048,2048]{1,0:T(8,128)(2,1)}), bf16[256,2048]{1,0:T(8,128)(2,1)}) %reduce-scatter.9.cloned.1.call-update) | async-done | bytes 1048592 | tf_op jit(solution)/shard_map/while/body/eval_jaxpr/reduce_scatter | solution.py:139
  432.1 77.4 %all-gather.23.cloned.1.call-done = bf16[2048,2048]{1,0:T(8,128)(2,1)} async-done(((bf16[256,2048]{1,0:T(8,128)(2,1)}), bf16[2048,2048]{1,0:T(8,128)(2,1)}) %all-gather.23.cloned.1.call-update) | async-done | bytes 8388624 | tf_op jit(solution)/shard_map/while/body/eval_jaxpr/all_gather | solution.py:147
  509.4 14.4 fusion.318
  523.8 67.8 %all-gather.25.cloned.1.call-done = bf16[1,2048,2048]{2,1,0:T(8,128)(2,1)} async-done(((bf16[1,256,2048]{2,1,0:T(8,128)(2,1)}), bf16[1,2048,2048]{2,1,0:T(8,128)(2,1)}) %all-gather.25.cloned.1.call-update) | async-done | bytes 8388624 | tf_op jit(solution)/shard_map/while/body/eval_jaxpr/all_gather | solution.py:163
  591.6 20.8 convert_reduce_fusion.14
  614.4 11.2 convolution_convert_fusion.17
  625.6 88.3 %reduce-scatter.11.cloned.1.call-done = bf16[256,2048]{1,0:T(8,128)(2,1)} async-done(((bf16[2048,2048]{1,0:T(8,128)(2,1)}), bf16[256,2048]{1,0:T(8,128)(2,1)}) %reduce-scatter.11.cloned.1.call-update) | async-done | bytes 1048592 | tf_op jit(solution)/shard_map/while/body/eval_jaxpr/reduce_scatter | solution.py:173
  723.0 16.5 fusion.330
  739.7 14.6 convolution_convert_fusion.21
  754.3 49.2 %all-gather.27.cloned.1.call-done = bf16[2048,2048]{1,0:T(8,128)(2,1)} async-done(((bf16[256,2048]{1,0:T(8,128)(2,1)}), bf16[2048,2048]{1,0:T(8,128)(2,1)}) %all-gather.27.cloned.1.call-update) | async-done | bytes 8388624 | tf_op jit(solution)/shard_map/while/body/eval_jaxpr/all_gather | solution.py:182
  803.5 5.7 convolution_convert_fusion.18
  810.1 5.3 multiply_reduce_fusion.11
  815.4 4.8 multiply_convert_fusion.15
  828.1 4.6 fusion.326
  837.7 4.4 fusion.327
  867.0 8.0 fusion.323
  876.3 6.2 convert_reduce_fusion.15
  882.4 10.6 convolution_convert_fusion.19
  893.1 10.9 convolution_convert_fusion.22
  904.1 15.7 convolution_convert_fusion.23
  928.0 16.2 reduce-scatter.15.cloned.1.call-done
  946.0 45.3 %reduce-scatter.13.cloned.1.call-done = bf16[512,3,256]{0,2,1:T(8,128)(2,1)} async-done(((bf16[2048,3,256]{0,2,1:T(8,128)(2,1)}), bf16[512,3,256]{0,2,1:T(8,128)(2,1)}) %reduce-scatter.13.cloned.1.call-update) | async-done | bytes 786448 | tf_op jit(solution)/shard_map/while/body/eval_jaxpr/reduce_scatter | solution.py:232
  993.8 89.3 %reduce-scatter.21.cloned.1.call-done = bf16[256,2048]{1,0:T(8,128)(2,1)} async-done(((bf16[2048,2048]{1,0:T(8,128)(2,1)}), bf16[256,2048]{1,0:T(8,128)(2,1)}) %reduce-scatter.21.cloned.1.call-update) | async-done | bytes 1048592 | tf_op jit(solution)/shard_map/while/body/eval_jaxpr/reduce_scatter | solution.py:202
  1085.6 87.8 %reduce-scatter.23.cloned.1.call-done = bf16[256,2048]{1,0:T(8,128)(2,1)} async-done(((bf16[2048,2048]{1,0:T(8,128)(2,1)}), bf16[256,2048]{1,0:T(8,128)(2,1)}) %reduce-scatter.23.cloned.1.call-update) | async-done | bytes 1048592 | tf_op jit(solution)/shard_map/while/body/eval_jaxpr/reduce_scatter | solution.py:154
  1173.4 4.9 fusion.332
  1184.4 5.5 fusion.304
  1189.9 72.7 %all-gather.21.cloned.1.call-done = bf16[2048,2048]{1,0:T(8,128)(2,1)} async-done(((bf16[256,2048]{1,0:T(8,128)(2,1)}), bf16[2048,2048]{1,0:T(8,128)(2,1)}) %all-gather.21.cloned.1.call-update) | async-done | bytes 8388624 | tf_op jit(solution)/shard_map/while/body/eval_jaxpr/all_gather | solution.py:131
  1262.6 10.4 fusion.301
  1310.3 7.2 convolution_convert_fusion.16
  1317.6 88.2 %reduce-scatter.9.cloned.1.call-done = bf16[256,2048]{1,0:T(8,128)(2,1)} async-done(((bf16[2048,2048]{1,0:T(8,128)(2,1)}), bf16[256,2048]{1,0:T(8,128)(2,1)}) %reduce-scatter.9.cloned.1.call-update) | async-done | bytes 1048592 | tf_op jit(solution)/shard_map/while/body/eval_jaxpr/reduce_scatter | solution.py:139
  1414.3 77.4 %all-gather.23.cloned.1.call-done = bf16[2048,2048]{1,0:T(8,128)(2,1)} async-done(((bf16[256,2048]{1,0:T(8,128)(2,1)}), bf16[2048,2048]{1,0:T(8,128)(2,1)}) %all-gather.23.cloned.1.call-update) | async-done | bytes 8388624 | tf_op jit(solution)/shard_map/while/body/eval_jaxpr/all_gather | solution.py:147
  1491.7 14.4 fusion.318
  1506.0 67.7 %all-gather.25.cloned.1.call-done = bf16[1,2048,2048]{2,1,0:T(8,128)(2,1)} async-done(((bf16[1,256,2048]{2,1,0:T(8,128)(2,1)}), bf16[1,2048,2048]{2,1,0:T(8,128)(2,1)}) %all-gather.25.cloned.1.call-update) | async-done | bytes 8388624 | tf_op jit(solution)/shard_map/while/body/eval_jaxpr/all_gather | solution.py:163
  1573.7 20.8 convert_reduce_fusion.14
  1596.5 11.2 convolution_convert_fusion.17
  1607.7 88.3 %reduce-scatter.11.cloned.1.call-done = bf16[256,2048]{1,0:T(8,128)(2,1)} async-done(((bf16[2048,2048]{1,0:T(8,128)(2,1)}), bf16[256,2048]{1,0:T(8,128)(2,1)}) %reduce-scatter.11.cloned.1.call-update) | async-done | bytes 1048592 | tf_op jit(solution)/shard_map/while/body/eval_jaxpr/reduce_scatter | solution.py:173
  1705.1 16.5 fusion.330
  1721.8 14.6 convolution_convert_fusion.21
  1736.4 49.2 %all-gather.27.cloned.1.call-done = bf16[2048,2048]{1,0:T(8,128)(2,1)} async-done(((bf16[256,2048]{1,0:T(8,128)(2,1)}), bf16[2048,2048]{1,0:T(8,128)(2,1)}) %all-gather.27.cloned.1.call-update) | async-done | bytes 8388624 | tf_op jit(solution)/shard_map/while/body/eval_jaxpr/all_gather | solution.py:182
  1785.6 5.7 convolution_convert_fusion.18
  1792.2 5.3 multiply_reduce_fusion.11
  1797.5 4.8 multiply_convert_fusion.15
  1810.2 4.6 fusion.326
  1849.0 8.0 fusion.323
  1858.3 6.2 convert_reduce_fusion.15
  1864.5 10.6 convolution_convert_fusion.19
  1875.2 10.9 convolution_convert_fusion.22
  1886.2 15.7 convolution_convert_fusion.23
  1910.7 15.6 reduce-scatter.15.cloned.1.call-done
  1928.2 45.1 %reduce-scatter.13.cloned.1.call-done = bf16[512,3,256]{0,2,1:T(8,128)(2,1)} async-done(((bf16[2048,3,256]{0,2,1:T(8,128)(2,1)}), bf16[512,3,256]{0,2,1:T(8,128)(2,1)}) %reduce-scatter.13.cloned.1.call-update) | async-done | bytes 786448 | tf_op jit(solution)/shard_map/while/body/eval_jaxpr/reduce_scatter | solution.py:232
  1976.4 88.8 %reduce-scatter.21.cloned.1.call-done = bf16[256,2048]{1,0:T(8,128)(2,1)} async-done(((bf16[2048,2048]{1,0:T(8,128)(2,1)}), bf16[256,2048]{1,0:T(8,128)(2,1)}) %reduce-scatter.21.cloned.1.call-update) | async-done | bytes 1048592 | tf_op jit(solution)/shard_map/while/body/eval_jaxpr/reduce_scatter | solution.py:202
  2067.7 87.9 %reduce-scatter.23.cloned.1.call-done = bf16[256,2048]{1,0:T(8,128)(2,1)} async-done(((bf16[2048,2048]{1,0:T(8,128)(2,1)}), bf16[256,2048]{1,0:T(8,128)(2,1)}) %reduce-scatter.23.cloned.1.call-update) | async-done | bytes 1048592 | tf_op jit(solution)/shard_map/while/body/eval_jaxpr/reduce_scatter | solution.py:154
  2155.6 4.9 fusion.332
  2167.4 121.6 %all-reduce.3.cloned.1.call-done = (f32[6,2048]{1,0:T(8,128)}, f32[2,2048]{1,0:T(2,128)}, f32[8192]{0:T(1024)}) async-done(((f32[6,2048]{1,0:T(8,128)}, f32[2,2048]{1,0:T(2,128)}, f32[8192]{0:T(1024)}), (f32[6,2048]{1,0:T(8,128)}, f32[2,2048]{1,0:T(2,128)}, f32[8192]{0:T(1024)})) %all-reduce.3.cloned.1.call-update) | async-done | bytes 98320 | tf_op jit(solution)/shard_map/psum | solution.py:272
  (493 shorter events, 254.2 us)
Async XLA Ops:
  7.2 49.8 %all-gather.13.cloned.1.call-start = ((), (), s32[]{:S(2)}) async-start(), calls=%async_computation.8 | async-start | bytes 3932160 | tf_op jit(solution)/shard_map/all_gather | solution.py:119
  9.5 75.8 %all-gather.15.cloned.1.call-start = ((), (), s32[]{:S(2)}) async-start(), calls=%async_computation.9 | async-start | bytes 1310720 | tf_op jit(solution)/shard_map/all_gather | solution.py:120
  10.3 183.9 %copy-start.4 = (bf16[2,256,2048]{2,1,0:T(8,128)(2,1)S(1)}, bf16[2,256,2048]{2,1,0:T(8,128)(2,1)}, u32[]{:S(2)}) copy-start(bf16[2,256,2048]{2,1,0:T(8,128)(2,1)} %param.17) | copy-start | bytes 6291460
  10.3 183.9 %copy-start.30 = (f32[2048]{0:T(1024)S(1)}, f32[2048]{0:T(1024)}, u32[]{:S(2)}) copy-start(f32[2048]{0:T(1024)} %param.24) | copy-start | bytes 24580
  10.3 183.9 %copy-start.37 = (f32[2048]{0:T(1024)S(1)}, f32[2048]{0:T(1024)}, u32[]{:S(2)}) copy-start(f32[2048]{0:T(1024)} %param.25) | copy-start | bytes 24580
  10.3 183.9 %copy-start.47 = (f32[2048]{0:T(1024)S(1)}, f32[2048]{0:T(1024)}, u32[]{:S(2)}) copy-start(f32[2048]{0:T(1024)} %param.26) | copy-start | bytes 24580
  10.3 183.9 %copy-start.58 = (f32[1024]{0:T(1024)S(1)}, f32[1024]{0:T(1024)}, u32[]{:S(2)}) copy-start(f32[1024]{0:T(1024)} %param.28) | copy-start | bytes 12292
  10.4 129.6 %all-gather.19.cloned.1.call-start = ((), (), s32[]{:S(2)}) async-start(), calls=%async_computation.11 | async-start | bytes 5242880 | tf_op jit(solution)/shard_map/all_gather | solution.py:121
  11.1 183.1 %all-gather.17.cloned.1.call-start = ((), (), s32[]{:S(2)}) async-start(), calls=%async_computation.10 | async-start | bytes 5242880 | tf_op jit(solution)/shard_map/all_gather | solution.py:122
  194.5 85.7 %all-gather.21.cloned.1.call-start = ((), (), s32[]{:S(2)}) async-start(), calls=%async_computation.13 | async-start | bytes 9437184 | tf_op jit(solution)/shard_map/while/body/eval_jaxpr/all_gather | solution.py:131
  198.0 225.7 %reduce-scatter.9.cloned.1.call-start = ((), (), s32[]{:S(2)}) async-start(), calls=%async_computation.14 | async-start | bytes 9437184 | tf_op jit(solution)/shard_map/while/body/eval_jaxpr/reduce_scatter | solution.py:139
  335.4 174.1 %all-gather.23.cloned.1.call-start = ((), (), s32[]{:S(2)}) async-start(), calls=%async_computation.15 | async-start | bytes 9437184 | tf_op jit(solution)/shard_map/while/body/eval_jaxpr/all_gather | solution.py:147
  428.9 162.8 %all-gather.25.cloned.1.call-start = ((), (), s32[]{:S(2)}) async-start(), calls=%async_computation.16 | async-start | bytes 9437184 | tf_op jit(solution)/shard_map/while/body/eval_jaxpr/all_gather | solution.py:163
  432.0 281.9 %reduce-scatter.11.cloned.1.call-start = ((), (), s32[]{:S(2)}) async-start(), calls=%async_computation.17 | async-start | bytes 9437184 | tf_op jit(solution)/shard_map/while/body/eval_jaxpr/reduce_scatter | solution.py:173
  625.6 177.9 %all-gather.27.cloned.1.call-start = ((), (), s32[]{:S(2)}) async-start(), calls=%async_computation.18 | async-start | bytes 9437184 | tf_op jit(solution)/shard_map/while/body/eval_jaxpr/all_gather | solution.py:182
  722.9 197.6 %reduce-scatter.19.cloned.1.call-start = ((), (), s32[]{:S(2)}) async-start(), calls=%async_computation.22 | async-start | bytes 5242880 | tf_op jit(solution)/shard_map/while/body/eval_jaxpr/reduce_scatter | solution.py:241
  739.5 183.8 %reduce-scatter.17.cloned.1.call-start = ((), (), s32[]{:S(2)}) async-start(), calls=%async_computation.21 | async-start | bytes 5242880 | tf_op jit(solution)/shard_map/while/body/eval_jaxpr/reduce_scatter | solution.py:238
  754.2 49.3 %copy-start.21 = (bf16[256,2048]{1,0:T(8,128)(2,1)S(1)}, bf16[256,2048]{1,0:T(8,128)(2,1)}, u32[]{:S(2)}) copy-start(bf16[256,2048]{1,0:T(8,128)(2,1)} %get-tuple-element.910) | copy-start | bytes 3145732 | tf_op jit(solution)/shard_map/while
  754.3 55.8 %copy-start.9 = (bf16[2048,2,128]{2,0,1:T(8,128)(2,1)S(1)}, bf16[2048,2,128]{2,0,1:T(8,128)(2,1)}, u32[]{:S(2)}) copy-start(bf16[2048,2,128]{2,0,1:T(8,128)(2,1)} %copy-done.8) | copy-start | bytes 3145732 | tf_op jit(solution)/shard_map/while
  754.3 189.9 %reduce-scatter.15.cloned.1.call-start = ((), (), s32[]{:S(2)}) async-start(), calls=%async_computation.20 | async-start | bytes 1310720 | tf_op jit(solution)/shard_map/while/body/eval_jaxpr/reduce_scatter | solution.py:235
  867.0 124.3 %reduce-scatter.13.cloned.1.call-start = ((), (), s32[]{:S(2)}) async-start(), calls=%async_computation.19 | async-start | bytes 3932160 | tf_op jit(solution)/shard_map/while/body/eval_jaxpr/reduce_scatter | solution.py:232
  893.1 190.1 %reduce-scatter.21.cloned.1.call-start = ((), (), s32[]{:S(2)}) async-start(), calls=%async_computation.23 | async-start | bytes 9437184 | tf_op jit(solution)/shard_map/while/body/eval_jaxpr/reduce_scatter | solution.py:202
  904.0 269.4 %reduce-scatter.23.cloned.1.call-start = ((), (), s32[]{:S(2)}) async-start(), calls=%async_computation.24 | async-start | bytes 9437184 | tf_op jit(solution)/shard_map/while/body/eval_jaxpr/reduce_scatter | solution.py:154
  924.7 158.5 %copy-start.5 = (bf16[2,256,2048]{2,1,0:T(8,128)(2,1)S(1)}, bf16[2,256,2048]{2,1,0:T(8,128)(2,1)}, u32[]{:S(2)}) copy-start(bf16[2,256,2048]{2,1,0:T(8,128)(2,1)} %get-tuple-element.975) | copy-start | bytes 6291460 | tf_op jit(solution)/shard_map/while
  924.7 158.5 %copy-start.44 = (f32[256]{0:T(256)S(1)}, f32[256]{0:T(256)}, u32[]{:S(2)}) copy-start(f32[256]{0:T(256)} %copy-done.43) | copy-start | bytes 3076 | tf_op jit(solution)/shard_map/while
  924.7 158.5 %copy-start.46 = (f32[256]{0:T(256)S(1)}, f32[256]{0:T(256)}, u32[]{:S(2)}) copy-start(f32[256]{0:T(256)} %copy-done.45) | copy-start | bytes 3076 | tf_op jit(solution)/shard_map/while
  927.8 157.6 %copy-start.39 = (f32[2048]{0:T(1024)S(1)}, f32[2048]{0:T(1024)}, u32[]{:S(2)}) copy-start(f32[2048]{0:T(1024)} %get-tuple-element.825) | copy-start | bytes 24580 | tf_op jit(solution)/shard_map/while
  927.8 157.6 %copy-start.40 = (f32[2048]{0:T(1024)S(1)}, f32[2048]{0:T(1024)}, u32[]{:S(2)}) copy-start(f32[2048]{0:T(1024)} %get-tuple-element.823) | copy-start | bytes 24580 | tf_op jit(solution)/shard_map/while
  927.8 157.6 %copy-start.41 = (f32[2048]{0:T(1024)S(1)}, f32[2048]{0:T(1024)}, u32[]{:S(2)}) copy-start(f32[2048]{0:T(1024)} %get-tuple-element.824) | copy-start | bytes 24580 | tf_op jit(solution)/shard_map/while
  927.9 157.6 %copy-start.42 = (f32[2048]{0:T(1024)S(1)}, f32[2048]{0:T(1024)}, u32[]{:S(2)}) copy-start(f32[2048]{0:T(1024)} %get-tuple-element.822) | copy-start | bytes 24580 | tf_op jit(solution)/shard_map/while
  927.9 157.7 %copy-start.35 = (f32[6,2048]{1,0:T(8,128)S(1)}, f32[6,2048]{1,0:T(8,128)}, u32[]{:S(2)}) copy-start(f32[6,2048]{1,0:T(8,128)} %get-tuple-element.868) | copy-start | bytes 147460 | tf_op jit(solution)/shard_map/while
  927.9 245.5 %copy-start.7 = (bf16[256,2048]{1,0:T(8,128)(2,1)S(1)}, bf16[256,2048]{1,0:T(8,128)(2,1)}, u32[]{:S(2)}) copy-start(bf16[256,2048]{1,0:T(8,128)(2,1)} %reduce-scatter.9.cloned.1.call-done) | copy-start | bytes 3145732 | tf_op jit(solution)/shard_map/while
  927.9 245.5 %copy-start.31 = (f32[2048]{0:T(1024)S(1)}, f32[2048]{0:T(1024)}, u32[]{:S(2)}) copy-start(f32[2048]{0:T(1024)} %get-tuple-element.1039) | copy-start | bytes 24580 | tf_op jit(solution)/shard_map/while
  927.9 245.5 %copy-start.49 = (f32[2048]{0:T(1024)S(1)}, f32[2048]{0:T(1024)}, u32[]{:S(2)}) copy-start(f32[2048]{0:T(1024)} %get-tuple-element.917) | copy-start | bytes 24580 | tf_op jit(solution)/shard_map/while
  927.9 250.4 %copy-start.55 = (f32[2,256]{1,0:T(2,128)}, f32[2,256]{1,0:T(2,128)S(1)}, u32[]{:S(2)}) copy-start(f32[2,256]{1,0:T(2,128)S(1)} %maximum_add_fusion.2) | copy-start | bytes 6148 | tf_op jit(solution)/shard_map/while
  1085.6 92.7 %copy-start.36 = (f32[6,2048]{1,0:T(8,128)}, f32[6,2048]{1,0:T(8,128)S(1)}, u32[]{:S(2)}) copy-start(f32[6,2048]{1,0:T(8,128)S(1)} %select_add_fusion.16) | copy-start | bytes 147460 | tf_op jit(solution)/shard_map/while
  1178.6 84.0 %all-gather.21.cloned.1.call-start = ((), (), s32[]{:S(2)}) async-start(), calls=%async_computation.13 | async-start | bytes 9437184 | tf_op jit(solution)/shard_map/while/body/eval_jaxpr/all_gather | solution.py:131
  1182.0 223.8 %reduce-scatter.9.cloned.1.call-start = ((), (), s32[]{:S(2)}) async-start(), calls=%async_computation.14 | async-start | bytes 9437184 | tf_op jit(solution)/shard_map/while/body/eval_jaxpr/reduce_scatter | solution.py:139
  1317.6 174.1 %all-gather.23.cloned.1.call-start = ((), (), s32[]{:S(2)}) async-start(), calls=%async_computation.15 | async-start | bytes 9437184 | tf_op jit(solution)/shard_map/while/body/eval_jaxpr/all_gather | solution.py:147
  1411.1 162.6 %all-gather.25.cloned.1.call-start = ((), (), s32[]{:S(2)}) async-start(), calls=%async_computation.16 | async-start | bytes 9437184 | tf_op jit(solution)/shard_map/while/body/eval_jaxpr/all_gather | solution.py:163
  1414.2 281.7 %reduce-scatter.11.cloned.1.call-start = ((), (), s32[]{:S(2)}) async-start(), calls=%async_computation.17 | async-start | bytes 9437184 | tf_op jit(solution)/shard_map/while/body/eval_jaxpr/reduce_scatter | solution.py:173
  1607.7 177.9 %all-gather.27.cloned.1.call-start = ((), (), s32[]{:S(2)}) async-start(), calls=%async_computation.18 | async-start | bytes 9437184 | tf_op jit(solution)/shard_map/while/body/eval_jaxpr/all_gather | solution.py:182
  1705.0 197.6 %reduce-scatter.19.cloned.1.call-start = ((), (), s32[]{:S(2)}) async-start(), calls=%async_computation.22 | async-start | bytes 5242880 | tf_op jit(solution)/shard_map/while/body/eval_jaxpr/reduce_scatter | solution.py:241
  1721.6 183.8 %reduce-scatter.17.cloned.1.call-start = ((), (), s32[]{:S(2)}) async-start(), calls=%async_computation.21 | async-start | bytes 5242880 | tf_op jit(solution)/shard_map/while/body/eval_jaxpr/reduce_scatter | solution.py:238
  1736.3 49.3 %copy-start.21 = (bf16[256,2048]{1,0:T(8,128)(2,1)S(1)}, bf16[256,2048]{1,0:T(8,128)(2,1)}, u32[]{:S(2)}) copy-start(bf16[256,2048]{1,0:T(8,128)(2,1)} %get-tuple-element.910) | copy-start | bytes 3145732 | tf_op jit(solution)/shard_map/while
  1736.3 55.8 %copy-start.9 = (bf16[2048,2,128]{2,0,1:T(8,128)(2,1)S(1)}, bf16[2048,2,128]{2,0,1:T(8,128)(2,1)}, u32[]{:S(2)}) copy-start(bf16[2048,2,128]{2,0,1:T(8,128)(2,1)} %copy-done.8) | copy-start | bytes 3145732 | tf_op jit(solution)/shard_map/while
  1736.3 189.9 %reduce-scatter.15.cloned.1.call-start = ((), (), s32[]{:S(2)}) async-start(), calls=%async_computation.20 | async-start | bytes 1310720 | tf_op jit(solution)/shard_map/while/body/eval_jaxpr/reduce_scatter | solution.py:235
  1849.0 124.4 %reduce-scatter.13.cloned.1.call-start = ((), (), s32[]{:S(2)}) async-start(), calls=%async_computation.19 | async-start | bytes 3932160 | tf_op jit(solution)/shard_map/while/body/eval_jaxpr/reduce_scatter | solution.py:232
  1875.1 190.1 %reduce-scatter.21.cloned.1.call-start = ((), (), s32[]{:S(2)}) async-start(), calls=%async_computation.23 | async-start | bytes 9437184 | tf_op jit(solution)/shard_map/while/body/eval_jaxpr/reduce_scatter | solution.py:202
  1886.1 269.5 %reduce-scatter.23.cloned.1.call-start = ((), (), s32[]{:S(2)}) async-start(), calls=%async_computation.24 | async-start | bytes 9437184 | tf_op jit(solution)/shard_map/while/body/eval_jaxpr/reduce_scatter | solution.py:154
  1906.7 158.5 %copy-start.5 = (bf16[2,256,2048]{2,1,0:T(8,128)(2,1)S(1)}, bf16[2,256,2048]{2,1,0:T(8,128)(2,1)}, u32[]{:S(2)}) copy-start(bf16[2,256,2048]{2,1,0:T(8,128)(2,1)} %get-tuple-element.975) | copy-start | bytes 6291460 | tf_op jit(solution)/shard_map/while
  1906.7 158.5 %copy-start.44 = (f32[256]{0:T(256)S(1)}, f32[256]{0:T(256)}, u32[]{:S(2)}) copy-start(f32[256]{0:T(256)} %copy-done.43) | copy-start | bytes 3076 | tf_op jit(solution)/shard_map/while
  1906.7 158.5 %copy-start.46 = (f32[256]{0:T(256)S(1)}, f32[256]{0:T(256)}, u32[]{:S(2)}) copy-start(f32[256]{0:T(256)} %copy-done.45) | copy-start | bytes 3076 | tf_op jit(solution)/shard_map/while
  1910.5 156.9 %copy-start.39 = (f32[2048]{0:T(1024)S(1)}, f32[2048]{0:T(1024)}, u32[]{:S(2)}) copy-start(f32[2048]{0:T(1024)} %get-tuple-element.825) | copy-start | bytes 24580 | tf_op jit(solution)/shard_map/while
  1910.5 156.9 %copy-start.40 = (f32[2048]{0:T(1024)S(1)}, f32[2048]{0:T(1024)}, u32[]{:S(2)}) copy-start(f32[2048]{0:T(1024)} %get-tuple-element.823) | copy-start | bytes 24580 | tf_op jit(solution)/shard_map/while
  1910.5 157.0 %copy-start.41 = (f32[2048]{0:T(1024)S(1)}, f32[2048]{0:T(1024)}, u32[]{:S(2)}) copy-start(f32[2048]{0:T(1024)} %get-tuple-element.824) | copy-start | bytes 24580 | tf_op jit(solution)/shard_map/while
  1910.6 157.0 %copy-start.42 = (f32[2048]{0:T(1024)S(1)}, f32[2048]{0:T(1024)}, u32[]{:S(2)}) copy-start(f32[2048]{0:T(1024)} %get-tuple-element.822) | copy-start | bytes 24580 | tf_op jit(solution)/shard_map/while
  1910.6 157.1 %copy-start.35 = (f32[6,2048]{1,0:T(8,128)S(1)}, f32[6,2048]{1,0:T(8,128)}, u32[]{:S(2)}) copy-start(f32[6,2048]{1,0:T(8,128)} %get-tuple-element.868) | copy-start | bytes 147460 | tf_op jit(solution)/shard_map/while
  1910.6 245.0 %copy-start.7 = (bf16[256,2048]{1,0:T(8,128)(2,1)S(1)}, bf16[256,2048]{1,0:T(8,128)(2,1)}, u32[]{:S(2)}) copy-start(bf16[256,2048]{1,0:T(8,128)(2,1)} %reduce-scatter.9.cloned.1.call-done) | copy-start | bytes 3145732 | tf_op jit(solution)/shard_map/while
  1910.6 245.0 %copy-start.31 = (f32[2048]{0:T(1024)S(1)}, f32[2048]{0:T(1024)}, u32[]{:S(2)}) copy-start(f32[2048]{0:T(1024)} %get-tuple-element.1039) | copy-start | bytes 24580 | tf_op jit(solution)/shard_map/while
  1910.6 245.0 %copy-start.49 = (f32[2048]{0:T(1024)S(1)}, f32[2048]{0:T(1024)}, u32[]{:S(2)}) copy-start(f32[2048]{0:T(1024)} %get-tuple-element.917) | copy-start | bytes 24580 | tf_op jit(solution)/shard_map/while
  1910.6 249.9 %copy-start.55 = (f32[2,256]{1,0:T(2,128)}, f32[2,256]{1,0:T(2,128)S(1)}, u32[]{:S(2)}) copy-start(f32[2,256]{1,0:T(2,128)S(1)} %maximum_add_fusion.2) | copy-start | bytes 6148 | tf_op jit(solution)/shard_map/while
  2067.7 92.8 %copy-start.36 = (f32[6,2048]{1,0:T(8,128)}, f32[6,2048]{1,0:T(8,128)S(1)}, u32[]{:S(2)}) copy-start(f32[6,2048]{1,0:T(8,128)S(1)} %select_add_fusion.16) | copy-start | bytes 147460 | tf_op jit(solution)/shard_map/while
  2162.1 127.0 %all-reduce.3.cloned.1.call-start = ((), (), s32[]{:S(2)}) async-start(), calls=%async_computation.12 | async-start | bytes 229376 | tf_op jit(solution)/shard_map/psum | solution.py:272
  (94 other events, 503.4 us)
Sparse Core Ops, SparseCore 0:
  10.4 46.5 all-gather.12
  58.8 26.4 all-gather.14
  87.2 52.6 all-gather.18
  141.6 52.5 all-gather.16
  198.1 82.0 all-gather.20
  335.5 88.1 reduce-scatter.8
  429.0 80.3 all-gather.22
  511.0 80.5 all-gather.24
  625.7 88.1 reduce-scatter.10
  723.1 80.3 all-gather.26
  806.5 51.1 reduce-scatter.18
  860.8 52.6 reduce-scatter.16
  916.4 27.7 reduce-scatter.14
  947.3 43.9 reduce-scatter.12
  993.5 89.5 reduce-scatter.20
  1085.4 87.9 reduce-scatter.22
  1182.2 80.4 all-gather.20
  1317.7 88.1 reduce-scatter.8
  1411.2 80.3 all-gather.22
  1493.1 80.5 all-gather.24
  1607.8 88.1 reduce-scatter.10
  1705.1 80.3 all-gather.26
  1788.5 51.1 reduce-scatter.18
  1842.9 52.6 reduce-scatter.16
  1898.5 27.6 reduce-scatter.14
  1929.3 43.9 reduce-scatter.12
  1975.6 89.5 reduce-scatter.20
  2067.6 87.9 reduce-scatter.22
  2168.9 120.1 all-reduce.2
where the time goes:
time: 2300 us
  waiting for transfers between devices  1670 us (73%)
  matrix products  417 us (18%)
  other arithmetic  127 us (6%)
  local copies, waits for them, and re-layouts  69.6 us (3%)
    reduce_scatter x2, waiting for transfers between devices, one_batch(): lax.psum_scatter(jnp.einsum('sc,dc->sd', piece, in_flat, preferred_elemen...  178 us
    reduce_scatter x2, waiting for transfers between devices, one_batch(): lax.psum_scatter(jnp.einsum('sf,df->sd', piece, up_all, preferred_element...  177 us
    reduce_scatter x2, waiting for transfers between devices, one_batch(): lax.psum_scatter(jnp.dot(piece, out_all, preferred_element_type=jnp.float...  176 us
    reduce_scatter x2, waiting for transfers between devices, one_batch(): lax.psum_scatter(jnp.dot(piece, down_all, preferred_element_type=jnp.floa...  176 us
    all_gather x2, waiting for transfers between devices, one_batch(): lax.all_gather(normed2.astype(jnp.bfloat16), 'tp', axis=0, tiled=True)  155 us
    all_gather x2, waiting for transfers between devices, one_batch(): lax.all_gather(normed1.astype(jnp.bfloat16), 'tp', axis=0, tiled=True)  147 us
    all_gather x2, waiting for transfers between devices, one_batch(): cot_full = lax.all_gather(cot, 'tp', axis=0, tiled=True)  136 us
    psum x1, waiting for transfers between devices, local(): lax.psum((wide_sums, spread_in, spread_up), ('dp', 'tp'))  122 us
  transfers between devices with their start and end apart: 29, of which 25 were waited for; matrix products, arithmetic and copies ran while one was open for 16% of the time, Pallas kernels for 0%

commit v1 on v0

v1 whole, which is shorter than its diff:
```python
import functools

import jax
import jax.numpy as jnp
from jax import lax
from jax.experimental import pallas as pl
from jax.experimental.pallas import tpu as pltpu
from jax.sharding import Mesh, PartitionSpec as P

HDIM = 128
EPSILON = 1e-05
MASKED = -1e30
LOG2E = 1.4426950408889634
F32 = jnp.float32
BF16 = jnp.bfloat16
VMEM_LIMIT = 48 * 1024 * 1024
DP = ("e", "b", "a")
TP = ("g", "h", "c")
SLOTS = (0, 2, 1, 3)


def dot(x, y, contract=((1,), (0,))):
    return lax.dot_general(x, y, (contract, ((), ())), preferred_element_type=F32)


def stats(rows):
    mean = jnp.mean(rows, axis=-1, keepdims=True)
    center = rows - mean
    inverse = lax.rsqrt(jnp.mean(center * center, axis=-1, keepdims=True) + EPSILON)
    return center * inverse, inverse


def norm_back(grad_normed, scaled, inverse, gain):
    weighted = grad_normed * gain
    return inverse * (
        weighted
        - jnp.mean(weighted, axis=-1, keepdims=True)
        - scaled * jnp.mean(weighted * scaled, axis=-1, keepdims=True)
    )


def flip(x, axis):
    return lax.ppermute(x, axis, [(0, 1), (1, 0)])


def after(x, *others):
    return lax.optimization_barrier((x,) + others)[0]


def gather4(own):
    core = flip(own, "c")
    far = flip(own, "h")
    return jnp.concatenate([own, far, core, flip(far, "c")], 0)


def scatter4(product):
    away = product(1).astype(BF16)
    kept = product(0) + flip(away, "c").astype(F32)
    local = kept.shape[0] // 2
    return kept[:local] + flip(kept[local:].astype(BF16), "h").astype(F32)


def turn(x, groups, by, axes=("e", "g")):
    extra, count = groups
    pairs = []
    for e in range(extra):
        for g in range(count):
            pairs.append((e * count + g, (e + by[0]) % extra * count + (g + by[1]) % count))
    return lax.ppermute(x, axes, pairs)


def square_gather(own):
    half = own.shape[0] // 2
    by_a = flip(own, "a")
    by_b = flip(own, "b")
    return own, by_a, by_b, flip(by_a[:half], "b"), flip(by_b[half:], "a")


def square_scatter(piece):
    diag = piece(1, 1)
    half = diag.shape[0] // 2
    first = flip(diag[:half], "a")
    second = flip(diag[half:], "b")
    to_a, to_b, own = piece(0, 1), piece(1, 0), piece(0, 0)
    a_top = flip(to_a[:half], "a")
    b_low = flip(to_b[half:], "b")
    a_low = flip((to_a[half:].astype(F32) + second.astype(F32)).astype(BF16), "a")
    b_top = flip((to_b[:half].astype(F32) + first.astype(F32)).astype(BF16), "b")
    top = own[:half].astype(F32) + a_top.astype(F32) + b_top.astype(F32)
    low = own[half:].astype(F32) + a_low.astype(F32) + b_low.astype(F32)
    return jnp.concatenate([top, low], 0)


def sum_axis(x, axis):
    if lax.axis_size(axis) == 1:
        return x
    if lax.axis_size(axis) == 2:
        return x + flip(x, axis)
    return jnp.sum(lax.all_gather(x, axis), 0)


def row_blocks(place, count, size):
    found = []
    for j in range(count):
        other = jnp.bitwise_xor(place, j)
        slot = (other >> 1) + 2 * (other & 1)
        found.append(pl.multiple_of(slot * size, size))
    return found


def causal(size):
    keys = lax.broadcasted_iota(jnp.int32, (size, size), 0)
    queries = lax.broadcasted_iota(jnp.int32, (size, size), 1)
    return keys <= queries


def first_key(block, size, segment):
    return 0 if segment is None else block * size // segment * segment


def forward_kernel(size, segment, scale, place, *refs):
    if segment is None:
        q_ref, k_ref, v_ref, kp_ref, vp_ref, out_ref, lse_ref, k_own, v_own = refs
    else:
        q_ref, k_ref, v_ref, out_ref, lse_ref, k_own, v_own = refs
        kp_ref = vp_ref = None
    length = q_ref.shape[0]
    count = length // size
    at = row_blocks(place[1], count, size)
    for j in range(count):
        k_own[j * size : (j + 1) * size] = k_ref[pl.ds(at[j], size), :]
        v_own[j * size : (j + 1) * size] = v_ref[pl.ds(at[j], size), :]

    def run(before):
        for i in range(count):
            q = q_ref[pl.ds(at[i], size), :]
            start, end = first_key(i, size, segment), i * size
            parts = [
                (kp_ref[n * length : (n + 1) * length], vp_ref[n * length : (n + 1) * length], None)
                for n in range(before)
            ]
            if end > start:
                parts.append((k_own[start:end], v_own[start:end], None))
            parts.append((k_own[end : end + size], v_own[end : end + size], causal(size)))
            scores = []
            for k, _, mask in parts:
                s = dot(k, q, ((1,), (1,)))
                scores.append(s if mask is None else jnp.where(mask, s, MASKED))
            top = functools.reduce(
                jnp.maximum, [jnp.max(s, axis=0, keepdims=True) for s in scores]
            )
            total = jnp.zeros((1, size), F32)
            out = jnp.zeros((HDIM, size), F32)
            for s, (_, v, _) in zip(scores, parts):
                p = jnp.exp2((s - top) * scale)
                total = total + jnp.sum(p, axis=0, keepdims=True)
                out = out + dot(v, p.astype(BF16), ((0,), (0,)))
            out_ref[pl.ds(at[i], size), :] = (out / total).T.astype(BF16)
            lse_ref[0, :, i * size : (i + 1) * size] = top * scale + jnp.log(total) * LOG2E

    if segment is not None:
        run(0)
    else:
        for n in range(kp_ref.shape[0] // length + 1):
            pl.when(place[0] == n)(functools.partial(run, n))


def backward_kernel(size, segment, scale, place, *refs):
    if segment is None:
        q_ref, k_ref, v_ref, out_ref, do_ref, lse_ref, kp_ref, vp_ref = refs[:8]
        dproj_ref, dp_ref, k_own, v_own, dk_own, dv_own, dk_pre, dv_pre = refs[8:]
    else:
        q_ref, k_ref, v_ref, out_ref, do_ref, lse_ref = refs[:6]
        dproj_ref, k_own, v_own, dk_own, dv_own = refs[6:]
        kp_ref = vp_ref = None
    length = q_ref.shape[0]
    count = length // size
    head = pl.program_id(0)
    width = pl.num_programs(0) * HDIM
    factor = HDIM**-0.5
    at = row_blocks(place[1], count, size)
    column = [pl.multiple_of(n * width + head * HDIM, HDIM) for n in range(3)]
    for j in range(count):
        k_own[j * size : (j + 1) * size] = k_ref[pl.ds(at[j], size), :]
        v_own[j * size : (j + 1) * size] = v_ref[pl.ds(at[j], size), :]
    dk_own[...] = jnp.zeros_like(dk_own)
    dv_own[...] = jnp.zeros_like(dv_own)
    if segment is None:
        dk_pre[...] = jnp.zeros_like(dk_pre)
        dv_pre[...] = jnp.zeros_like(dv_pre)

    def run(before):
        for i in range(count):
            q = q_ref[pl.ds(at[i], size), :]
            do = do_ref[pl.ds(at[i], size), :]
            product = do.astype(F32) * out_ref[pl.ds(at[i], size), :].astype(F32)
            delta = lax.dot_general(
                jnp.ones((8, HDIM), F32),
                product,
                (((1,), (1,)), ((), ())),
                precision=lax.Precision.HIGHEST,
                preferred_element_type=F32,
            )[:1]
            lse = lse_ref[0, :, i * size : (i + 1) * size]
            start, end = first_key(i, size, segment), i * size
            parts = [
                (kp_ref, vp_ref, dk_pre, dv_pre, n * length, (n + 1) * length, None)
                for n in range(before)
            ]
            if end > start:
                parts.append((k_own, v_own, dk_own, dv_own, start, end, None))
            parts.append((k_own, v_own, dk_own, dv_own, end, end + size, causal(size)))
            dq = jnp.zeros((HDIM, size), F32)
            for k_at, v_at, dk, dv, low, high, mask in parts:
                k, v = k_at[low:high], v_at[low:high]
                s = dot(k, q, ((1,), (1,))) * scale - lse
                p = jnp.exp2(s if mask is None else jnp.where(mask, s, MASKED))
                dscores = (p * (dot(v, do, ((1,), (1,))) - delta)).astype(BF16)
                dv[low:high] += dot(p.astype(BF16), do)
                dk[low:high] += dot(dscores, q)
                dq = dq + dot(k, dscores, ((0,), (0,)))
            dproj_ref[pl.ds(at[i], size), pl.ds(column[0], HDIM)] = (dq * factor).T.astype(BF16)

    if segment is not None:
        run(0)
    else:
        for n in range(kp_ref.shape[0] // length + 1):
            pl.when(place[0] == n)(functools.partial(run, n))
        dp_ref[:, pl.ds(column[0], HDIM)] = (dk_pre[...] * factor).astype(BF16)
        dp_ref[:, pl.ds(column[1], HDIM)] = dv_pre[...].astype(BF16)
    for j in range(count):
        rows = slice(j * size, (j + 1) * size)
        dproj_ref[pl.ds(at[j], size), pl.ds(column[1], HDIM)] = (dk_own[rows] * factor).astype(BF16)
        dproj_ref[pl.ds(at[j], size), pl.ds(column[2], HDIM)] = dv_own[rows].astype(BF16)


def head_spec(length, first):
    return pl.BlockSpec((length, HDIM), lambda h: (0, first + h))


def attention_cost(length, heads, prefix, matmuls):
    pairs = heads * length * (prefix + length // 2)
    return pl.CostEstimate(
        flops=2 * matmuls * pairs * HDIM * 2, bytes_accessed=length * heads * 2048, transcendentals=pairs
    )


def attend(place, proj, size, segment=None, prefix=None):
    length = proj.shape[0]
    heads = proj.shape[1] // (3 * HDIM)
    scale = HDIM**-0.5 * LOG2E
    operands = [place, proj, proj, proj]
    specs = [pl.BlockSpec(memory_space=pltpu.SMEM)] + [head_spec(length, n * heads) for n in range(3)]
    if segment is None:
        operands += [prefix, prefix]
        specs += [head_spec(prefix.shape[0], n * heads) for n in range(2)]
    return pl.pallas_call(
        functools.partial(forward_kernel, size, segment, scale),
        grid=(heads,),
        in_specs=specs,
        out_specs=[head_spec(length, 0), pl.BlockSpec((1, 1, length), lambda h: (h, 0, 0))],
        out_shape=[
            jax.ShapeDtypeStruct((length, heads * HDIM), BF16),
            jax.ShapeDtypeStruct((heads, 1, length), F32),
        ],
        scratch_shapes=[pltpu.VMEM((length, HDIM), BF16)] * 2,
        compiler_params=pltpu.CompilerParams(vmem_limit_bytes=VMEM_LIMIT),
        cost_estimate=attention_cost(length, heads, 0 if prefix is None else prefix.shape[0], 2),
    )(*operands)


def attend_back(place, proj, out, grad_out, lse, size, segment=None, prefix=None):
    length = proj.shape[0]
    heads = proj.shape[1] // (3 * HDIM)
    scale = HDIM**-0.5 * LOG2E
    operands = [place, proj, proj, proj, out, grad_out, lse]
    specs = [pl.BlockSpec(memory_space=pltpu.SMEM)] + [head_spec(length, n * heads) for n in range(3)]
    specs += [head_spec(length, 0)] * 2 + [pl.BlockSpec((1, 1, length), lambda h: (h, 0, 0))]
    out_specs = [pl.BlockSpec(proj.shape, lambda h: (0, 0))]
    out_shape = [jax.ShapeDtypeStruct(proj.shape, BF16)]
    scratch = [pltpu.VMEM((length, HDIM), BF16)] * 2 + [pltpu.VMEM((length, HDIM), F32)] * 2
    if segment is None:
        operands += [prefix, prefix]
        specs += [head_spec(prefix.shape[0], n * heads) for n in range(2)]
        out_specs.append(pl.BlockSpec(prefix.shape, lambda h: (0, 0)))
        out_shape.append(jax.ShapeDtypeStruct(prefix.shape, BF16))
        scratch += [pltpu.VMEM((prefix.shape[0], HDIM), F32)] * 2
    return pl.pallas_call(
        functools.partial(backward_kernel, size, segment, scale),
        grid=(heads,),
        in_specs=specs,
        out_specs=out_specs,
        out_shape=out_shape,
        scratch_shapes=scratch,
        compiler_params=pltpu.CompilerParams(vmem_limit_bytes=VMEM_LIMIT),
        cost_estimate=attention_cost(length, heads, 0 if prefix is None else prefix.shape[0], 5),
    )(*operands)


def local(
    tokens,
    segments,
    first_gain,
    first_shift,
    in_weight,
    in_bias,
    out_weight,
    out_bias,
    second_gain,
    second_shift,
    up_weight,
    up_bias,
    down_weight,
    down_bias,
    cotangent,
):
    extra, groups = lax.axis_size("e"), lax.axis_size("g")
    split = (extra, groups)
    size, width = tokens.shape[1:]
    cols, hidden, depth = in_weight.shape[2], up_weight.shape[1], in_weight.shape[0]
    quarter = segments.shape[1] // 4
    at_e, at_b, at_a, at_g = (lax.axis_index(n) for n in ("e", "b", "a", "g"))
    place = jnp.stack([at_g, 2 * lax.axis_index("h") + lax.axis_index("c")]).astype(jnp.int32)
    sources = [(e, g) for g in range(groups) for e in range(extra)]

    single = jnp.where(segments[0, -1] == 0, 0, 1)
    order = (single, 1 - single)

    def pick(x):
        return [lax.dynamic_index_in_dim(x, r, 0, keepdims=False) for r in order]

    def unpick(first, second):
        return jnp.where(single == 0, jnp.stack([first, second]), jnp.stack([second, first]))

    rows = [r.astype(F32) for r in pick(tokens)]
    cots = pick(cotangent)

    def dp_place(e_off, i, j):
        return ((at_e + e_off) % extra) * 4 + (at_b ^ i) * 2 + (at_a ^ j)

    def gather_weight(weight, full_shape, put, wait=()):
        half = weight.shape[0] // 2
        full = jnp.zeros(full_shape, BF16)
        held = after(weight, *wait) if wait else weight
        arrived = []
        for e_off, g_off in sources:
            piece = held if (e_off, g_off) == (0, 0) else turn(held, split, (e_off, g_off))
            own, by_a, by_b, top, low = square_gather(piece)
            arrived += [by_a, by_b]
            full = put(full, own, dp_place(-e_off, 0, 0), g_off, 0)
            full = put(full, by_a, dp_place(-e_off, 0, 1), g_off, 0)
            full = put(full, by_b, dp_place(-e_off, 1, 0), g_off, 0)
            full = put(full, top, dp_place(-e_off, 1, 1), g_off, 0)
            full = put(full, low, dp_place(-e_off, 1, 1), g_off, half)
        return full, arrived

    def put_in(full, piece, d, g, skip):
        for n in range(3):
            full = lax.dynamic_update_slice(
                full,
                piece[:, n * cols : (n + 1) * cols],
                (d * depth + skip, (n * groups + g) * cols),
            )
        return full

    def put_rows(full, piece, d, g, skip):
        return lax.dynamic_update_slice(full, piece, (d * depth + skip, g * hidden))

    def put_columns(full, piece, d, g, skip):
        return lax.dynamic_update_slice(
            full, piece, (g * (full.shape[0] // groups) + skip, d * depth)
        )

    in_all, came_in = gather_weight(
        in_weight.reshape(depth, 3 * cols), (width, 3 * groups * cols), put_in
    )
    out_all, came_out = gather_weight(out_weight, (groups * cols, width), put_columns, came_in[:2])
    up_all, came_up = gather_weight(up_weight, (width, groups * hidden), put_rows, came_in)
    down_all, _ = gather_weight(down_weight, (groups * hidden, width), put_columns, came_up[:2])
    kv_all = in_all[:, groups * cols :]

    biases = jnp.concatenate([in_bias.reshape(-1), up_bias])
    shares = [biases if g == 0 else turn(biases, split, (0, g)) for g in range(groups)]
    bias_q = jnp.concatenate([s[:cols] for s in shares])
    bias_v = jnp.concatenate([s[cols : 2 * cols] for s in shares])
    bias_k = jnp.zeros_like(bias_q)
    bias_up = jnp.concatenate([s[2 * cols :] for s in shares])
    bias_proj = jnp.concatenate([bias_q, bias_k, bias_v])
    bias_kv = jnp.concatenate([bias_k, bias_v])

    scaled1, inverse1, full1 = [], [], []
    for r in range(2):
        scaled, inverse = stats(rows[r])
        scaled1.append(scaled)
        inverse1.append(inverse)
        full1.append((scaled * first_gain + first_shift).astype(BF16))
    low1 = full1
    full1 = [gather4(x) for x in low1]
    prefix1 = [
        lax.ppermute(low1[0], "g", [(g, g + k) for g in range(groups - k)])
        for k in range(1, groups)
    ]
    prefix1 = jnp.concatenate([gather4(x) for x in prefix1], 0)
    proj = [(dot(x, in_all) + bias_proj).astype(BF16) for x in full1]
    proj_prefix = (dot(prefix1, kv_all) + bias_kv).astype(BF16)
    attended, lse = [None, None], [None, None]
    attended[1], lse[1] = attend(place, proj[1], size, segment=quarter)
    attended[0], lse[0] = attend(place, proj[0], size, prefix=proj_prefix)

    def halves(x):
        middle = x.shape[0] // 2
        return lambda i: x[i * middle : (i + 1) * middle]

    def product_of(x, weight, contract):
        part = halves(x)
        return lambda i: dot(part(i), weight, contract)

    resid, scaled2, inverse2, full2 = [None] * 2, [None] * 2, [None] * 2, [None] * 2
    for r in (1, 0):
        summed = scatter4(product_of(attended[r], out_all, ((1,), (0,))))
        resid[r] = rows[r] + summed + out_bias
        scaled2[r], inverse2[r] = stats(resid[r])
        full2[r] = gather4((scaled2[r] * second_gain + second_shift).astype(BF16))

    active, slope, full_cot, dup = [None] * 2, [None] * 2, [None] * 2, [None] * 2
    for r in (1, 0):
        full_cot[r] = gather4(after(cots[r], full1[r]))
        upward = dot(full2[r], up_all) + bias_up
        tanh = jnp.tanh(0.7978845608028654 * (upward + 0.044715 * upward * upward * upward))
        active[r] = (0.5 * upward * (1.0 + tanh)).astype(BF16)
        slope[r] = (
            0.5 * (1.0 + tanh)
            + 0.5
            * upward
            * (1.0 - tanh * tanh)
            * 0.7978845608028654
            * (1.0 + 3 * 0.044715 * upward * upward)
        )
    dres, sums2 = [None] * 2, []
    for r in (0, 1):
        dup[r] = (dot(full_cot[r], down_all, ((1,), (1,))) * slope[r]).astype(BF16)
        dnormed2 = scatter4(product_of(dup[r], up_all, ((1,), (1,))))
        cot = cots[r].astype(F32)
        dres[r] = cot + norm_back(dnormed2, scaled2[r], inverse2[r], second_gain)
        sums2.append(
            jnp.stack(
                [
                    jnp.sum(dres[r], 0),
                    jnp.sum(dnormed2 * scaled2[r], 0),
                    jnp.sum(dnormed2, 0),
                    jnp.sum(cot, 0),
                ]
            )
        )
    full_dres = [gather4(x.astype(BF16)) for x in dres]
    mixed = [None] * 2
    for r in (1, 0):
        summed = scatter4(product_of(active[r], down_all, ((1,), (0,))))
        mixed[r] = (resid[r] + summed + down_bias).astype(BF16)

    def scatter_weight(grad, shape, take):
        middle = {}
        for e_off, g_off in sources[::-1]:
            summed = square_scatter(
                lambda i, j: take(grad, dp_place(-e_off, i, j), g_off)
            )
            if (e_off, g_off) != (0, 0):
                summed = turn(
                    summed.astype(BF16), split, ((-e_off) % extra, (-g_off) % groups)
                ).astype(F32)
            middle[e_off, g_off] = summed
        return functools.reduce(jnp.add, [middle[s] for s in sources])

    def take_rows(grad, d, g):
        return lax.dynamic_slice(grad, (d * depth, g * hidden), (depth, hidden))

    def take_columns(grad, d, g):
        count = grad.shape[0] // groups
        return lax.dynamic_slice(grad, (g * count, d * depth), (count, depth))

    def take_in(grad, d, g):
        return jnp.concatenate(
            [
                lax.dynamic_slice(grad, (d * depth, (n * groups + g) * cols), (depth, cols))
                for n in range(3)
            ],
            1,
        )

    def weight_grad(lefts, rights):
        left, right = jnp.concatenate(lefts, 0), jnp.concatenate(rights, 0)
        return dot(left, right, ((0,), (0,))).astype(BF16)

    grad_down = scatter_weight(weight_grad(active, full_cot), down_weight.shape, take_columns)
    grad_up = scatter_weight(weight_grad(full2, dup), up_weight.shape, take_rows)
    grad_up_bias = jnp.sum(dup[0], 0, dtype=F32) + jnp.sum(dup[1], 0, dtype=F32)

    dattended = [dot(x, out_all, ((1,), (1,))).astype(BF16) for x in full_dres]
    dproj = [None, None]
    dproj[0], dprefix = attend_back(
        place, proj[0], attended[0], dattended[0], lse[0], size, prefix=proj_prefix
    )
    dproj[1] = attend_back(
        place, proj[1], attended[1], dattended[1], lse[1], size, segment=quarter
    )[0]
    grad_out = scatter_weight(weight_grad(attended, full_dres), out_weight.shape, take_columns)

    dnormed1 = [None, None]
    length = 4 * size
    returned = []
    for k in range(1, groups):
        part = scatter4(
            product_of(dprefix[(k - 1) * length : k * length], kv_all, ((1,), (1,)))
        ).astype(BF16)
        returned.append(
            lax.ppermute(part, "g", [(g + k, g) for g in range(groups - k)]).astype(F32)
        )
    for r in (1, 0):
        dnormed1[r] = scatter4(product_of(dproj[r], in_all, ((1,), (1,))))
    dnormed1[0] = functools.reduce(jnp.add, [dnormed1[0]] + returned)

    grad_q = weight_grad(full1, [x[:, : groups * cols] for x in dproj])
    grad_kv = weight_grad(full1 + [prefix1], [x[:, groups * cols :] for x in dproj] + [dprefix])
    grad_in = scatter_weight(
        jnp.concatenate([grad_q, grad_kv], 1), in_weight.shape, take_in
    ).reshape(in_weight.shape)
    tokens_grad, sums1 = [], []
    for r in range(2):
        tokens_grad.append(
            (dres[r] + norm_back(dnormed1[r], scaled1[r], inverse1[r], first_gain)).astype(BF16)
        )
        sums1.append(jnp.stack([jnp.sum(dnormed1[r] * scaled1[r], 0), jnp.sum(dnormed1[r], 0)]))

    grad_q_bias = jnp.sum(dproj[0][:, : groups * cols], 0, dtype=F32) + jnp.sum(
        dproj[1][:, : groups * cols], 0, dtype=F32
    )
    grad_v_bias = (
        jnp.sum(dproj[0][:, 2 * groups * cols :], 0, dtype=F32)
        + jnp.sum(dproj[1][:, 2 * groups * cols :], 0, dtype=F32)
        + jnp.sum(dprefix[:, groups * cols :], 0, dtype=F32)
    )

    def to_owner(x):
        share = x.reshape(groups, -1)
        return functools.reduce(
            jnp.add,
            [share[0]] + [turn(share[g], split, (0, (-g) % groups)) for g in range(1, groups)],
        )

    def sum_over(x, axes):
        for axis in axes:
            x = sum_axis(x, axis)
        return x

    early = sum_over(sums2[0] + sums2[1], ("c", "h", "g") + DP)
    grad_up_bias = sum_over(to_owner(grad_up_bias), DP)
    late = sum_over(sums1[0] + sums1[1], ("c", "h", "g") + DP)
    grad_in_bias = sum_over(jnp.stack([to_owner(grad_q_bias), to_owner(grad_v_bias)]), DP)
    return (
        unpick(*mixed),
        unpick(*tokens_grad),
        late[0],
        late[1],
        grad_in,
        grad_in_bias,
        grad_out,
        early[0],
        early[1],
        early[2],
        grad_up,
        grad_up_bias,
        grad_down,
        early[3],
    )


def solution(mesh):
    dp, tp = mesh.shape["dp"], mesh.shape["tp"]
    split = Mesh(mesh.devices.reshape(dp // 4, 2, 2, tp // 4, 2, 2), DP + TP)
    in_specs = (
        P(DP, TP, None),
        P(DP, None),
        P(),
        P(),
        P(DP, None, TP),
        P(None, TP),
        P(TP, DP),
        P(),
        P(),
        P(),
        P(DP, TP),
        P(TP),
        P(TP, DP),
        P(),
        P(DP, TP, None),
    )
    out_specs = (
        P(DP, TP, None),
        P(DP, TP, None),
        P(),
        P(),
        P(DP, None, TP),
        P(None, TP),
        P(TP, DP),
        P(),
        P(),
        P(),
        P(DP, TP),
        P(TP),
        P(TP, DP),
        P(),
    )
    return jax.shard_map(local, mesh=split, in_specs=in_specs, out_specs=out_specs, check_vma=False)
```

time: 2300 us -> 1290 us (0.56)
  waiting for transfers between devices: 1670 us -> 533 us
  starting transfers between devices: 1.24 us -> 168 us
  matrix products: 417 us -> 315 us
  local copies, waits for them, and re-layouts: 69.6 us -> 152 us
  other arithmetic: 127 us -> 64.2 us
  Pallas kernels: 0 us -> 43.4 us
    reduce_scatter x16 -> x0, waiting for transfers between devices: 829 us -> none  [the longest x2 178 us: one_batch(): lax.psum_scatter(jnp.einsum('sc,dc->sd', piece, in_flat, preferred_elemen...]
    all_gather x12 -> x0, waiting for transfers between devices: 713 us -> none  [the longest x2 155 us: one_batch(): lax.all_gather(normed2.astype(jnp.bfloat16), 'tp', axis=0, tiled=True)]
    ppermute x0 -> x153, waiting for transfers between devices: none -> 533 us  [the longest x139 463 us: flip(): return lax.ppermute(x, axis, [(0, 1), (1, 0)])]
    ppermute x0 -> x153, starting transfers between devices: none -> 168 us  [the longest x139 116 us: flip(): return lax.ppermute(x, axis, [(0, 1), (1, 0)])]
    psum x1 -> x0, waiting for transfers between devices: 122 us -> none  [local(): lax.psum((wide_sums, spread_in, spread_up), ('dp', 'tp'))]
    dot_general x72 -> x32, matrix products: 417 us -> 315 us  [dot(): lax.dot_general(x, y, (contract, ((), ())), preferred_element_type=F32)]
    unnamed x17 -> x272, local copies, waits for them, and re-layouts: 10.6 us -> 62.4 us
    dynamic_update_slice x2 -> x60, local copies, waits for them, and re-layouts: 1.59 us -> 52 us  [the longest x30 33.1 us: put_in(): lax.dynamic_update_slice(full, piece[:, n * cols:(n + 1) * cols], (d * de...]
  transfers between devices with their start and end apart: 29 -> 153, of which waited for: 25 -> 61; matrix products, arithmetic and copies ran while one was open for 16% -> 29% of each run, Pallas kernels for 0% -> 1%
where the time goes in v1:
time: 1290 us; the launch traced here: 1280 us
  waiting for transfers between devices  533 us (41%)
  matrix products  315 us (24%)
  starting transfers between devices  168 us (13%)
  local copies, waits for them, and re-layouts  152 us (12%)
  other arithmetic  64.2 us (5%)
  Pallas kernels  43.4 us (3%)
    ppermute x139, waiting for transfers between devices, flip(): return lax.ppermute(x, axis, [(0, 1), (1, 0)])  463 us
    dot_general x32, matrix products, dot(): lax.dot_general(x, y, (contract, ((), ())), preferred_element_type=F32)  315 us
    ppermute x139, starting transfers between devices, flip(): return lax.ppermute(x, axis, [(0, 1), (1, 0)])  116 us
    unnamed x272, local copies, waits for them, and re-layouts  62.4 us
    ppermute x12, starting transfers between devices, turn(): return lax.ppermute(x, axes, pairs)  45.5 us
    ppermute x12, waiting for transfers between devices, turn(): return lax.ppermute(x, axes, pairs)  39.2 us
    dynamic_update_slice x30, local copies, waits for them, and re-layouts, put_in(): lax.dynamic_update_slice(full, piece[:, n * cols:(n + 1) * cols], (d * de...  33.1 us
    ppermute x1, waiting for transfers between devices, local(): lax.ppermute(part, 'g', [(g + k, g) for g in range(groups - k)]).astype(F32)  30.5 us
  transfers between devices with their start and end apart: 153, of which 61 were waited for; matrix products, arithmetic and copies ran while one was open for 29% of the time, Pallas kernels for 1%

profile of v1, /device:TPU:0, one launch (start us, length us, event | category | flops | bytes accessed | tf_op | source)
XLA Modules:
  0.0 1279.9 jit_solution(6446396041247640359)
XLA Ops:
  34.2 8.0 collective-permute-done.12
  62.7 9.7 collective-permute-done
  91.8 5.7 collective-permute-done.6
  110.6 7.8 collective-permute-done.22
  132.2 5.7 collective-permute-done.10
  140.4 8.0 collective-permute-done.11
  157.1 19.0 %collective-permute-done.14 = bf16[256,2048]{1,0:T(8,128)(2,1)S(1)} collective-permute-done((bf16[256,2048]{1,0:T(8,128)(2,1)S(1)}, bf16[256,2048]{1,0:T(8,128)(2,1)S(1)}, u32[]{:S(2)}, u32[]{:S(2)}) %collective-permute-start.14) | collective-permute-done | bytes 1048608 | tf_op jit(solution)/shard_map/ppermute | solution.py:43
  176.1 13.4 %add_convert_fusion.1.refs_0_.refs_1_.refs_2_ = bf16[1024,1536]{1,0:T(8,128)(2,1)} fusion(bf16[2048,1536]{0,1:T(8,128)(2,1)} %slice_dynamic-update-slice_fusion.18, f32[1536]{0:T(1024)S(1)} %get-tuple-element.226, bf16[256,2048]{1,0:T(8,128)(2,1)S(1)} %collective-permute-done.2, bf16[256,2048]{1,0:T(8,128)(2,1)} %collective-permute-done.1, ...), kind=kOutput, calls=%fused_computation.87 | convolution fusion | flops 6462373888 | bytes 13637632 | tf_op jit(solution)/shard_map/dot_general | solution.py:23
  192.2 6.4 collective-permute-done.51
  198.6 7.8 add_convert_fusion.2.refs_3_.refs_4_.refs_6_.refs_7_
  206.4 9.7 shard_map.254
  220.0 12.5 add_convert_fusion.refs_0_.refs_1_.refs_2_
  232.5 6.7 shard_map.255
  273.1 10.3 collective-permute-start.35
  285.9 10.3 collective-permute-start.44
  308.7 21.7 %collective-permute-done.27 = bf16[256,2048]{1,0:T(8,128)(2,1)} collective-permute-done((bf16[256,2048]{1,0:T(8,128)(2,1)}, bf16[256,2048]{1,0:T(8,128)(2,1)}, u32[]{:S(2)}, u32[]{:S(2)}) %collective-permute-start.27) | collective-permute-done | bytes 1048608 | tf_op jit(solution)/shard_map/ppermute | solution.py:43
  331.8 20.2 %collective-permute-done.55 = bf16[256,2048]{1,0:T(8,128)(2,1)} collective-permute-done((bf16[256,2048]{1,0:T(8,128)(2,1)}, bf16[256,2048]{1,0:T(8,128)(2,1)}, u32[]{:S(2)}, u32[]{:S(2)}) %collective-permute-start.55) | collective-permute-done | bytes 1048608 | tf_op jit(solution)/shard_map/ppermute | solution.py:43
  358.5 8.4 collective-permute-done.33
  373.7 8.5 collective-permute-done.40
  384.8 19.8 %collective-permute-done.36 = bf16[512,1024]{1,0:T(8,128)(2,1)S(1)} collective-permute-done((bf16[512,1024]{1,0:T(8,128)(2,1)}, bf16[512,1024]{1,0:T(8,128)(2,1)S(1)}, u32[]{:S(2)}, u32[]{:S(2)}) %collective-permute-start.36) | collective-permute-done | bytes 1048608 | tf_op jit(solution)/shard_map/ppermute | solution.py:43
  425.0 11.9 collective-permute-done.45
  439.5 11.0 collective-permute-done.38
  465.1 13.9 %fusion.50 = f32[1024,2048]{1,0:T(8,128)} fusion(bf16[2048,2048]{1,0:T(8,128)(2,1)S(1)} %constant_dynamic-update-slice_fusion.66, bf16[256,2048]{1,0:T(8,128)(2,1)S(1)} %collective-permute-done.58, bf16[256,2048]{1,0:T(8,128)(2,1)S(1)} %collective-permute-done.57, bf16[256,2048]{1,0:T(8,128)(2,1)S(1)} %collective-permute-done.56, ...), kind=kOutput, calls=%fused_computation.106 | convolution fusion | flops 8606711808 | bytes 20971520 | tf_op jit(solution)/shard_map/dot_general | solution.py:23
  479.1 24.1 %multiply_convert_fusion.1 = (bf16[1024,2048]{1,0:T(8,128)(2,1)}, bf16[1024,2048]{1,0:T(8,128)(2,1)}, f32[1024,2048]{1,0:T(8,128)}) fusion(f32[2048]{0:T(1024)S(1)} %pad_maximum_fusion.15, f32[1024,2048]{1,0:T(8,128)} %fusion.50, bf16[2048,2048]{1,0:T(8,128)(2,1)} %copy-done.28, bf16[256,2048]{1,0:T(8,128)(2,1)S(1)} %copy-done.62, ...), kind=kOutput, calls=%fused_computation.77 | convolution fusion | flops 8648654848 | bytes 37756928 | tf_op jit(solution)/shard_map/dot_general | solution.py:23
  503.2 21.5 %convert_reduce_fusion = (f32[2048]{0:T(1024)S(1)}, bf16[1024,2048]{1,0:T(8,128)(2,1)}) fusion(f32[1024,2048]{1,0:T(8,128)} %fusion.50, f32[2048]{0:T(1024)S(1)} %pad_maximum_fusion.15, bf16[2048,2048]{1,0:T(8,128)(2,1)} %constant_dynamic-update-slice_fusion.76, bf16[256,2048]{1,0:T(8,128)(2,1)} %collective-permute-done.76, ...), kind=kOutput, calls=%fused_computation.74 | convolution fusion | flops 8652847104 | bytes 25182208 | tf_op jit(solution)/shard_map/dot_general | solution.py:23
  524.7 21.4 %convert_reduce_fusion.1 = (f32[2048]{0:T(1024)S(1)}, bf16[1024,2048]{1,0:T(8,128)(2,1)}) fusion(f32[1024,2048]{1,0:T(8,128)} %get-tuple-element.229, f32[2048]{0:T(1024)S(1)} %pad_maximum_fusion.15, bf16[2048,2048]{1,0:T(8,128)(2,1)} %constant_dynamic-update-slice_fusion.76, bf16[256,2048]{1,0:T(8,128)(2,1)} %collective-permute-done.63, ...), kind=kOutput, calls=%fused_computation.75 | convolution fusion | flops 8652847104 | bytes 25182208 | tf_op jit(solution)/shard_map/dot_general | solution.py:23
  547.2 22.6 %fusion.22 = bf16[2048,2048]{1,0:T(8,128)(2,1)S(1)} fusion(bf16[2048,2048]{1,0:T(8,128)(2,1)} %constant_dynamic-update-slice_fusion.29, bf16[1024,2048]{1,0:T(8,128)(2,1)} %get-tuple-element.233, bf16[1024,2048]{1,0:T(8,128)(2,1)} %get-tuple-element.231), kind=kOutput, calls=%fused_computation.78 | convolution fusion | flops 17200840704 | bytes 25165824 | tf_op jit(solution)/shard_map/dot_general | solution.py:23
  575.4 22.4 %fusion.25 = bf16[2048,2048]{1,0:T(8,128)(2,1)S(1)} fusion(bf16[2048,2048]{1,0:T(8,128)(2,1)} %constant_dynamic-update-slice_fusion.37, bf16[1024,2048]{1,0:T(8,128)(2,1)} %get-tuple-element.224, bf16[1024,2048]{1,0:T(8,128)(2,1)} %get-tuple-element.223), kind=kOutput, calls=%fused_computation.79 | convolution fusion | flops 17200840704 | bytes 25165824 | tf_op jit(solution)/shard_map/dot_general | solution.py:23
  609.5 10.5 collective-permute-done.124
  620.7 6.3 collective-permute-done.147
  628.7 9.9 convolution_convert_fusion.3
  644.1 10.3 collective-permute-done.129
  655.3 10.3 collective-permute-done.132
  666.5 9.9 convolution_convert_fusion.5
  681.8 6.3 collective-permute-done.143
  688.7 10.6 collective-permute-done.148
  700.0 9.5 convolution_convert_fusion.8
  717.3 9.8 convolution_convert_fusion.6
  730.5 7.6 collective-permute-done.142
  748.1 9.1 convert_add_fusion.1
  759.7 10.0 convert_add_fusion.7
  773.3 6.8 convert_add_fusion.4
  781.1 9.2 convert_add_fusion.5
  790.5 59.4 %collective-permute-done.65 = bf16[256,2048]{1,0:T(8,128)(2,1)S(1)} collective-permute-done((bf16[256,2048]{1,0:T(8,128)(2,1)S(1)}, bf16[256,2048]{1,0:T(8,128)(2,1)S(1)}, u32[]{:S(2)}, u32[]{:S(2)}) %collective-permute-start.65) | collective-permute-done | bytes 1048608 | tf_op jit(solution)/shard_map/ppermute | solution.py:43
  856.4 40.0 %collective-permute-done.60 = bf16[256,2048]{1,0:T(8,128)(2,1)S(1)} collective-permute-done((bf16[256,2048]{1,0:T(8,128)(2,1)S(1)}, bf16[256,2048]{1,0:T(8,128)(2,1)S(1)}, u32[]{:S(2)}, u32[]{:S(2)}) %collective-permute-start.60) | collective-permute-done | bytes 1048608 | tf_op jit(solution)/shard_map/ppermute | solution.py:43
  902.9 22.4 %collective-permute-done.120 = f32[4,2048]{1,0:T(4,128)S(1)} collective-permute-done((f32[4,2048]{1,0:T(4,128)S(1)}, f32[4,2048]{1,0:T(4,128)S(1)}, u32[]{:S(2)}, u32[]{:S(2)}) %collective-permute-start.120) | collective-permute-done | bytes 32800 | tf_op jit(solution)/shard_map/ppermute | solution.py:43
  943.8 16.0 %shard_map.256 = (bf16[1024,1536]{1,0:T(8,128)(2,1)}, bf16[1024,1024]{1,0:T(8,128)(2,1)S(1)}) custom-call(s32[2]{0:T(128)S(1)} %pad_add_fusion.place, bf16[1024,1536]{1,0:T(8,128)(2,1)} %add_convert_fusion.1.refs_0_.refs_1_.refs_2_, bf16[1024,1536]{1,0:T(8,128)(2,1)} %add_convert_fusion.1.refs_0_.refs_1_.refs_2_, ...), custom_call_target="tpu_custom_call" | custom-call | flops 16106127360 | bytes 8388608 | tf_op jit(solution)/shard_map/pallas_call | solution.py:288
  959.8 6.7 convolution_convert_fusion.4
  977.6 16.9 %collective-permute-done.79 = bf16[256,2048]{1,0:T(8,128)(2,1)S(1)} collective-permute-done((bf16[256,2048]{1,0:T(8,128)(2,1)S(1)}, bf16[256,2048]{1,0:T(8,128)(2,1)S(1)}, u32[]{:S(2)}, u32[]{:S(2)}) %collective-permute-start.79) | collective-permute-done | bytes 1048608 | tf_op jit(solution)/shard_map/ppermute | solution.py:43
  996.8 5.5 convert_add_fusion.3
  1016.4 11.0 shard_map.257
  1029.0 8.1 convolution_convert_fusion.2
  1037.1 5.9 convolution_convert_fusion.1
  1043.0 17.3 %fusion.88 = bf16[2048,1024]{0,1:T(8,128)(2,1)S(1)} fusion(bf16[3072,2048]{1,0:T(8,128)(2,1)} %constant_dynamic-update-slice_fusion.9, bf16[1024,1024]{1,0:T(8,128)(2,1)S(1)} %get-tuple-element.33, bf16[1024,1024]{1,0:T(8,128)(2,1)S(1)} %slice-done, bf16[1024,1024]{1,0:T(8,128)(2,1)} %slice.634), kind=kOutput, calls=%fused_computation.154 | convolution fusion | flops 12905873408 | bytes 23068672 | tf_op jit(solution)/shard_map/dot_general | solution.py:23
  1070.8 10.5 collective-permute-start.103
  1109.4 6.1 collective-permute-done.108
  1118.5 13.2 %collective-permute-done.110 = bf16[128,512]{1,0:T(8,128)(2,1)S(1)} collective-permute-done((bf16[128,512]{1,0:T(8,128)(2,1)S(1)}, bf16[128,512]{1,0:T(8,128)(2,1)S(1)}, u32[]{:S(2)}, u32[]{:S(2)}) %collective-permute-start.110) | collective-permute-done | bytes 131104 | tf_op jit(solution)/shard_map/ppermute | solution.py:43
  1136.2 9.3 collective-permute-done.100
  1146.0 5.6 collective-permute-done.97
  1170.9 15.6 %collective-permute-done.118 = bf16[256,512]{1,0:T(8,128)(2,1)S(1)} collective-permute-done((bf16[256,512]{1,0:T(8,128)(2,1)S(1)}, bf16[256,512]{1,0:T(8,128)(2,1)S(1)}, u32[]{:S(2)}, u32[]{:S(2)}) %collective-permute-start.118) | collective-permute-done | bytes 262176 | tf_op jit(solution)/shard_map/ppermute | solution.py:69
  1189.6 15.6 %collective-permute-done.101 = bf16[512,768]{0,1:T(8,128)(2,1)S(1)} collective-permute-done((bf16[512,768]{0,1:T(8,128)(2,1)S(1)}, bf16[512,768]{0,1:T(8,128)(2,1)S(1)}, u32[]{:S(2)}, u32[]{:S(2)}) %collective-permute-start.101) | collective-permute-done | bytes 786464 | tf_op jit(solution)/shard_map/ppermute | solution.py:69
  1209.7 7.1 collective-permute-done.70
  1216.8 30.5 %collective-permute-done.73 = bf16[256,2048]{1,0:T(8,128)(2,1)} collective-permute-done((bf16[256,2048]{1,0:T(8,128)(2,1)}, bf16[256,2048]{1,0:T(8,128)(2,1)}, u32[]{:S(2)}, u32[]{:S(2)}) %collective-permute-start.73) | collective-permute-done | bytes 1048608 | tf_op jit(solution)/shard_map/ppermute | solution.py:516
  1247.3 10.0 collective-permute-done.83
  (773 shorter events, 439.0 us)
Async XLA Ops:
  3.1 82.2 %collective-permute-start.7 = (bf16[512,768]{0,1:T(8,128)(2,1)}, bf16[512,768]{0,1:T(8,128)(2,1)}, u32[]{:S(2)}, u32[]{:S(2)}) collective-permute-start(bf16[512,768]{0,1:T(8,128)(2,1)} %bitcast.4), channel_id=1, source_target_pairs={{0,4},{4,0},{1,5},{5,1},{2,6},{6,2},{3,7},{7,3},{8,12},{12,8},{9,1... | collective-permute-start | bytes 2359304 | tf_op jit(solution)/shard_map/ppermute | solution.py:69
  7.2 35.8 %collective-permute-start.4 = (bf16[512,768]{0,1:T(8,128)(2,1)}, bf16[512,768]{0,1:T(8,128)(2,1)}, u32[]{:S(2)}, u32[]{:S(2)}) collective-permute-start(bf16[512,768]{0,1:T(8,128)(2,1)} %bitcast.4), channel_id=1, source_target_pairs={{0,16},{16,0},{1,17},{17,1},{2,18},{18,2},{3,19},{19,3},{4,20},{20... | collective-permute-start | bytes 2359304 | tf_op jit(solution)/shard_map/ppermute | solution.py:43
  8.7 34.3 %collective-permute-start.3 = (bf16[512,768]{0,1:T(8,128)(2,1)}, bf16[512,768]{0,1:T(8,128)(2,1)}, u32[]{:S(2)}, u32[]{:S(2)}) collective-permute-start(bf16[512,768]{0,1:T(8,128)(2,1)} %bitcast.4), channel_id=1, source_target_pairs={{0,8},{8,0},{1,9},{9,1},{2,10},{10,2},{3,11},{11,3},{4,12},{12,4},... | collective-permute-start | bytes 2359304 | tf_op jit(solution)/shard_map/ppermute | solution.py:43
  11.6 30.6 %collective-permute-start.12 = (f32[1536]{0:T(1024)S(1)}, f32[1536]{0:T(1024)S(1)}, u32[]{:S(2)}, u32[]{:S(2)}) collective-permute-start(f32[1536]{0:T(1024)S(1)} %pad_maximum_fusion.14), channel_id=1, source_target_pairs={{0,4},{4,0},{1,5},{5,1},{2,6},{6,2},{3,7},{7,3},{8,12},{12,8},{9,1... | collective-permute-start | bytes 18440 | tf_op jit(solution)/shard_map/ppermute | solution.py:69
  18.3 56.9 %collective-permute-start.1 = (bf16[256,2048]{1,0:T(8,128)(2,1)}, bf16[256,2048]{1,0:T(8,128)(2,1)}, u32[]{:S(2)}, u32[]{:S(2)}) collective-permute-start(bf16[256,2048]{1,0:T(8,128)(2,1)} %get-tuple-element.111), channel_id=1, source_target_pairs={{0,1},{1,0},{2,3},{3,2},{4,5},{5,4},{6,7},{7,6},{8,9},{9,8},{10,11... | collective-permute-start | bytes 3145736 | tf_op jit(solution)/shard_map/ppermute | solution.py:43
  80.2 45.7 %collective-permute-start.13 = (bf16[256,2048]{1,0:T(8,128)(2,1)}, bf16[256,2048]{1,0:T(8,128)(2,1)S(1)}, u32[]{:S(2)}, u32[]{:S(2)}) collective-permute-start(bf16[256,2048]{1,0:T(8,128)(2,1)} %get-tuple-element.111), channel_id=1, source_target_pairs={{0,4},{1,5},{2,6},{3,7},{8,12},{9,13},{10,14},{11,15},{16,20},{17,... | collective-permute-start | bytes 3145736 | tf_op jit(solution)/shard_map/ppermute | solution.py:400
  86.0 40.6 %collective-permute-start.9 = (bf16[512,768]{0,1:T(8,128)(2,1)}, bf16[512,768]{0,1:T(8,128)(2,1)S(1)}, u32[]{:S(2)}, u32[]{:S(2)}) collective-permute-start(bf16[512,768]{0,1:T(8,128)(2,1)} %collective-permute-done.7), channel_id=1, source_target_pairs={{0,16},{16,0},{1,17},{17,1},{2,18},{18,2},{3,19},{19,3},{4,20},{20... | collective-permute-start | bytes 2359304 | tf_op jit(solution)/shard_map/ppermute | solution.py:43
  87.5 38.7 %collective-permute-start.8 = (bf16[512,768]{0,1:T(8,128)(2,1)}, bf16[512,768]{0,1:T(8,128)(2,1)S(1)}, u32[]{:S(2)}, u32[]{:S(2)}) collective-permute-start(bf16[512,768]{0,1:T(8,128)(2,1)} %collective-permute-done.7), channel_id=1, source_target_pairs={{0,8},{8,0},{1,9},{9,1},{2,10},{10,2},{3,11},{11,3},{4,12},{12,4},... | collective-permute-start | bytes 2359304 | tf_op jit(solution)/shard_map/ppermute | solution.py:43
  123.4 120.0 %collective-permute-start.62 = (bf16[256,2048]{1,0:T(8,128)(2,1)S(1)}, bf16[256,2048]{1,0:T(8,128)(2,1)}, u32[]{:S(2)}, u32[]{:S(2)}) collective-permute-start(bf16[256,2048]{1,0:T(8,128)(2,1)S(1)} %copy-done.24), channel_id=1, source_target_pairs={{0,1},{1,0},{2,3},{3,2},{4,5},{5,4},{6,7},{7,6},{8,9},{9,8},{10,11... | collective-permute-start | bytes 3145736 | tf_op jit(solution)/shard_map/ppermute | solution.py:43
  123.5 66.1 %collective-permute-start.61 = (bf16[256,2048]{1,0:T(8,128)(2,1)S(1)}, bf16[256,2048]{1,0:T(8,128)(2,1)}, u32[]{:S(2)}, u32[]{:S(2)}) collective-permute-start(bf16[256,2048]{1,0:T(8,128)(2,1)S(1)} %copy-done.24), channel_id=1, source_target_pairs={{0,2},{2,0},{1,3},{3,1},{4,6},{6,4},{5,7},{7,5},{8,10},{10,8},{9,1... | collective-permute-start | bytes 3145736 | tf_op jit(solution)/shard_map/ppermute | solution.py:43
  126.2 65.4 %collective-permute-start.15 = (bf16[256,2048]{1,0:T(8,128)(2,1)S(1)}, bf16[256,2048]{1,0:T(8,128)(2,1)S(1)}, u32[]{:S(2)}, u32[]{:S(2)}) collective-permute-start(bf16[256,2048]{1,0:T(8,128)(2,1)S(1)} %collective-permute-done.13), channel_id=1, source_target_pairs={{0,1},{1,0},{2,3},{3,2},{4,5},{5,4},{6,7},{7,6},{8,9},{9,8},{10,11... | collective-permute-start | bytes 3145736 | tf_op jit(solution)/shard_map/ppermute | solution.py:43
  157.1 41.5 %collective-permute-start.51 = (bf16[256,2048]{1,0:T(8,128)(2,1)S(1)}, bf16[256,2048]{1,0:T(8,128)(2,1)S(1)}, u32[]{:S(2)}, u32[]{:S(2)}) collective-permute-start(bf16[256,2048]{1,0:T(8,128)(2,1)S(1)} %get-tuple-element.109), channel_id=1, source_target_pairs={{0,2},{2,0},{1,3},{3,1},{4,6},{6,4},{5,7},{7,5},{8,10},{10,8},{9,1... | collective-permute-start | bytes 3145736 | tf_op jit(solution)/shard_map/ppermute | solution.py:43
  189.5 53.5 %collective-permute-start.74 = (bf16[256,2048]{1,0:T(8,128)(2,1)S(1)}, bf16[256,2048]{1,0:T(8,128)(2,1)}, u32[]{:S(2)}, u32[]{:S(2)}) collective-permute-start(bf16[256,2048]{1,0:T(8,128)(2,1)S(1)} %get-tuple-element.34), channel_id=1, source_target_pairs={{0,2},{2,0},{1,3},{3,1},{4,6},{6,4},{5,7},{7,5},{8,10},{10,8},{9,1... | collective-permute-start | bytes 3145736 | tf_op jit(solution)/shard_map/ppermute | solution.py:43
  191.6 60.9 %collective-permute-start.63 = (bf16[256,2048]{1,0:T(8,128)(2,1)}, bf16[256,2048]{1,0:T(8,128)(2,1)}, u32[]{:S(2)}, u32[]{:S(2)}) collective-permute-start(bf16[256,2048]{1,0:T(8,128)(2,1)} %collective-permute-done.61), channel_id=1, source_target_pairs={{0,1},{1,0},{2,3},{3,2},{4,5},{5,4},{6,7},{7,6},{8,9},{9,8},{10,11... | collective-permute-start | bytes 3145736 | tf_op jit(solution)/shard_map/ppermute | solution.py:43
  218.7 41.9 %collective-permute-start.26 = (bf16[512,2048]{1,0:T(8,128)(2,1)}, bf16[512,2048]{1,0:T(8,128)(2,1)}, u32[]{:S(2)}, u32[]{:S(2)}) collective-permute-start(bf16[512,2048]{1,0:T(8,128)(2,1)} %convolution_convert_fusion.9), channel_id=1, source_target_pairs={{0,1},{1,0},{2,3},{3,2},{4,5},{5,4},{6,7},{7,6},{8,9},{9,8},{10,11... | collective-permute-start | bytes 6291464 | tf_op jit(solution)/shard_map/ppermute | solution.py:43
  252.5 33.2 %collective-permute-start.32 = (bf16[512,1024]{1,0:T(8,128)(2,1)}, bf16[512,1024]{1,0:T(8,128)(2,1)S(1)}, u32[]{:S(2)}, u32[]{:S(2)}) collective-permute-start(bf16[512,1024]{1,0:T(8,128)(2,1)} %param.25), channel_id=1, source_target_pairs={{0,16},{16,0},{1,17},{17,1},{2,18},{18,2},{3,19},{19,3},{4,20},{20... | collective-permute-start | bytes 3145736 | tf_op jit(solution)/shard_map/ppermute | solution.py:43
  265.2 65.2 %collective-permute-start.27 = (bf16[256,2048]{1,0:T(8,128)(2,1)}, bf16[256,2048]{1,0:T(8,128)(2,1)}, u32[]{:S(2)}, u32[]{:S(2)}) collective-permute-start(bf16[256,2048]{1,0:T(8,128)(2,1)} %slice.994), channel_id=1, source_target_pairs={{0,2},{2,0},{1,3},{3,1},{4,6},{6,4},{5,7},{7,5},{8,10},{10,8},{9,1... | collective-permute-start | bytes 3145736 | tf_op jit(solution)/shard_map/ppermute | solution.py:43
  270.6 81.4 %collective-permute-start.55 = (bf16[256,2048]{1,0:T(8,128)(2,1)}, bf16[256,2048]{1,0:T(8,128)(2,1)}, u32[]{:S(2)}, u32[]{:S(2)}) collective-permute-start(bf16[256,2048]{1,0:T(8,128)(2,1)} %slice.992), channel_id=1, source_target_pairs={{0,2},{2,0},{1,3},{3,1},{4,6},{6,4},{5,7},{7,5},{8,10},{10,8},{9,1... | collective-permute-start | bytes 3145736 | tf_op jit(solution)/shard_map/ppermute | solution.py:43
  273.1 82.7 %collective-permute-start.35 = (bf16[512,1024]{1,0:T(8,128)(2,1)}, bf16[512,1024]{1,0:T(8,128)(2,1)}, u32[]{:S(2)}, u32[]{:S(2)}) collective-permute-start(bf16[512,1024]{1,0:T(8,128)(2,1)} %param.25), channel_id=1, source_target_pairs={{0,4},{4,0},{1,5},{5,1},{2,6},{6,2},{3,7},{7,3},{8,12},{12,8},{9,1... | collective-permute-start | bytes 3145736 | tf_op jit(solution)/shard_map/ppermute | solution.py:69
  285.9 120.0 %collective-permute-start.44 = (bf16[1024,512]{1,0:T(8,128)(2,1)}, bf16[1024,512]{1,0:T(8,128)(2,1)}, u32[]{:S(2)}, u32[]{:S(2)}) collective-permute-start(bf16[1024,512]{1,0:T(8,128)(2,1)} %param.27), channel_id=1, source_target_pairs={{0,4},{4,0},{1,5},{5,1},{2,6},{6,2},{3,7},{7,3},{8,12},{12,8},{9,1... | collective-permute-start | bytes 3145736 | tf_op jit(solution)/shard_map/ppermute | solution.py:69
  296.2 74.3 %collective-permute-start.41 = (bf16[1024,512]{1,0:T(8,128)(2,1)}, bf16[1024,512]{1,0:T(8,128)(2,1)S(1)}, u32[]{:S(2)}, u32[]{:S(2)}) collective-permute-start(bf16[1024,512]{1,0:T(8,128)(2,1)} %param.27), channel_id=1, source_target_pairs={{0,16},{16,0},{1,17},{17,1},{2,18},{18,2},{3,19},{19,3},{4,20},{20... | collective-permute-start | bytes 3145736 | tf_op jit(solution)/shard_map/ppermute | solution.py:43
  357.4 49.4 %collective-permute-start.37 = (bf16[512,1024]{1,0:T(8,128)(2,1)}, bf16[512,1024]{1,0:T(8,128)(2,1)S(1)}, u32[]{:S(2)}, u32[]{:S(2)}) collective-permute-start(bf16[512,1024]{1,0:T(8,128)(2,1)} %collective-permute-done.35), channel_id=1, source_target_pairs={{0,16},{16,0},{1,17},{17,1},{2,18},{18,2},{3,19},{19,3},{4,20},{20... | collective-permute-start | bytes 3145736 | tf_op jit(solution)/shard_map/ppermute | solution.py:43
  367.7 37.0 %collective-permute-start.36 = (bf16[512,1024]{1,0:T(8,128)(2,1)}, bf16[512,1024]{1,0:T(8,128)(2,1)S(1)}, u32[]{:S(2)}, u32[]{:S(2)}) collective-permute-start(bf16[512,1024]{1,0:T(8,128)(2,1)} %collective-permute-done.35), channel_id=1, source_target_pairs={{0,8},{8,0},{1,9},{9,1},{2,10},{10,2},{3,11},{11,3},{4,12},{12,4},... | collective-permute-start | bytes 3145736 | tf_op jit(solution)/shard_map/ppermute | solution.py:43
  370.5 37.7 %collective-permute-start.28 = (bf16[256,2048]{1,0:T(8,128)(2,1)S(1)}, bf16[256,2048]{1,0:T(8,128)(2,1)S(1)}, u32[]{:S(2)}, u32[]{:S(2)}) collective-permute-start(bf16[256,2048]{1,0:T(8,128)(2,1)S(1)} %get-tuple-element.95), channel_id=1, source_target_pairs={{0,2},{2,0},{1,3},{3,1},{4,6},{6,4},{5,7},{7,5},{8,10},{10,8},{9,1... | collective-permute-start | bytes 3145736 | tf_op jit(solution)/shard_map/ppermute | solution.py:43
  382.2 39.4 %collective-permute-start.43 = (bf16[512,512]{1,0:T(8,128)(2,1)S(1)}, bf16[512,512]{1,0:T(8,128)(2,1)S(1)}, u32[]{:S(2)}, u32[]{:S(2)}) collective-permute-start(bf16[512,512]{1,0:T(8,128)(2,1)S(1)} %slice.763), channel_id=1, source_target_pairs={{0,8},{8,0},{1,9},{9,1},{2,10},{10,2},{3,11},{11,3},{4,12},{12,4},... | collective-permute-start | bytes 1572872 | tf_op jit(solution)/shard_map/ppermute | solution.py:43
  405.9 45.8 %collective-permute-start.46 = (bf16[1024,512]{1,0:T(8,128)(2,1)}, bf16[1024,512]{1,0:T(8,128)(2,1)S(1)}, u32[]{:S(2)}, u32[]{:S(2)}) collective-permute-start(bf16[1024,512]{1,0:T(8,128)(2,1)} %collective-permute-done.44), channel_id=1, source_target_pairs={{0,16},{16,0},{1,17},{17,1},{2,18},{18,2},{3,19},{19,3},{4,20},{20... | collective-permute-start | bytes 3145736 | tf_op jit(solution)/shard_map/ppermute | solution.py:43
  416.4 36.9 %collective-permute-start.56 = (bf16[256,2048]{1,0:T(8,128)(2,1)S(1)}, bf16[256,2048]{1,0:T(8,128)(2,1)S(1)}, u32[]{:S(2)}, u32[]{:S(2)}) collective-permute-start(bf16[256,2048]{1,0:T(8,128)(2,1)S(1)} %get-tuple-element.93), channel_id=1, source_target_pairs={{0,2},{2,0},{1,3},{3,1},{4,6},{6,4},{5,7},{7,5},{8,10},{10,8},{9,1... | collective-permute-start | bytes 3145736 | tf_op jit(solution)/shard_map/ppermute | solution.py:43
  419.5 30.9 %collective-permute-start.38 = (bf16[256,1024]{1,0:T(8,128)(2,1)S(1)}, bf16[256,1024]{1,0:T(8,128)(2,1)S(1)}, u32[]{:S(2)}, u32[]{:S(2)}) collective-permute-start(bf16[256,1024]{1,0:T(8,128)(2,1)S(1)} %slice.758), channel_id=1, source_target_pairs={{0,16},{16,0},{1,17},{17,1},{2,18},{18,2},{3,19},{19,3},{4,20},{20... | collective-permute-start | bytes 1572872 | tf_op jit(solution)/shard_map/ppermute | solution.py:43
  421.6 31.6 %collective-permute-start.39 = (bf16[256,1024]{1,0:T(8,128)(2,1)S(1)}, bf16[256,1024]{1,0:T(8,128)(2,1)S(1)}, u32[]{:S(2)}, u32[]{:S(2)}) collective-permute-start(bf16[256,1024]{1,0:T(8,128)(2,1)S(1)} %slice.759), channel_id=1, source_target_pairs={{0,8},{8,0},{1,9},{9,1},{2,10},{10,2},{3,11},{11,3},{4,12},{12,4},... | collective-permute-start | bytes 1572872 | tf_op jit(solution)/shard_map/ppermute | solution.py:43
  546.1 53.2 %collective-permute-start.137 = (f32[1024]{0:T(1024)S(1)}, f32[1024]{0:T(1024)S(1)}, u32[]{:S(2)}, u32[]{:S(2)}) collective-permute-start(f32[1024]{0:T(1024)S(1)} %slice.816), channel_id=1, source_target_pairs={{0,4},{4,0},{1,5},{5,1},{2,6},{6,2},{3,7},{7,3},{8,12},{12,8},{9,1... | collective-permute-start | bytes 12296 | tf_op jit(solution)/shard_map/ppermute | solution.py:69
  571.3 35.1 %collective-permute-start.130 = (bf16[256,1024]{1,0:T(8,128)(2,1)S(1)}, bf16[256,1024]{1,0:T(8,128)(2,1)S(1)}, u32[]{:S(2)}, u32[]{:S(2)}) collective-permute-start(bf16[256,1024]{1,0:T(8,128)(2,1)S(1)} %get-tuple-element.136), channel_id=1, source_target_pairs={{0,8},{8,0},{1,9},{9,1},{2,10},{10,2},{3,11},{11,3},{4,12},{12,4},... | collective-permute-start | bytes 1572872 | tf_op jit(solution)/shard_map/ppermute | solution.py:43
  573.4 35.3 %collective-permute-start.125 = (bf16[256,1024]{1,0:T(8,128)(2,1)S(1)}, bf16[256,1024]{1,0:T(8,128)(2,1)S(1)}, u32[]{:S(2)}, u32[]{:S(2)}) collective-permute-start(bf16[256,1024]{1,0:T(8,128)(2,1)S(1)} %get-tuple-element.138), channel_id=1, source_target_pairs={{0,8},{8,0},{1,9},{9,1},{2,10},{10,2},{3,11},{11,3},{4,12},{12,4},... | collective-permute-start | bytes 1572872 | tf_op jit(solution)/shard_map/ppermute | solution.py:43
  574.7 45.2 %collective-permute-start.124 = (bf16[256,1024]{1,0:T(8,128)(2,1)S(1)}, bf16[256,1024]{1,0:T(8,128)(2,1)S(1)}, u32[]{:S(2)}, u32[]{:S(2)}) collective-permute-start(bf16[256,1024]{1,0:T(8,128)(2,1)S(1)} %get-tuple-element.139), channel_id=1, source_target_pairs={{0,8},{8,0},{1,9},{9,1},{2,10},{10,2},{3,11},{11,3},{4,12},{12,4},... | collective-permute-start | bytes 1572872 | tf_op jit(solution)/shard_map/ppermute | solution.py:43
  605.5 35.2 %collective-permute-start.133 = (bf16[256,1024]{1,0:T(8,128)(2,1)}, bf16[256,1024]{1,0:T(8,128)(2,1)}, u32[]{:S(2)}, u32[]{:S(2)}) collective-permute-start(bf16[256,1024]{1,0:T(8,128)(2,1)} %get-tuple-element.140), channel_id=1, source_target_pairs={{0,16},{16,0},{1,17},{17,1},{2,18},{18,2},{3,19},{19,3},{4,20},{20... | collective-permute-start | bytes 1572872 | tf_op jit(solution)/shard_map/ppermute | solution.py:43
  606.4 34.8 %collective-permute-start.135 = (bf16[256,1024]{1,0:T(8,128)(2,1)}, bf16[256,1024]{1,0:T(8,128)(2,1)}, u32[]{:S(2)}, u32[]{:S(2)}) collective-permute-start(bf16[256,1024]{1,0:T(8,128)(2,1)} %get-tuple-element.141), channel_id=1, source_target_pairs={{0,16},{16,0},{1,17},{17,1},{2,18},{18,2},{3,19},{19,3},{4,20},{20... | collective-permute-start | bytes 1572872 | tf_op jit(solution)/shard_map/ppermute | solution.py:43
  608.7 34.4 %collective-permute-start.127 = (bf16[256,1024]{1,0:T(8,128)(2,1)}, bf16[256,1024]{1,0:T(8,128)(2,1)}, u32[]{:S(2)}, u32[]{:S(2)}) collective-permute-start(bf16[256,1024]{1,0:T(8,128)(2,1)} %get-tuple-element.142), channel_id=1, source_target_pairs={{0,16},{16,0},{1,17},{17,1},{2,18},{18,2},{3,19},{19,3},{4,20},{20... | collective-permute-start | bytes 1572872 | tf_op jit(solution)/shard_map/ppermute | solution.py:43
  619.9 34.4 %collective-permute-start.129 = (bf16[256,1024]{1,0:T(8,128)(2,1)}, bf16[256,1024]{1,0:T(8,128)(2,1)}, u32[]{:S(2)}, u32[]{:S(2)}) collective-permute-start(bf16[256,1024]{1,0:T(8,128)(2,1)} %get-tuple-element.143), channel_id=1, source_target_pairs={{0,16},{16,0},{1,17},{17,1},{2,18},{18,2},{3,19},{19,3},{4,20},{20... | collective-permute-start | bytes 1572872 | tf_op jit(solution)/shard_map/ppermute | solution.py:43
  627.8 37.8 %collective-permute-start.132 = (bf16[256,1024]{1,0:T(8,128)(2,1)}, bf16[256,1024]{1,0:T(8,128)(2,1)}, u32[]{:S(2)}, u32[]{:S(2)}) collective-permute-start(bf16[256,1024]{1,0:T(8,128)(2,1)} %add_convert_fusion.14), channel_id=1, source_target_pairs={{0,16},{16,0},{1,17},{17,1},{2,18},{18,2},{3,19},{19,3},{4,20},{20... | collective-permute-start | bytes 1572872 | tf_op jit(solution)/shard_map/ppermute | solution.py:43
  640.7 38.5 %collective-permute-start.146 = (bf16[512,512]{1,0:T(8,128)(2,1)}, bf16[512,512]{1,0:T(8,128)(2,1)}, u32[]{:S(2)}, u32[]{:S(2)}) collective-permute-start(bf16[512,512]{1,0:T(8,128)(2,1)} %get-tuple-element.121), channel_id=1, source_target_pairs={{0,8},{8,0},{1,9},{9,1},{2,10},{10,2},{3,11},{11,3},{4,12},{12,4},... | collective-permute-start | bytes 1572872 | tf_op jit(solution)/shard_map/ppermute | solution.py:43
  641.2 38.5 %collective-permute-start.141 = (bf16[512,512]{1,0:T(8,128)(2,1)S(1)}, bf16[512,512]{1,0:T(8,128)(2,1)}, u32[]{:S(2)}, u32[]{:S(2)}) collective-permute-start(bf16[512,512]{1,0:T(8,128)(2,1)S(1)} %get-tuple-element.123), channel_id=1, source_target_pairs={{0,8},{8,0},{1,9},{9,1},{2,10},{10,2},{3,11},{11,3},{4,12},{12,4},... | collective-permute-start | bytes 1572872 | tf_op jit(solution)/shard_map/ppermute | solution.py:43
  643.1 37.9 %collective-permute-start.149 = (bf16[512,512]{1,0:T(8,128)(2,1)S(1)}, bf16[512,512]{1,0:T(8,128)(2,1)}, u32[]{:S(2)}, u32[]{:S(2)}) collective-permute-start(bf16[512,512]{1,0:T(8,128)(2,1)S(1)} %get-tuple-element.125), channel_id=1, source_target_pairs={{0,16},{16,0},{1,17},{17,1},{2,18},{18,2},{3,19},{19,3},{4,20},{20... | collective-permute-start | bytes 1572872 | tf_op jit(solution)/shard_map/ppermute | solution.py:43
  654.3 33.7 %collective-permute-start.143 = (bf16[512,512]{1,0:T(8,128)(2,1)S(1)}, bf16[512,512]{1,0:T(8,128)(2,1)}, u32[]{:S(2)}, u32[]{:S(2)}) collective-permute-start(bf16[512,512]{1,0:T(8,128)(2,1)S(1)} %get-tuple-element.127), channel_id=1, source_target_pairs={{0,16},{16,0},{1,17},{17,1},{2,18},{18,2},{3,19},{19,3},{4,20},{20... | collective-permute-start | bytes 1572872 | tf_op jit(solution)/shard_map/ppermute | solution.py:43
  665.6 33.7 %collective-permute-start.148 = (bf16[512,512]{1,0:T(8,128)(2,1)}, bf16[512,512]{1,0:T(8,128)(2,1)}, u32[]{:S(2)}, u32[]{:S(2)}) collective-permute-start(bf16[512,512]{1,0:T(8,128)(2,1)} %add_convert_fusion.8), channel_id=1, source_target_pairs={{0,16},{16,0},{1,17},{17,1},{2,18},{18,2},{3,19},{19,3},{4,20},{20... | collective-permute-start | bytes 1572872 | tf_op jit(solution)/shard_map/ppermute | solution.py:43
  679.2 33.0 %collective-permute-start.140 = (bf16[512,512]{1,0:T(8,128)(2,1)S(1)}, bf16[512,512]{1,0:T(8,128)(2,1)S(1)}, u32[]{:S(2)}, u32[]{:S(2)}) collective-permute-start(bf16[512,512]{1,0:T(8,128)(2,1)S(1)} %get-tuple-element.124), channel_id=1, source_target_pairs={{0,8},{8,0},{1,9},{9,1},{2,10},{10,2},{3,11},{11,3},{4,12},{12,4},... | collective-permute-start | bytes 1572872 | tf_op jit(solution)/shard_map/ppermute | solution.py:43
  679.7 32.6 %collective-permute-start.151 = (bf16[512,512]{1,0:T(8,128)(2,1)S(1)}, bf16[512,512]{1,0:T(8,128)(2,1)S(1)}, u32[]{:S(2)}, u32[]{:S(2)}) collective-permute-start(bf16[512,512]{1,0:T(8,128)(2,1)S(1)} %get-tuple-element.126), channel_id=1, source_target_pairs={{0,16},{16,0},{1,17},{17,1},{2,18},{18,2},{3,19},{19,3},{4,20},{20... | collective-permute-start | bytes 1572872 | tf_op jit(solution)/shard_map/ppermute | solution.py:43
  681.0 33.5 %collective-permute-start.126 = (bf16[256,1024]{1,0:T(8,128)(2,1)S(1)}, bf16[256,1024]{1,0:T(8,128)(2,1)S(1)}, u32[]{:S(2)}, u32[]{:S(2)}) collective-permute-start(bf16[256,1024]{1,0:T(8,128)(2,1)S(1)} %get-tuple-element.133), channel_id=1, source_target_pairs={{0,16},{16,0},{1,17},{17,1},{2,18},{18,2},{3,19},{19,3},{4,20},{20... | collective-permute-start | bytes 1572872 | tf_op jit(solution)/shard_map/ppermute | solution.py:43
  712.2 31.7 %collective-permute-start.77 = (bf16[512,2048]{1,0:T(8,128)(2,1)S(1)}, bf16[512,2048]{1,0:T(8,128)(2,1)S(1)}, u32[]{:S(2)}, u32[]{:S(2)}) collective-permute-start(bf16[512,2048]{1,0:T(8,128)(2,1)S(1)} %copy-done.107), channel_id=1, source_target_pairs={{0,1},{1,0},{2,3},{3,2},{4,5},{5,4},{6,7},{7,6},{8,9},{9,8},{10,11... | collective-permute-start | bytes 6291464 | tf_op jit(solution)/shard_map/ppermute | solution.py:43
  730.5 49.8 %collective-permute-start.59 = (bf16[512,2048]{1,0:T(8,128)(2,1)}, bf16[512,2048]{1,0:T(8,128)(2,1)}, u32[]{:S(2)}, u32[]{:S(2)}) collective-permute-start(bf16[512,2048]{1,0:T(8,128)(2,1)} %convolution_convert_fusion.6), channel_id=1, source_target_pairs={{0,1},{1,0},{2,3},{3,2},{4,5},{5,4},{6,7},{7,6},{8,9},{9,8},{10,11... | collective-permute-start | bytes 6291464 | tf_op jit(solution)/shard_map/ppermute | solution.py:43
  738.1 32.9 %collective-permute-start.64 = (bf16[512,2048]{1,0:T(8,128)(2,1)}, bf16[512,2048]{1,0:T(8,128)(2,1)}, u32[]{:S(2)}, u32[]{:S(2)}) collective-permute-start(bf16[512,2048]{1,0:T(8,128)(2,1)} %convolution_convert_fusion.5), channel_id=1, source_target_pairs={{0,1},{1,0},{2,3},{3,2},{4,5},{5,4},{6,7},{7,6},{8,9},{9,8},{10,11... | collective-permute-start | bytes 6291464 | tf_op jit(solution)/shard_map/ppermute | solution.py:43
  739.4 163.0 %collective-permute-start.139 = (f32[1024]{0:T(1024)S(1)}, f32[1024]{0:T(1024)S(1)}, u32[]{:S(2)}, u32[]{:S(2)}) collective-permute-start(f32[1024]{0:T(1024)S(1)} %add.953), channel_id=1, source_target_pairs={{0,8},{8,0},{1,9},{9,1},{2,10},{10,2},{3,11},{11,3},{4,12},{12,4},... | collective-permute-start | bytes 12296 | tf_op jit(solution)/shard_map/ppermute | solution.py:43
  745.2 180.9 %collective-permute-start.136 = (bf16[512,1024]{1,0:T(8,128)(2,1)}, bf16[512,1024]{1,0:T(8,128)(2,1)}, u32[]{:S(2)}, u32[]{:S(2)}) collective-permute-start(bf16[512,1024]{1,0:T(8,128)(2,1)} %pad_maximum_fusion.2), channel_id=1, source_target_pairs={{0,4},{4,0},{1,5},{5,1},{2,6},{6,2},{3,7},{7,3},{8,12},{12,8},{9,1... | collective-permute-start | bytes 3145736 | tf_op jit(solution)/shard_map/ppermute | solution.py:69
  759.7 91.4 %collective-permute-start.78 = (bf16[256,2048]{1,0:T(8,128)(2,1)}, bf16[256,2048]{1,0:T(8,128)(2,1)S(1)}, u32[]{:S(2)}, u32[]{:S(2)}) collective-permute-start(bf16[256,2048]{1,0:T(8,128)(2,1)} %slice.987), channel_id=1, source_target_pairs={{0,2},{2,0},{1,3},{3,1},{4,6},{6,4},{5,7},{7,5},{8,10},{10,8},{9,1... | collective-permute-start | bytes 3145736 | tf_op jit(solution)/shard_map/ppermute | solution.py:43
  772.0 80.5 %collective-permute-start.50 = (bf16[256,2048]{1,0:T(8,128)(2,1)}, bf16[256,2048]{1,0:T(8,128)(2,1)}, u32[]{:S(2)}, u32[]{:S(2)}) collective-permute-start(bf16[256,2048]{1,0:T(8,128)(2,1)} %slice.993), channel_id=1, source_target_pairs={{0,2},{2,0},{1,3},{3,1},{4,6},{6,4},{5,7},{7,5},{8,10},{10,8},{9,1... | collective-permute-start | bytes 3145736 | tf_op jit(solution)/shard_map/ppermute | solution.py:43
  780.3 69.6 %collective-permute-start.65 = (bf16[256,2048]{1,0:T(8,128)(2,1)S(1)}, bf16[256,2048]{1,0:T(8,128)(2,1)S(1)}, u32[]{:S(2)}, u32[]{:S(2)}) collective-permute-start(bf16[256,2048]{1,0:T(8,128)(2,1)S(1)} %slice.990), channel_id=1, source_target_pairs={{0,2},{2,0},{1,3},{3,1},{4,6},{6,4},{5,7},{7,5},{8,10},{10,8},{9,1... | collective-permute-start | bytes 3145736 | tf_op jit(solution)/shard_map/ppermute | solution.py:43
  849.8 81.6 %collective-permute-start.152 = (bf16[1024,512]{1,0:T(8,128)(2,1)S(1)}, bf16[1024,512]{1,0:T(8,128)(2,1)S(1)}, u32[]{:S(2)}, u32[]{:S(2)}) collective-permute-start(bf16[1024,512]{1,0:T(8,128)(2,1)S(1)} %copy-done.58), channel_id=1, source_target_pairs={{0,4},{4,0},{1,5},{5,1},{2,6},{6,2},{3,7},{7,3},{8,12},{12,8},{9,1... | collective-permute-start | bytes 3145736 | tf_op jit(solution)/shard_map/ppermute | solution.py:69
  851.1 45.4 %collective-permute-start.60 = (bf16[256,2048]{1,0:T(8,128)(2,1)S(1)}, bf16[256,2048]{1,0:T(8,128)(2,1)S(1)}, u32[]{:S(2)}, u32[]{:S(2)}) collective-permute-start(bf16[256,2048]{1,0:T(8,128)(2,1)S(1)} %slice.991), channel_id=1, source_target_pairs={{0,2},{2,0},{1,3},{3,1},{4,6},{6,4},{5,7},{7,5},{8,10},{10,8},{9,1... | collective-permute-start | bytes 3145736 | tf_op jit(solution)/shard_map/ppermute | solution.py:43
  899.0 32.4 %collective-permute-start.66 = (bf16[256,2048]{1,0:T(8,128)(2,1)S(1)}, bf16[256,2048]{1,0:T(8,128)(2,1)S(1)}, u32[]{:S(2)}, u32[]{:S(2)}) collective-permute-start(bf16[256,2048]{1,0:T(8,128)(2,1)S(1)} %get-tuple-element.107), channel_id=1, source_target_pairs={{0,2},{2,0},{1,3},{3,1},{4,6},{6,4},{5,7},{7,5},{8,10},{10,8},{9,1... | collective-permute-start | bytes 3145736 | tf_op jit(solution)/shard_map/ppermute | solution.py:43
  902.9 35.5 %collective-permute-start.67 = (bf16[256,2048]{1,0:T(8,128)(2,1)S(1)}, bf16[256,2048]{1,0:T(8,128)(2,1)S(1)}, u32[]{:S(2)}, u32[]{:S(2)}) collective-permute-start(bf16[256,2048]{1,0:T(8,128)(2,1)S(1)} %get-tuple-element.107), channel_id=1, source_target_pairs={{0,1},{1,0},{2,3},{3,2},{4,5},{5,4},{6,7},{7,6},{8,9},{9,8},{10,11... | collective-permute-start | bytes 3145736 | tf_op jit(solution)/shard_map/ppermute | solution.py:43
  1107.7 52.2 %collective-permute-start.82 = (bf16[512,2048]{1,0:T(8,128)(2,1)S(1)}, bf16[512,2048]{1,0:T(8,128)(2,1)S(1)}, u32[]{:S(2)}, u32[]{:S(2)}) collective-permute-start(bf16[512,2048]{1,0:T(8,128)(2,1)S(1)} %copy-done.106), channel_id=1, source_target_pairs={{0,1},{1,0},{2,3},{3,2},{4,5},{5,4},{6,7},{7,6},{8,9},{9,8},{10,11... | collective-permute-start | bytes 6291464 | tf_op jit(solution)/shard_map/ppermute | solution.py:43
  1155.7 30.7 %collective-permute-start.118 = (bf16[256,512]{1,0:T(8,128)(2,1)S(1)}, bf16[256,512]{1,0:T(8,128)(2,1)S(1)}, u32[]{:S(2)}, u32[]{:S(2)}) collective-permute-start(bf16[256,512]{1,0:T(8,128)(2,1)S(1)} %pad_maximum_fusion.13), channel_id=1, source_target_pairs={{0,4},{4,0},{1,5},{5,1},{2,6},{6,2},{3,7},{7,3},{8,12},{12,8},{9,1... | collective-permute-start | bytes 786440 | tf_op jit(solution)/shard_map/ppermute | solution.py:69
  1159.8 45.4 %collective-permute-start.101 = (bf16[512,768]{0,1:T(8,128)(2,1)S(1)}, bf16[512,768]{0,1:T(8,128)(2,1)S(1)}, u32[]{:S(2)}, u32[]{:S(2)}) collective-permute-start(bf16[512,768]{0,1:T(8,128)(2,1)S(1)} %pad_maximum_fusion.12), channel_id=1, source_target_pairs={{0,4},{4,0},{1,5},{5,1},{2,6},{6,2},{3,7},{7,3},{8,12},{12,8},{9,1... | collective-permute-start | bytes 2359304 | tf_op jit(solution)/shard_map/ppermute | solution.py:69
  1167.8 48.9 %collective-permute-start.70 = (bf16[256,2048]{1,0:T(8,128)(2,1)}, bf16[256,2048]{1,0:T(8,128)(2,1)}, u32[]{:S(2)}, u32[]{:S(2)}) collective-permute-start(bf16[256,2048]{1,0:T(8,128)(2,1)} %slice.989), channel_id=1, source_target_pairs={{0,2},{2,0},{1,3},{3,1},{4,6},{6,4},{5,7},{7,5},{8,10},{10,8},{9,1... | collective-permute-start | bytes 3145736 | tf_op jit(solution)/shard_map/ppermute | solution.py:43
  1186.4 60.9 %collective-permute-start.73 = (bf16[256,2048]{1,0:T(8,128)(2,1)}, bf16[256,2048]{1,0:T(8,128)(2,1)}, u32[]{:S(2)}, u32[]{:S(2)}) collective-permute-start(bf16[256,2048]{1,0:T(8,128)(2,1)} %fusion.139), channel_id=1, source_target_pairs={{4,0},{5,1},{6,2},{7,3},{12,8},{13,9},{14,10},{15,11},{20,16},{21,... | collective-permute-start | bytes 3145736 | tf_op jit(solution)/shard_map/ppermute | solution.py:516
  1187.7 69.5 %collective-permute-start.83 = (bf16[256,2048]{1,0:T(8,128)(2,1)}, bf16[256,2048]{1,0:T(8,128)(2,1)S(1)}, u32[]{:S(2)}, u32[]{:S(2)}) collective-permute-start(bf16[256,2048]{1,0:T(8,128)(2,1)} %slice.986), channel_id=1, source_target_pairs={{0,2},{2,0},{1,3},{3,1},{4,6},{6,4},{5,7},{7,5},{8,10},{10,8},{9,1... | collective-permute-start | bytes 3145736 | tf_op jit(solution)/shard_map/ppermute | solution.py:43
  (209 other events, 5298.4 us)

commit v2 on v1

v2 whole, which is shorter than its diff:
```python
import functools

import jax
import jax.numpy as jnp
from jax import lax
from jax.experimental import pallas as pl
from jax.experimental.pallas import tpu as pltpu
from jax.sharding import Mesh, PartitionSpec as P

HDIM = 128
EPSILON = 1e-05
MASKED = -1e30
LOG2E = 1.4426950408889634
F32 = jnp.float32
BF16 = jnp.bfloat16
VMEM_LIMIT = 48 * 1024 * 1024
KERNEL_VMEM = 63 * 1024 * 1024
DP = ("e", "b", "a")
TP = ("g", "h", "c")
SLOTS = (0, 2, 1, 3)


def dot(x, y, contract=((1,), (0,))):
    return lax.dot_general(x, y, (contract, ((), ())), preferred_element_type=F32)


def stats(rows):
    mean = jnp.mean(rows, axis=-1, keepdims=True)
    center = rows - mean
    inverse = lax.rsqrt(jnp.mean(center * center, axis=-1, keepdims=True) + EPSILON)
    return center * inverse, inverse


def norm_back(grad_normed, scaled, inverse, gain):
    weighted = grad_normed * gain
    return inverse * (
        weighted
        - jnp.mean(weighted, axis=-1, keepdims=True)
        - scaled * jnp.mean(weighted * scaled, axis=-1, keepdims=True)
    )


def flip(x, axis):
    return lax.ppermute(x, axis, [(0, 1), (1, 0)])


def scatter4(product):
    away = product(1).astype(BF16)
    kept = product(0) + flip(away, "c").astype(F32)
    local = kept.shape[0] // 2
    return kept[:local] + flip(kept[local:].astype(BF16), "h").astype(F32)


def turn(x, groups, by, axes=("e", "g")):
    extra, count = groups
    pairs = []
    for e in range(extra):
        for g in range(count):
            pairs.append((e * count + g, (e + by[0]) % extra * count + (g + by[1]) % count))
    return lax.ppermute(x, axes, pairs)


def sum_axis(x, axis):
    if lax.axis_size(axis) == 1:
        return x
    if lax.axis_size(axis) == 2:
        return x + flip(x, axis)
    return jnp.sum(lax.all_gather(x, axis), 0)


def row_blocks(place, count, size):
    found = []
    for j in range(count):
        other = jnp.bitwise_xor(place, j)
        slot = (other >> 1) + 2 * (other & 1)
        found.append(pl.multiple_of(slot * size, size))
    return found


def causal(size):
    keys = lax.broadcasted_iota(jnp.int32, (size, size), 0)
    queries = lax.broadcasted_iota(jnp.int32, (size, size), 1)
    return keys <= queries


def first_key(block, size, segment):
    return 0 if segment is None else block * size // segment * segment


class Copies:
    def __init__(self, send, recv, near):
        self.send, self.recv, self.near = send, recv, near
        self.remotes, self.locals = 0, 0
        self.open_sends, self.open_locals = [], []

    def remote(self, source, target, device, tracked=True):
        copy = pltpu.make_async_remote_copy(
            src_ref=source,
            dst_ref=target,
            send_sem=self.send.at[self.remotes],
            recv_sem=self.recv.at[self.remotes],
            device_id=device,
            device_id_type=pl.DeviceIdType.MESH,
        )
        self.remotes += 1
        if tracked:
            copy.start()
            self.open_sends.append(copy)
        return copy

    def local(self, source, target, tracked=True):
        copy = pltpu.make_async_copy(source, target, self.near.at[self.locals])
        self.locals += 1
        copy.start()
        if tracked:
            self.open_locals.append(copy)
        return copy

    def sent(self, copy):
        copy.wait_send()
        self.open_sends = [c for c in self.open_sends if c is not copy]

    def finish(self):
        for copy in self.open_sends:
            copy.wait_send()
        for copy in self.open_locals:
            copy.wait()


class Places:
    def __init__(self, extra, groups):
        self.extra, self.groups = extra, groups
        self.e, self.b, self.a, self.g, self.h, self.c = (lax.axis_index(n) for n in DP + TP)
        self.to_a, self.to_b = {"a": 1 - self.a}, {"b": 1 - self.b}
        self.to_h, self.to_c = {"h": 1 - self.h}, {"c": 1 - self.c}
        self.offsets = [(e, g) for g in range(groups) for e in range(extra)]

    def further(self, offset):
        return {
            "e": lax.rem(self.e + offset[0] + self.extra, self.extra),
            "g": lax.rem(self.g + offset[1] + self.groups, self.groups),
        }

    def share(self, offset, i, j):
        e = lax.rem(self.e - offset[0] + self.extra, self.extra)
        b = self.b if i == 0 else 1 - self.b
        a = self.a if j == 0 else 1 - self.a
        return e * 4 + b * 2 + a

    def barrier(self):
        semaphore = pltpu.get_barrier_semaphore()
        partners = [self.to_a, self.to_b, self.to_h, self.to_c]
        partners += [self.further(o) for o in self.offsets[1:]]
        for partner in partners:
            pl.semaphore_signal(
                semaphore, inc=1, device_id=partner, device_id_type=pl.DeviceIdType.MESH
            )
        pl.semaphore_wait(semaphore, len(partners))


class WeightGather:
    def __init__(self, copies, places, shard, full, at):
        self.copies, self.places, self.shard, self.full, self.at = copies, places, shard, full, at
        self.rows = shard.shape[0]
        self.steps = {}

    def piece(self, n, i, j, low=0, count=None):
        place = self.at(n, self.places.share(self.places.offsets[n], i, j))
        return self.full.at[
            pl.ds(place[0] + low, self.rows if count is None else count), place[1]
        ]

    def own(self):
        self.here = self.copies.local(self.shard, self.piece(0, 0, 0), tracked=False)
        self._first(0, self.shard)

    def turn(self):
        for n, offset in enumerate(self.places.offsets):
            if n:
                e, g = offset
                share = self.places.share((0, 0), 0, 0)
                place = self.at(n, share)
                target = self.full.at[pl.ds(place[0], self.rows), place[1]]
                self.steps["t", n] = self.copies.remote(
                    self.shard, target, self.places.further(offset)
                )

    def _first(self, n, source):
        piece = self.piece(n, 0, 0)
        self.steps["a", n] = self.copies.remote(source, piece, self.places.to_a)
        self.steps["b", n] = self.copies.remote(source, piece, self.places.to_b)

    def turned(self):
        for n in range(1, len(self.places.offsets)):
            self.steps["t", n].wait_recv()
            self._first(n, self.piece(n, 0, 0))

    def second(self, far):
        half = self.rows // 2
        for n in range(1, len(self.places.offsets)) if far else (0,):
            self.steps["a", n].wait_recv()
            top = self.piece(n, 0, 1, 0, half)
            self.steps["ab", n] = self.copies.remote(top, top, self.places.to_b)
            self.steps["b", n].wait_recv()
            low = self.piece(n, 1, 0, half, half)
            self.steps["ba", n] = self.copies.remote(low, low, self.places.to_a)

    def finish(self, far):
        if not far:
            self.here.wait()
        for n in range(1, len(self.places.offsets)) if far else (0,):
            self.steps["ab", n].wait_recv()
            self.steps["ba", n].wait_recv()


def in_tiles(rows, size, body):
    lax.fori_loop(0, rows // size, lambda n, _: (body(pl.multiple_of(n * size, size)), 0)[1], 0)


def layer_forward(extra, groups, quarter, *refs):
    (
        rows_ref, in_ref, out_ref, up_ref, down_ref, wide_ref, bias_ref, cots_ref,
        in_all, out_all, up_all, down_all, bias_all, full1, prefix1, proj_out, prefix_out, att_out,
        lse_out, resid_out, full2, full_cot,
        in_here, out_here, norm_here, prefix_here, proj, prefix_proj, att, lse, c_send, c_recv, h_send,
        h_recv, resid, normed2, k_own, v_own, send_sem, recv_sem, near_sem,
    ) = refs
    size, width = rows_ref.shape[1:]
    length = 4 * size
    cols = in_ref.shape[1] // 3
    hidden, depth = up_ref.shape[1], up_ref.shape[0]
    heads = groups * cols // HDIM
    per = cols // HDIM
    scale = HDIM**-0.5 * LOG2E
    places = Places(extra, groups)
    copies = Copies(send_sem, recv_sem, near_sem)
    bias_here = bias_all
    place = 2 * places.h + places.c
    at = row_blocks(place, 4, size)
    chunk = min(64, size)

    def in_at(wide):
        return lambda n, share: (share * depth, pl.ds((n // extra) * wide, wide))

    def column_at(rows):
        def where(n, share):
            return (n // extra) * rows, pl.ds(pl.multiple_of(share * depth, depth), depth)

        return where

    w_in = WeightGather(copies, places, in_ref, in_here, in_at(3 * cols))
    w_out = WeightGather(copies, places, out_ref, out_here, column_at(cols))
    w_up = WeightGather(copies, places, up_ref, up_all, in_at(hidden))
    w_down = WeightGather(copies, places, down_ref, down_all, column_at(hidden))

    def spread_to(source, full, row):
        return Spread(copies, places, source, full, row, size)

    def normalized(values, gain, shift):
        mean = jnp.mean(values, axis=-1, keepdims=True)
        center = values - mean
        inverse = lax.rsqrt(jnp.mean(center * center, axis=-1, keepdims=True) + EPSILON)
        return (center * inverse * wide_ref[gain : gain + 1] + wide_ref[shift : shift + 1]).astype(BF16)

    def first_norm(r):
        def body(at_row):
            values = rows_ref[r, pl.ds(at_row, chunk), :].astype(F32)
            norm_here[pl.ds(r * length + at_row, chunk), :] = normalized(values, 0, 1)

        in_tiles(size, chunk, body)

    def project(source, row, target, row_to, kind):
        wide = (3 - kind) * cols

        def body(n, _):
            g, m = n // 4, lax.rem(n, 4)
            x = source[pl.ds(pl.multiple_of(row + m * size, size), size), :]
            w = in_here[:, pl.ds(pl.multiple_of((g * 3 + kind) * cols, HDIM), wide)]
            bias = bias_here[g, :1, kind * cols : 3 * cols]
            to = pl.ds(pl.multiple_of(g * wide, HDIM), wide)
            target[pl.ds(pl.multiple_of(row_to + m * size, size), size), to] = (dot(x, w) + bias).astype(BF16)
            return 0

        lax.fori_loop(0, 4 * groups, body, 0)

    def attention(r, segment):
        def head(n, _):
            g, i = n // per, lax.rem(n, per)
            base = g * 3 * cols + i * HDIM
            q_at, k_at, v_at = (pl.ds(pl.multiple_of(base + m * cols, HDIM), HDIM) for m in range(3))
            pre = g * 2 * cols + i * HDIM
            kp_at, vp_at = (pl.ds(pl.multiple_of(pre + m * cols, HDIM), HDIM) for m in range(2))
            out_at = pl.ds(pl.multiple_of(n * HDIM, HDIM), HDIM)
            for j in range(4):
                there = pl.ds(r * length + at[j], size)
                k_own[j * size : (j + 1) * size] = proj[there, k_at]
                v_own[j * size : (j + 1) * size] = proj[there, v_at]

            def run(before):
                for j in range(4):
                    there = pl.ds(r * length + at[j], size)
                    q = proj[there, q_at]
                    start, end = first_key(j, size, segment), j * size
                    parts = [
                        (
                            prefix_proj[m * length : (m + 1) * length, kp_at],
                            prefix_proj[m * length : (m + 1) * length, vp_at],
                            None,
                        )
                        for m in range(before)
                    ]
                    if end > start:
                        parts.append((k_own[start:end], v_own[start:end], None))
                    parts.append((k_own[end : end + size], v_own[end : end + size], causal(size)))
                    scores = []
                    for k, _, mask in parts:
                        s = dot(k, q, ((1,), (1,)))
                        scores.append(s if mask is None else jnp.where(mask, s, MASKED))
                    top = functools.reduce(
                        jnp.maximum, [jnp.max(s, axis=0, keepdims=True) for s in scores]
                    )
                    total = jnp.zeros((1, size), F32)
                    out = jnp.zeros((HDIM, size), F32)
                    for s, (_, v, _) in zip(scores, parts):
                        p = jnp.exp2((s - top) * scale)
                        total = total + jnp.sum(p, axis=0, keepdims=True)
                        out = out + dot(v, p.astype(BF16), ((0,), (0,)))
                    att[there, out_at] = (out / total).T.astype(BF16)
                    lse[r * heads + n, :, j * size : (j + 1) * size] = top * scale + jnp.log(total) * LOG2E

            if segment is not None:
                run(0)
            else:
                for m in range(groups):
                    pl.when(places.g == m)(functools.partial(run, m))
            return 0

        lax.fori_loop(0, heads, head, 0)

    to_core, to_far = [None, None], [None, None]

    def out_product(r):
        def away(t):
            c_send[r, pl.ds(t, size), :] = dot(
                att[pl.ds(r * length + 2 * size + t, size), :], out_here[...]
            ).astype(BF16)

        in_tiles(2 * size, size, away)
        to_core[r] = copies.remote(c_send.at[r], c_recv.at[r], places.to_c)

    def out_sum(r):
        to_core[r].wait_recv()

        def far(t):
            h_send[r, pl.ds(t, size), :] = (
                dot(att[pl.ds(r * length + size + t, size), :], out_here[...])
                + c_recv[r, pl.ds(size + t, size), :].astype(F32)
            ).astype(BF16)

        in_tiles(size, size, far)
        to_far[r] = copies.remote(h_send.at[r], h_recv.at[r], places.to_h)

        def own(t):
            resid[r, pl.ds(t, size), :] = (
                dot(att[pl.ds(r * length + t, size), :], out_here[...])
                + c_recv[r, pl.ds(t, size), :].astype(F32)
                + rows_ref[r, pl.ds(t, size), :].astype(F32)
                + wide_ref[2:3]
            )

        in_tiles(size, size, own)

    def second_norm(r):
        to_far[r].wait_recv()

        def body(t):
            values = resid[r, pl.ds(t, chunk), :] + h_recv[r, pl.ds(t, chunk), :].astype(F32)
            resid[r, pl.ds(t, chunk), :] = values
            normed2[r, pl.ds(t, chunk), :] = normalized(values, 3, 4)

        in_tiles(size, chunk, body)
        copies.local(resid.at[r], resid_out.at[r])
        copies.local(normed2.at[r], full2.at[pl.ds(r * length, size), :])
        return spread_to(normed2.at[r], full2, r * length)

    def clear(t):
        prefix_here[pl.ds(t, size), :] = jnp.zeros((size, width), BF16)

    places.barrier()
    w_in.own()
    w_in.turn()
    bias_steps = [
        copies.remote(bias_ref, bias_here.at[n // extra], places.further(o))
        for n, o in enumerate(places.offsets)
        if n and o[0] == 0
    ]
    bias_here[0] = bias_ref[...]
    first_norm(0)
    spread = [spread_to(norm_here.at[pl.ds(0, size), :], norm_here, 0), None]
    before = []
    for k in range(1, groups):
        copy = copies.remote(
            norm_here.at[pl.ds(0, size), :],
            prefix_here.at[pl.ds((k - 1) * length, size), :],
            places.further((0, k)),
            tracked=False,
        )
        pl.when(places.g + k < groups)(copy.start)
        before.append(copy)
    first_norm(1)
    spread[1] = spread_to(norm_here.at[pl.ds(length, size), :], norm_here, length)
    w_in.second(False)
    w_out.own()
    w_out.turn()
    spread[0].forward()
    w_in.turned()
    w_out.second(False)
    spread[1].forward()
    w_in.second(True)
    w_up.own()
    w_up.turn()
    spread_cot = []
    for r in range(2):
        copies.local(cots_ref.at[r], full_cot.at[pl.ds(r * length, size), :])
        spread_cot.append(spread_to(cots_ref.at[r], full_cot, r * length))

    later = []
    for k in range(1, groups):
        row = (k - 1) * length
        slot = [prefix_here.at[pl.ds(row + n * size, size), :] for n in range(4)]
        far = copies.remote(slot[0], slot[1], places.to_h, tracked=False)
        core = copies.remote(slot[0], slot[2], places.to_c, tracked=False)
        last = copies.remote(slot[1], slot[3], places.to_c, tracked=False)
        later.append((far, core, last))

        @pl.when(places.g >= k)
        def _():
            before[k - 1].wait_recv()
            far.start()
            core.start()

        @pl.when(places.g < k)
        def _():
            in_tiles(length, size, lambda t: clear(row + t))

    w_in.finish(False)
    w_in.finish(True)
    copies.local(in_here, in_all)
    for copy in bias_steps:
        copy.wait_recv()
    spread[1].finish()
    project(norm_here, length, proj, length, 0)
    w_out.turned()
    attention(1, quarter)
    w_out.second(True)
    w_up.second(False)
    for k in range(1, groups):
        far, core, last = later[k - 1]

        @pl.when(places.g >= k)
        def _():
            far.wait_recv()
            last.start()

    spread[0].finish()
    copies.local(norm_here, full1)
    project(norm_here, 0, proj, 0, 0)
    w_out.finish(False)
    w_out.finish(True)
    copies.local(out_here, out_all)
    out_product(1)
    w_down.own()
    for k in range(1, groups):
        far, core, last = later[k - 1]

        @pl.when(places.g >= k)
        def _():
            core.wait_recv()
            last.wait_recv()

    for k in range(1, groups):
        project(prefix_here, (k - 1) * length, prefix_proj, (k - 1) * length, 1)
    copies.local(prefix_here, prefix1)
    copies.local(prefix_proj, prefix_out)
    copies.local(proj, proj_out)
    out_sum(1)
    w_up.turned()
    w_down.turn()
    spread_cot[0].forward()
    spread_cot[1].forward()
    attention(0, None)
    copies.local(att, att_out)
    copies.local(lse, lse_out)
    out_product(0)
    w_down.second(False)
    spread2 = [None, second_norm(1)]
    out_sum(0)
    w_up.second(True)
    spread2[0] = second_norm(0)
    spread2[1].forward()
    w_down.turned()
    spread2[0].forward()
    w_up.finish(False)
    w_up.finish(True)
    w_down.second(True)
    w_down.finish(False)
    spread2[1].finish()
    spread2[0].finish()
    spread_cot[0].finish()
    spread_cot[1].finish()
    w_down.finish(True)

    for k in range(1, groups):
        far, core, last = later[k - 1]
        pl.when(places.g + k < groups)(before[k - 1].wait_send)

        @pl.when(places.g >= k)
        def _():
            far.wait_send()
            core.wait_send()
            last.wait_send()

    copies.finish()


def run_forward(split, quarter, rows, in_w, out_w, up_w, down_w, wide, bias, cots):
    extra, groups = split
    size, width = rows.shape[1:]
    length = 4 * size
    cols, hidden = in_w.shape[1] // 3, up_w.shape[1]
    all_cols = groups * cols
    heads = all_cols // HDIM
    shape = jax.ShapeDtypeStruct
    anywhere = pl.BlockSpec(memory_space=pl.ANY)
    inside = pl.BlockSpec(memory_space=pltpu.VMEM)
    count = extra * groups * 20 + 4 * groups + 24
    out_shape = [
        shape((width, 3 * all_cols), BF16),
        shape((all_cols, width), BF16),
        shape((width, groups * hidden), BF16),
        shape((groups * hidden, width), BF16),
        shape((groups,) + bias.shape, F32),
        shape((2 * length, width), BF16),
        shape(((groups - 1) * length, width), BF16),
        shape((2 * length, 3 * all_cols), BF16),
        shape(((groups - 1) * length, 2 * all_cols), BF16),
        shape((2 * length, all_cols), BF16),
        shape((2 * heads, 1, length), F32),
        shape((2, size, width), F32),
        shape((2 * length, width), BF16),
        shape((2 * length, width), BF16),
    ]
    return pl.pallas_call(
        functools.partial(layer_forward, extra, groups, quarter),
        in_specs=[inside] + [anywhere] * 4 + [inside] * 2 + [anywhere],
        out_specs=[inside if n == 4 else anywhere for n in range(len(out_shape))],
        out_shape=out_shape,
        scratch_shapes=[
            pltpu.VMEM((width, 3 * all_cols), BF16),
            pltpu.VMEM((all_cols, width), BF16),
            pltpu.VMEM((2 * length, width), BF16),
            pltpu.VMEM(((groups - 1) * length, width), BF16),
            pltpu.VMEM((2 * length, 3 * all_cols), BF16),
            pltpu.VMEM(((groups - 1) * length, 2 * all_cols), BF16),
            pltpu.VMEM((2 * length, all_cols), BF16),
            pltpu.VMEM((2 * heads, 1, length), F32),
            pltpu.VMEM((2, 2 * size, width), BF16),
            pltpu.VMEM((2, 2 * size, width), BF16),
            pltpu.VMEM((2, size, width), BF16),
            pltpu.VMEM((2, size, width), BF16),
            pltpu.VMEM((2, size, width), F32),
            pltpu.VMEM((2, size, width), BF16),
            pltpu.VMEM((length, HDIM), BF16),
            pltpu.VMEM((length, HDIM), BF16),
            pltpu.SemaphoreType.DMA((count,)),
            pltpu.SemaphoreType.DMA((count,)),
            pltpu.SemaphoreType.DMA((24,)),
        ],
        compiler_params=kernel_params(0),
        cost_estimate=pl.CostEstimate(flops=10**11, bytes_accessed=10**8, transcendentals=10**7),
    )(rows, in_w, out_w, up_w, down_w, wide, bias, cots)


class GradScatter:
    def __init__(self, copies, places, parts, land, turned, work, own, fetched, out):
        self.copies, self.places, self.parts = copies, places, parts
        self.land, self.turned, self.work, self.own = land, turned, work, own
        self.fetched, self.out = fetched, out
        self.half, self.cols = land.shape[2:]
        self.steps = {}

    def piece(self, n, i, j, part):
        places = self.places
        offset = places.offsets[n]
        index = offset[1] * places.extra * 4 + places.share(offset, i, j)
        return self.parts.at[index, pl.ds(part * self.half, self.half), :]

    def _send(self, n, key, source, partner):
        self.steps[n, key] = self.copies.remote(source, self.land.at[n, key], partner)

    def start(self, n):
        to_a, to_b = self.places.to_a, self.places.to_b
        self._send(n, 0, self.piece(n, 1, 1, 0), to_a)
        self._send(n, 1, self.piece(n, 1, 1, 1), to_b)
        self._send(n, 2, self.piece(n, 0, 1, 0), to_a)
        self._send(n, 3, self.piece(n, 1, 0, 1), to_b)

    def _fetch(self, sources):
        got = [self.fetched.at[m, : self.half, : self.cols] for m in range(len(sources))]
        loads = [self.copies.local(s, t, tracked=False) for s, t in zip(sources, got)]
        for load in loads:
            load.wait()
        return functools.reduce(jnp.add, [t[...].astype(F32) for t in got])

    def middle(self, n):
        self.steps[n, 0].wait_recv()
        self.work[n, 0] = self._fetch([self.land.at[n, 0], self.piece(n, 1, 0, 0)]).astype(BF16)
        self._send(n, 5, self.work.at[n, 0], self.places.to_b)
        self.steps[n, 1].wait_recv()
        self.work[n, 1] = self._fetch([self.land.at[n, 1], self.piece(n, 0, 1, 1)]).astype(BF16)
        self._send(n, 4, self.work.at[n, 1], self.places.to_a)

    def last(self, n):
        for part, keys in ((0, (2, 5)), (1, (3, 4))):
            for key in keys:
                self.steps[n, key].wait_recv()
            summed = self._fetch([self.piece(n, 0, 0, part)] + [self.land.at[n, k] for k in keys])
            rows = slice(part * self.half, (part + 1) * self.half)
            if n == 0:
                self.out[rows, :] = summed
            else:
                self.own[n - 1, rows, :] = summed.astype(BF16)
        if n:
            e, g = self.places.offsets[n]
            self.steps[n, "t"] = self.copies.remote(
                self.own.at[n - 1], self.turned.at[n - 1], self.places.further((-e, -g))
            )

    def total(self):
        for n in range(1, len(self.places.offsets)):
            self.steps[n, "t"].wait_recv()
            for part in range(2):
                rows = slice(part * self.half, (part + 1) * self.half)
                self.out[rows, :] += self._fetch(
                    [self.turned.at[n - 1, pl.ds(part * self.half, self.half), :]]
                )

    @staticmethod
    def landing(sources, rows, cols):
        return [
            jax.ShapeDtypeStruct((sources, 6, rows // 2, cols), BF16),
            jax.ShapeDtypeStruct((max(sources - 1, 1), rows, cols), BF16),
        ]

    @staticmethod
    def working(sources, rows, cols):
        return [
            pltpu.VMEM((sources, 2, rows // 2, cols), BF16),
            pltpu.VMEM((max(sources - 1, 1), rows, cols), BF16),
        ]


class Fold:
    def __init__(self, copies, places, c_send, c_recv, h_send, free, size):
        self.copies, self.places, self.size = copies, places, size
        self.c_send, self.c_recv, self.h_send, self.free = c_send, c_recv, h_send, free
        self.core = self.far = None

    def away(self, block):
        if self.core is not None:
            self.copies.sent(self.core)
        for t in range(2):
            self.c_send[t * self.size : (t + 1) * self.size, :] = block(2 + t).astype(BF16)
        if self.core is not None:
            pl.semaphore_wait(self.free, 1)
        self.core = self.copies.remote(self.c_send, self.c_recv, self.places.to_c)

    def kept(self, block, target, h_recv, more):
        size = self.size
        far = block(1)
        self.core.wait_recv()
        if self.far is not None:
            self.copies.sent(self.far)
        self.h_send[...] = (far + self.c_recv[size:, :].astype(F32)).astype(BF16)
        self.far = self.copies.remote(self.h_send, h_recv, self.places.to_h)
        target[...] = (block(0) + self.c_recv[:size, :].astype(F32)).astype(target.dtype)
        if more:
            pl.semaphore_signal(
                self.free, inc=1, device_id=self.places.to_c, device_id_type=pl.DeviceIdType.MESH
            )
        return self.far


class Stream:
    def __init__(self, copies, slots, blocks):
        self.copies, self.slots, self.blocks = copies, slots, blocks
        self.loads = {}
        self._load(0)

    def _load(self, n):
        if n < len(self.blocks):
            targets = [s[n % 2] for s in self.slots]
            self.loads[n] = [
                self.copies.local(s, t, tracked=False) for s, t in zip(self.blocks[n], targets)
            ]

    def take(self, n):
        for load in self.loads[n]:
            load.wait()
        self._load(n + 1)
        return n % 2


class Spread:
    def __init__(self, copies, places, source, full, row, size):
        self.copies, self.places, self.full, self.row, self.size = copies, places, full, row, size
        self.far = copies.remote(source, self.slot(1), places.to_h)
        self.core = copies.remote(source, self.slot(2), places.to_c)

    def slot(self, n):
        return self.full.at[pl.ds(self.row + n * self.size, self.size), :]

    def forward(self):
        self.far.wait_recv()
        self.last = self.copies.remote(self.slot(1), self.slot(3), self.places.to_c)

    def finish(self):
        self.core.wait_recv()
        self.last.wait_recv()


def middle_kernel(extra, groups, *refs):
    (
        dup, act, full2, full_cot, up_all, cots, resid, wide,
        dres, full_dres, grad_down, up_parts, sums, down_parts, land, turned,
        big, narrow, tiles, c_send, c_recv, h_send, h_recv, low, stage_down, stage_up, work, own,
        fetched, send_sem, recv_sem, near_sem, free,
    ) = refs
    size, width = cots.shape[1:]
    length = 4 * size
    hidden, depth = grad_down.shape
    shares = extra * 4
    chunk = min(64, size)
    places = Places(extra, groups)
    copies = Copies(send_sem, recv_sem, near_sem)
    sources = len(places.offsets)
    down = GradScatter(
        copies, places, down_parts, land, turned, work, own, fetched, grad_down
    )
    fold = Fold(copies, places, c_send, c_recv, h_send, free, size)
    folded = []

    def load_big(source):
        return copies.local(source, big.at[: source.shape[0]], tracked=False)

    loading = load_big(up_all)
    order = [(r, slot) for r in range(2) for slot in (2, 3, 1, 0)]
    tile_slots = [tiles.at[0], tiles.at[1]]
    narrow_slots = [narrow.at[0], narrow.at[1]]
    stream = Stream(
        copies, [tile_slots], [[dup.at[pl.ds(r * length + s * size, size), :]] for r, s in order]
    )
    places.barrier()
    sums[...] = jnp.zeros_like(sums)
    loading.wait()

    def block_of(r):
        def block(slot):
            at = stream.take(order.index((r, slot)))
            return dot(tiles[at], big[:width], ((1,), (1,)))

        return block

    for r in range(2):
        fold.away(block_of(r))
        folded.append(fold.kept(block_of(r), dres.at[r], h_recv.at[r], r == 0))

    def norm_back_rows(r):
        folded[r].wait_recv()

        def body(t):
            rows = pl.ds(t, chunk)
            grad = dres[r, rows, :] + h_recv[r, rows, :].astype(F32)
            scaled, inverse = stats(resid[r, rows, :])
            cot = cots[r, rows, :].astype(F32)
            value = cot + norm_back(grad, scaled, inverse, wide[3:4])
            dres[r, rows, :] = value
            low[r, rows, :] = value.astype(BF16)
            for n, term in enumerate((value, grad * scaled, grad, cot)):
                sums[n : n + 1, :] += jnp.sum(term, axis=0, keepdims=True)

        in_tiles(size, chunk, body)
        copies.local(low.at[r], full_dres.at[pl.ds(r * length, size), :])
        return Spread(copies, places, low.at[r], full_dres, r * length, size)

    def columns(source):
        return [
            [source.at[:, pl.ds(d * depth, depth)]] for g in range(groups) for d in range(shares)
        ]

    turn_order = list(range(groups))[::-1]
    loading = load_big(act)
    stream_cot = Stream(copies, [narrow_slots], columns(full_cot))
    loading.wait()
    put = {}
    count = 0
    spread = [None, None]

    def down_grad(g):
        nonlocal count
        for d in range(shares):
            at = stream_cot.take(count)
            slot = count % 2
            if count - 2 in put:
                put.pop(count - 2).wait()

            def body(t):
                left = big[: 2 * length, pl.ds(pl.multiple_of(g * hidden + t, HDIM), hidden // 2)]
                stage_down[slot, pl.ds(t, hidden // 2), :] = dot(
                    left, narrow[at], ((0,), (0,))
                ).astype(BF16)

            in_tiles(hidden, hidden // 2, body)
            put[count] = copies.local(
                stage_down.at[slot], down_parts.at[g * shares + d], tracked=False
            )
            count += 1

    def of_group(g):
        return [n for n in range(sources) if places.offsets[n][1] == g][::-1]

    def flush():
        for n in range(max(count - 2, 0), count):
            if n in put:
                put.pop(n).wait()

    for step, g in enumerate(turn_order):
        down_grad(g)
        flush()
        for n in of_group(g):
            down.start(n)
        if step == 0:
            spread[0] = norm_back_rows(0)
    spread[1] = norm_back_rows(1)
    loading = load_big(dup)
    stream_two = Stream(copies, [narrow_slots], columns(full2))
    for n in of_group(turn_order[0]):
        down.middle(n)
    spread[0].forward()
    loading.wait()
    put_up = {}
    done = 0
    for step, g in enumerate(turn_order):
        for d in range(shares):
            at = stream_two.take(done)
            slot = done % 2
            if done >= 2:
                put_up.pop(done - 2).wait()
            stage_up[slot] = dot(
                narrow[at], big[: 2 * length, g * hidden : (g + 1) * hidden], ((0,), (0,))
            ).astype(BF16)
            put_up[done] = copies.local(
                stage_up.at[slot], up_parts.at[g * shares + d], tracked=False
            )
            done += 1
        if step == 0:
            for n in of_group(turn_order[0]):
                if n:
                    down.last(n)
            spread[1].forward()
            for g_next in turn_order[1:]:
                for n in of_group(g_next):
                    down.middle(n)
    for copy in put_up.values():
        copy.wait()
    spread[0].finish()
    spread[1].finish()
    for g in turn_order:
        for n in of_group(g):
            if (n, "t") not in down.steps:
                down.last(n)
    down.total()
    copies.finish()


def attention_back_rows(places, row, length, size, heads, per, segment, refs, column):
    (
        proj, prefix_proj, att, datt, lse, dproj, dprefix,
        k_own, v_own, dk_own, dv_own, dk_pre, dv_pre,
    ) = refs
    scale = HDIM**-0.5 * LOG2E
    factor = HDIM**-0.5
    at = row_blocks(2 * places.h + places.c, 4, size)
    base = row * length

    def head(n, _):
        q_at, k_at, v_at = (pl.ds(column(n, 3, m), HDIM) for m in range(3))
        kp_at, vp_at = (pl.ds(column(n, 2, m), HDIM) for m in range(2))
        out_at = pl.ds(pl.multiple_of(n * HDIM, HDIM), HDIM)
        for j in range(4):
            there = pl.ds(base + at[j], size)
            k_own[j * size : (j + 1) * size] = proj[there, k_at]
            v_own[j * size : (j + 1) * size] = proj[there, v_at]
        dk_own[...] = jnp.zeros_like(dk_own)
        dv_own[...] = jnp.zeros_like(dv_own)
        if segment is None:
            dk_pre[...] = jnp.zeros_like(dk_pre)
            dv_pre[...] = jnp.zeros_like(dv_pre)

        def run(before):
            for j in range(4):
                there = pl.ds(base + at[j], size)
                q = proj[there, q_at]
                do = datt[there, out_at]
                product = do.astype(F32) * att[there, out_at].astype(F32)
                delta = lax.dot_general(
                    jnp.ones((8, HDIM), F32),
                    product,
                    (((1,), (1,)), ((), ())),
                    precision=lax.Precision.HIGHEST,
                    preferred_element_type=F32,
                )[:1]
                log_total = lse[row * heads + n, :, j * size : (j + 1) * size]
                start, end = first_key(j, size, segment), j * size
                parts = []
                step = min(512, length)
                for m in range(0, before * length, step):
                    rows = slice(m, m + step)
                    parts.append(
                        (prefix_proj[rows, kp_at], prefix_proj[rows, vp_at], dk_pre, dv_pre, rows, None)
                    )
                if end > start:
                    rows = slice(start, end)
                    parts.append((k_own[rows], v_own[rows], dk_own, dv_own, rows, None))
                rows = slice(end, end + size)
                parts.append((k_own[rows], v_own[rows], dk_own, dv_own, rows, causal(size)))
                dq = jnp.zeros((HDIM, size), F32)
                for k, v, dk, dv, rows, mask in parts:
                    s = dot(k, q, ((1,), (1,))) * scale - log_total
                    p = jnp.exp2(s if mask is None else jnp.where(mask, s, MASKED))
                    dscores = (p * (dot(v, do, ((1,), (1,))) - delta)).astype(BF16)
                    dv[rows] += dot(p.astype(BF16), do)
                    dk[rows] += dot(dscores, q)
                    dq = dq + dot(k, dscores, ((0,), (0,)))
                dproj[there, q_at] = (dq * factor).T.astype(BF16)

        if segment is not None:
            run(0)
        else:
            for m in range(places.groups):
                pl.when(places.g == m)(functools.partial(run, m))
            dprefix[:, q_at] = jnp.zeros_like(dk_pre, dtype=BF16)
            dprefix[:, k_at] = (dk_pre[...] * factor).astype(BF16)
            dprefix[:, v_at] = dv_pre[...].astype(BF16)
        for j in range(4):
            rows = slice(j * size, (j + 1) * size)
            there = pl.ds(base + at[j], size)
            dproj[there, k_at] = (dk_own[rows] * factor).astype(BF16)
            dproj[there, v_at] = dv_own[rows].astype(BF16)
        return 0

    lax.fori_loop(0, heads, head, 0)


def last_kernel(extra, groups, quarter, *refs):
    (
        proj_in, prefix_in, att_in, full_dres, out_all, in_all, full1, prefix1, up_parts, lse,
        grad_in, grad_out, grad_up, dnormed1, h_recv, returned, dproj_sums,
        in_parts, out_parts, land_in, turned_in, land_out, turned_out, land_up, turned_up,
        proj, prefix_proj, att, datt, dprefix, w_in, w_out, spare,
        k_own, v_own, dk_own, dv_own, dk_pre, dv_pre,
        c_send, c_recv, h_send, back, stage_in, stage_out,
        work_in, own_in, work_out, own_out, work_up, own_up, fetched, send_sem, recv_sem, near_sem, free,
    ) = refs
    size, width = dnormed1.shape[1:]
    length = 4 * size
    cols = grad_in.shape[1] // 3
    depth = grad_in.shape[0]
    wide = 3 * cols
    heads = groups * cols // HDIM
    per = cols // HDIM
    shares = extra * 4
    places = Places(extra, groups)
    copies = Copies(send_sem, recv_sem, near_sem)
    sources = len(places.offsets)
    far_first = list(range(sources))[::-1]
    up = GradScatter(
        copies, places, up_parts, land_up, turned_up, work_up, own_up, fetched, grad_up
    )
    out = GradScatter(
        copies, places, out_parts, land_out, turned_out, work_out, own_out, fetched, grad_out
    )
    into = GradScatter(
        copies, places, in_parts, land_in, turned_in, work_in, own_in, fetched, grad_in
    )
    dproj = proj
    folds = Fold(copies, places, c_send, c_recv, h_send, free, size)
    folded = {}

    def column(n, parts, m):
        return pl.multiple_of((n // per * parts + m) * cols + lax.rem(n, per) * HDIM, HDIM)

    here = [
        copies.local(s, t, tracked=False)
        for s, t in (
            (out_all, w_out), (proj_in, proj), (prefix_in, prefix_proj), (att_in, att), (in_all, w_in),
        )
    ]
    order = [(r, slot) for r in range(2) for slot in range(4)]
    tiles = [c_send.at[pl.ds(n * size, size), :] for n in range(2)]
    stream = Stream(
        copies, [tiles], [[full_dres.at[pl.ds(r * length + s * size, size), :]] for r, s in order]
    )
    places.barrier()
    for n in far_first:
        up.start(n)
    for copy in here:
        copy.wait()

    def attended_grad(r):
        for slot in range(4):
            at = stream.take(r * 4 + slot)
            datt[r * length + slot * size : r * length + (slot + 1) * size, :] = dot(
                tiles[at][...], w_out[...], ((1,), (1,))
            ).astype(BF16)

    def attention_back(r, segment):
        attention_back_rows(
            places, r, length, size, heads, per, segment,
            (
                proj, prefix_proj, att, datt, lse, dproj, dprefix,
                k_own, v_own, dk_own, dv_own, dk_pre, dv_pre,
            ),
            column,
        )

    def block_of(source, row):
        def block(slot):
            rows = source[row + slot * size : row + (slot + 1) * size, :]
            return dot(rows, w_in[...], ((1,), (1,)))

        return block

    def fold(number, source, row, target, more=True):
        folds.away(block_of(source, row))
        folded[number] = folds.kept(block_of(source, row), target, h_recv.at[number], more)

    attended_grad(0)
    attended_grad(1)
    attention_back(0, None)
    for n in far_first:
        up.middle(n)
    for k in range(1, groups):
        fold(1 + k, dprefix, (k - 1) * length, back.at[k - 1])
    attention_back(1, quarter)
    for n in far_first:
        up.last(n)

    home = []
    for k in range(1, groups):
        folded[1 + k].wait_recv()
        back[k - 1] = (back[k - 1].astype(F32) + h_recv[1 + k].astype(F32)).astype(BF16)
        copy = copies.remote(
            back.at[k - 1], returned.at[k - 1], places.further((0, -k)), tracked=False
        )
        pl.when(places.g >= k)(copy.start)
        home.append(copy)

    slots = [datt.at[:, pl.ds(0, depth)], spare]
    prefix_rows = prefix1.shape[0]
    slots_pre = [prefix_proj.at[:, pl.ds(n * depth, depth)] for n in range(2)]

    class Columns:
        def __init__(self, sources_and_slots, count):
            self.pairs, self.count, self.loads = sources_and_slots, count, {}
            self._load(0)

        def _load(self, n):
            if n < self.count:
                d = n % shares
                self.loads[n] = [
                    copies.local(s.at[:, pl.ds(d * depth, depth)], slot[n % 2], tracked=False)
                    for s, slot in self.pairs
                ]

        def take(self, n):
            for load in self.loads[n]:
                load.wait()
            self._load(n + 1)
            return n % 2

    put = []

    def store(stage, target):
        put.append(copies.local(stage, target, tracked=False))

    def drain(left):
        while len(put) > left:
            put.pop(0).wait()

    stream_in = Columns([(full1, slots), (prefix1, slots_pre)], groups * shares)
    count = 0
    for g in range(groups)[::-1]:
        for d in range(shares):
            at = stream_in.take(count)
            drain(1)
            which = pl.ds(g * wide, wide)
            value = dot(slots[at][...], dproj[:, which], ((0,), (0,)))
            if prefix_rows:
                value = value + dot(slots_pre[at][...], dprefix[:, which], ((0,), (0,)))
            stage_in[count % 2] = value.astype(BF16)
            store(stage_in.at[count % 2], in_parts.at[g * shares + d])
            count += 1
        drain(0)
        for n in far_first:
            if places.offsets[n][1] == g:
                into.start(n)
    stream_out = Columns([(full_dres, slots)], shares)
    for d in range(shares):
        at = stream_out.take(d)
        for g in range(groups):
            drain(1)
            slot = (d * groups + g) % 2
            stage_out[slot] = dot(
                att[:, g * cols : (g + 1) * cols], slots[at][...], ((0,), (0,))
            ).astype(BF16)
            store(stage_out.at[slot], out_parts.at[g * shares + d])
    drain(0)
    for n in far_first:
        out.start(n)
    fold(0, dproj, 0, dnormed1.at[0])
    for n in far_first:
        if places.offsets[n][1] == groups - 1:
            into.middle(n)
    fold(1, dproj, length, dnormed1.at[1], False)
    for n in far_first:
        if places.offsets[n][1] != groups - 1:
            into.middle(n)
    for n in far_first:
        if n and places.offsets[n][1] == groups - 1:
            into.last(n)
    for n in far_first:
        out.middle(n)
    dproj_sums[...] = jnp.zeros_like(dproj_sums)

    def add_rows(t):
        dproj_sums[0:1, :] += jnp.sum(dproj[pl.ds(t, size), :].astype(F32), axis=0, keepdims=True)

    in_tiles(2 * length, size, add_rows)

    def add_prefix(t):
        dproj_sums[1:2, :] += jnp.sum(dprefix[pl.ds(t, size), :].astype(F32), axis=0, keepdims=True)

    in_tiles(prefix_rows, size, add_prefix)
    up.total()
    for n in far_first:
        if (n, "t") not in into.steps:
            into.last(n)
    for n in far_first:
        out.last(n)
    for r in range(2):
        folded[r].wait_recv()
    out.total()
    into.total()
    for k in range(1, groups):
        pl.when(places.g + k < groups)(home[k - 1].wait_recv)
        pl.when(places.g >= k)(home[k - 1].wait_send)
    copies.finish()


def kernel_params(number):
    return pltpu.CompilerParams(
        collective_id=number, has_side_effects=True, vmem_limit_bytes=KERNEL_VMEM
    )


def run_middle(split, dup, act, full2, full_cot, up_all, cots, resid, wide, hidden, depth):
    extra, groups = split
    sources = extra * groups
    size, width = cots.shape[1:]
    length = 4 * size
    shape = jax.ShapeDtypeStruct
    anywhere = pl.BlockSpec(memory_space=pl.ANY)
    inside = pl.BlockSpec(memory_space=pltpu.VMEM)
    shares = sources * 4
    return pl.pallas_call(
        functools.partial(middle_kernel, extra, groups),
        in_specs=[anywhere] * 5 + [inside] * 3,
        out_specs=[inside, anywhere, inside, anywhere, inside] + [anywhere] * 3,
        out_shape=[
            shape((2, size, width), F32),
            shape((2 * length, width), BF16),
            shape((hidden, depth), F32),
            shape((shares, depth, hidden), BF16),
            shape((4, width), F32),
            shape((shares, hidden, depth), BF16),
        ]
        + GradScatter.landing(sources, hidden, depth),
        scratch_shapes=[
            pltpu.VMEM((max(width, 2 * length), groups * hidden), BF16),
            pltpu.VMEM((2, 2 * length, depth), BF16),
            pltpu.VMEM((2, size, groups * hidden), BF16),
            pltpu.VMEM((2 * size, width), BF16),
            pltpu.VMEM((2 * size, width), BF16),
            pltpu.VMEM((size, width), BF16),
            pltpu.VMEM((2, size, width), BF16),
            pltpu.VMEM((2, size, width), BF16),
            pltpu.VMEM((2, hidden, depth), BF16),
            pltpu.VMEM((2, depth, hidden), BF16),
        ]
        + GradScatter.working(sources, hidden, depth)
        + [
            pltpu.VMEM((3, hidden // 2, depth), BF16),
            pltpu.SemaphoreType.DMA((sources * 8 + 16,)),
            pltpu.SemaphoreType.DMA((sources * 8 + 16,)),
            pltpu.SemaphoreType.DMA((sources * 16 + 6 * shares + 24,)),
            pltpu.SemaphoreType.REGULAR,
        ],
        compiler_params=kernel_params(1),
        cost_estimate=pl.CostEstimate(flops=10**11, bytes_accessed=10**8, transcendentals=10**6),
    )(dup, act, full2, full_cot, up_all, cots, resid, wide)


def run_last(split, quarter, proj, prefix_proj, att, full_dres, out_all, in_all, full1, prefix1, up_parts, lse):
    extra, groups = split
    sources = extra * groups
    shares = sources * 4
    length, width = full1.shape[0] // 2, full1.shape[1]
    size = length // 4
    cols = att.shape[1] // groups
    depth, hidden = up_parts.shape[1:]
    wide, all_wide = 3 * cols, 3 * cols * groups
    prefix_rows = prefix1.shape[0]
    shape = jax.ShapeDtypeStruct
    anywhere = pl.BlockSpec(memory_space=pl.ANY)
    inside = pl.BlockSpec(memory_space=pltpu.VMEM)
    heads_rows = [pltpu.VMEM((length, HDIM), BF16)] * 2 + [pltpu.VMEM((length, HDIM), F32)] * 2
    return pl.pallas_call(
        functools.partial(last_kernel, extra, groups, quarter),
        in_specs=[anywhere] * 9 + [inside],
        out_specs=[inside] * 7 + [anywhere] * 8,
        out_shape=[
            shape((depth, wide), F32),
            shape((cols, depth), F32),
            shape((depth, hidden), F32),
            shape((2, size, width), BF16),
            shape((1 + groups, size, width), BF16),
            shape((max(groups - 1, 1), size, width), BF16),
            shape((2, all_wide), F32),
            shape((shares, depth, wide), BF16),
            shape((shares, cols, depth), BF16),
        ]
        + GradScatter.landing(sources, depth, wide)
        + GradScatter.landing(sources, cols, depth)
        + GradScatter.landing(sources, depth, hidden),
        scratch_shapes=[
            pltpu.VMEM(proj.shape, BF16),
            pltpu.VMEM(prefix_proj.shape, BF16),
            pltpu.VMEM(att.shape, BF16),
            pltpu.VMEM(att.shape, BF16),
            pltpu.VMEM((prefix_rows, all_wide), BF16),
            pltpu.VMEM(in_all.shape, BF16),
            pltpu.VMEM(out_all.shape, BF16),
            pltpu.VMEM((2 * length, depth), BF16),
        ]
        + heads_rows
        + [pltpu.VMEM((prefix_rows, HDIM), F32)] * 2
        + [
            pltpu.VMEM((2 * size, width), BF16),
            pltpu.VMEM((2 * size, width), BF16),
            pltpu.VMEM((size, width), BF16),
            pltpu.VMEM((max(groups - 1, 1), size, width), BF16),
            pltpu.VMEM((2, depth, wide), BF16),
            pltpu.VMEM((2, cols, depth), BF16),
        ]
        + GradScatter.working(sources, depth, wide)
        + GradScatter.working(sources, cols, depth)
        + GradScatter.working(sources, depth, hidden)
        + [
            pltpu.VMEM((3, depth // 2, max(wide, hidden, depth)), BF16),
            pltpu.SemaphoreType.DMA((sources * 24 + 4 * groups + 16,)),
            pltpu.SemaphoreType.DMA((sources * 24 + 4 * groups + 16,)),
            pltpu.SemaphoreType.DMA((sources * 48 + 10 * shares + 32,)),
            pltpu.SemaphoreType.REGULAR,
        ],
        compiler_params=kernel_params(2),
        cost_estimate=pl.CostEstimate(flops=10**11, bytes_accessed=10**8, transcendentals=10**7),
    )(proj, prefix_proj, att, full_dres, out_all, in_all, full1, prefix1, up_parts, lse)


def local(
    tokens,
    segments,
    first_gain,
    first_shift,
    in_weight,
    in_bias,
    out_weight,
    out_bias,
    second_gain,
    second_shift,
    up_weight,
    up_bias,
    down_weight,
    down_bias,
    cotangent,
):
    extra, groups = lax.axis_size("e"), lax.axis_size("g")
    split = (extra, groups)
    size, width = tokens.shape[1:]
    cols, hidden, depth = in_weight.shape[2], up_weight.shape[1], in_weight.shape[0]
    quarter = segments.shape[1] // 4

    single = jnp.where(segments[0, -1] == 0, 0, 1)
    order = (single, 1 - single)

    def pick(x):
        return [lax.dynamic_index_in_dim(x, r, 0, keepdims=False) for r in order]

    def unpick(first, second):
        return jnp.where(single == 0, jnp.stack([first, second]), jnp.stack([second, first]))

    rows = [r.astype(F32) for r in pick(tokens)]
    cots = pick(cotangent)

    no_bias = jnp.zeros_like(in_bias[0])
    biases = jnp.concatenate([in_bias[0], no_bias, in_bias[1], up_bias])
    biases = jnp.broadcast_to(biases, (8, biases.shape[0]))
    wide = jnp.stack([first_gain, first_shift, out_bias, second_gain, second_shift])
    (
        in_all, out_all, up_all, down_all, biases, full1, prefix1, proj, proj_prefix, attended, lse,
        resid, full2, full_cot,
    ) = run_forward(
        split,
        quarter,
        jnp.stack(pick(tokens)),
        in_weight.reshape(depth, 3 * cols),
        out_weight,
        up_weight,
        down_weight,
        wide,
        biases,
        jnp.stack(cots),
    )
    bias_up = biases[:, 0, 3 * cols :].reshape(-1)
    length = 4 * size
    both = (slice(0, length), slice(length, 2 * length))

    def halves(x):
        middle = x.shape[0] // 2
        return lambda i: x[i * middle : (i + 1) * middle]

    def product_of(x, weight, contract):
        part = halves(x)
        return lambda i: dot(part(i), weight, contract)

    scaled1, inverse1 = zip(*[stats(x) for x in rows])

    active, dup = [None] * 2, [None] * 2
    for r in (1, 0):
        upward = dot(full2[both[r]], up_all) + bias_up
        tanh = jnp.tanh(0.7978845608028654 * (upward + 0.044715 * upward * upward * upward))
        active[r] = (0.5 * upward * (1.0 + tanh)).astype(BF16)
        slope = (
            0.5 * (1.0 + tanh)
            + 0.5
            * upward
            * (1.0 - tanh * tanh)
            * 0.7978845608028654
            * (1.0 + 3 * 0.044715 * upward * upward)
        )
        dup[r] = (dot(full_cot[both[r]], down_all, ((1,), (1,))) * slope).astype(BF16)
    grad_up_bias = jnp.sum(dup[0], 0, dtype=F32) + jnp.sum(dup[1], 0, dtype=F32)
    dup, act = jnp.concatenate(dup, 0), jnp.concatenate(active, 0)
    dres, full_dres, grad_down, up_parts, sums2 = run_middle(
        split, dup, act, full2, full_cot, up_all, jnp.stack(cots), resid, wide, hidden, depth
    )[:5]
    mixed = [None] * 2
    for r in (1, 0):
        summed = scatter4(product_of(active[r], down_all, ((1,), (0,))))
        mixed[r] = (resid[r] + summed + down_bias).astype(BF16)

    grad_in, grad_out, grad_up, kept, halves_far, returned, dproj_sums = run_last(
        split, quarter, proj, proj_prefix, attended, full_dres, out_all, in_all, full1, prefix1, up_parts, lse
    )[:7]
    dnormed1 = [kept[r].astype(F32) + halves_far[r].astype(F32) for r in range(2)]
    at_g = lax.axis_index("g")
    for k in range(1, groups):
        dnormed1[0] += jnp.where(at_g + k < groups, returned[k - 1].astype(F32), 0.0)
    grad_in = grad_in.reshape(in_weight.shape)
    tokens_grad, sums1 = [], []
    for r in range(2):
        tokens_grad.append(
            (dres[r] + norm_back(dnormed1[r], scaled1[r], inverse1[r], first_gain)).astype(BF16)
        )
        sums1.append(jnp.stack([jnp.sum(dnormed1[r] * scaled1[r], 0), jnp.sum(dnormed1[r], 0)]))

    sums = dproj_sums.reshape(2, groups, 3, cols)
    grad_q_bias = sums[0, :, 0]
    grad_v_bias = sums[0, :, 2] + sums[1, :, 2]

    def to_owner(x):
        share = x.reshape(groups, -1)
        return functools.reduce(
            jnp.add,
            [share[0]] + [turn(share[g], split, (0, (-g) % groups)) for g in range(1, groups)],
        )

    def sum_over(x, axes):
        for axis in axes:
            x = sum_axis(x, axis)
        return x

    early = sum_over(sums2, ("c", "h", "g") + DP)
    grad_up_bias = sum_over(to_owner(grad_up_bias), DP)
    late = sum_over(sums1[0] + sums1[1], ("c", "h", "g") + DP)
    grad_in_bias = sum_over(jnp.stack([to_owner(grad_q_bias), to_owner(grad_v_bias)]), DP)
    return (
        unpick(*mixed),
        unpick(*tokens_grad),
        late[0],
        late[1],
        grad_in,
        grad_in_bias,
        grad_out,
        early[0],
        early[1],
        early[2],
        grad_up,
        grad_up_bias,
        grad_down,
        early[3],
    )


def solution(mesh):
    dp, tp = mesh.shape["dp"], mesh.shape["tp"]
    split = Mesh(mesh.devices.reshape(dp // 4, 2, 2, tp // 4, 2, 2), DP + TP)
    in_specs = (
        P(DP, TP, None),
        P(DP, None),
        P(),
        P(),
        P(DP, None, TP),
        P(None, TP),
        P(TP, DP),
        P(),
        P(),
        P(),
        P(DP, TP),
        P(TP),
        P(TP, DP),
        P(),
        P(DP, TP, None),
    )
    out_specs = (
        P(DP, TP, None),
        P(DP, TP, None),
        P(),
        P(),
        P(DP, None, TP),
        P(None, TP),
        P(TP, DP),
        P(),
        P(),
        P(),
        P(DP, TP),
        P(TP),
        P(TP, DP),
        P(),
    )
    return jax.shard_map(local, mesh=split, in_specs=in_specs, out_specs=out_specs, check_vma=False)
```

time: 1290 us -> 1010 us (0.78)
  Pallas kernels: 43.4 us -> 708 us
  waiting for transfers between devices: 533 us -> 36.3 us
  matrix products: 315 us -> 105 us
  local copies, waits for them, and re-layouts: 152 us -> 20.5 us
  starting transfers between devices: 168 us -> 90.5 us
  other arithmetic: 64.2 us -> 38.5 us
    pallas_call x4 -> x3, Pallas kernels: 43.4 us -> 708 us  [the longest x1 295 us: run_forward(): pl.pallas_call(functools.partial(layer_forward, extra, groups, quarter),...]
    ppermute x139 -> x18, waiting for transfers between devices: 463 us -> 36.3 us  [flip(): return lax.ppermute(x, axis, [(0, 1), (1, 0)])]
    dot_general x32 -> x8, matrix products: 315 us -> 105 us  [dot(): lax.dot_general(x, y, (contract, ((), ())), preferred_element_type=F32)]
    ppermute x139 -> x18, starting transfers between devices: 116 us -> 24.7 us  [flip(): return lax.ppermute(x, axis, [(0, 1), (1, 0)])]
    unnamed x272 -> x69, local copies, waits for them, and re-layouts: 62.4 us -> 10 us
    dynamic_update_slice x60 -> x0, local copies, waits for them, and re-layouts: 52 us -> none  [the longest x30 33.1 us: put_in(): lax.dynamic_update_slice(full, piece[:, n * cols:(n + 1) * cols], (d * de...]
    ppermute x12 -> x3, waiting for transfers between devices: 39.2 us -> 0.01 us  [turn(): return lax.ppermute(x, axes, pairs)]
    ppermute x2 -> x0, waiting for transfers between devices: 30.5 us -> none  [the longest x1 30.5 us: local(): lax.ppermute(part, 'g', [(g + k, g) for g in range(groups - k)]).astype(F32)]
  transfers between devices with their start and end apart: 153 -> 21, of which waited for: 61 -> 5; matrix products, arithmetic and copies ran while one was open for 29% -> 7% of each run, Pallas kernels for 1% -> 41%
where the time goes in v2:
time: 1010 us; the launch traced here: 1000 us
  Pallas kernels  708 us (70%)
  matrix products  105 us (10%)
  starting transfers between devices  90.5 us (9%)
  other arithmetic  38.5 us (4%)
  waiting for transfers between devices  36.3 us (4%)
  local copies, waits for them, and re-layouts  20.5 us (2%)
    pallas_call x1, Pallas kernels, run_forward(): pl.pallas_call(functools.partial(layer_forward, extra, groups, quarter),...  295 us
    pallas_call x1, Pallas kernels, run_last(): pl.pallas_call(functools.partial(last_kernel, extra, groups, quarter), in...  242 us
    pallas_call x1, Pallas kernels, run_middle(): pl.pallas_call(functools.partial(middle_kernel, extra, groups), in_specs=...  172 us
    dot_general x8, matrix products, dot(): lax.dot_general(x, y, (contract, ((), ())), preferred_element_type=F32)  105 us
    ppermute x3, starting transfers between devices, turn(): return lax.ppermute(x, axes, pairs)  65.8 us
    ppermute x18, waiting for transfers between devices, flip(): return lax.ppermute(x, axis, [(0, 1), (1, 0)])  36.3 us
    ppermute x18, starting transfers between devices, flip(): return lax.ppermute(x, axis, [(0, 1), (1, 0)])  24.7 us
  transfers between devices with their start and end apart: 21, of which 5 were waited for; matrix products, arithmetic and copies ran while one was open for 7% of the time, Pallas kernels for 41%

profile of v2, /device:TPU:0, one launch (start us, length us, event | category | flops | bytes accessed | tf_op | source)
XLA Modules:
  0.0 1001.2 jit_solution(15657414430307794300)
XLA Ops:
  0.7 1.4 slice.125
  2.7 0.8 fusion.75
  3.5 1.4 copy.31
  4.9 1.2 copy.32.refs_1_
  6.2 1.4 copy-done.11
  7.6 0.9 convert_reduce_fusion.3
  8.6 1.5 pad_maximum_fusion.3.refs_7_.refs_5_
  10.1 1.5 pad_maximum_fusion.2.refs_0_
  11.7 0.7 stack.88.refs_5_.refs_7_
  12.4 0.6 broadcast_in_dim.8.refs_6_
  13.0 295.4 %shard_map.254 = (bf16[2048,1536]{1,0:T(8,128)(2,1)}, bf16[512,2048]{1,0:T(8,128)(2,1)}, bf16[2048,2048]{1,0:T(8,128)(2,1)}, bf16[2048,2048]{1,0:T(8,128)(2,1)},...) custom-call(bf16[2,256,2048]{2,1,0:T(8,128)(2,1)} %pad_maximum_fusio, ...), custom_call_target="tpu_custom_call" | custom-call | flops 99999997952 | bytes 100000000 | tf_op jit(solution)/shard_map/pallas_call | solution.py:553
  308.4 0.8 slice.130
  309.3 14.7 %fusion.16 = f32[1024,2048]{1,0:T(8,128)} fusion(bf16[2048,2048]{1,0:T(8,128)(2,1)} %get-tuple-element.42.refs_4_, bf16[2048,2048]{1,0:T(8,128)(2,1)} %get-tuple-element.41.refs_2_), kind=kOutput, calls=%fused_computation.27 | convolution fusion | flops 8589934592 | bytes 20971520 | tf_op jit(solution)/shard_map/dot_general | solution.py:24
  323.9 21.6 %multiply_convert_fusion.1 = (bf16[1024,2048]{1,0:T(8,128)(2,1)}, bf16[1024,2048]{1,0:T(8,128)(2,1)S(1)}, f32[1024,2048]{1,0:T(8,128)}) fusion(f32[2048]{0:T(1024)S(1)} %bitcast.118, f32[1024,2048]{1,0:T(8,128)} %fusion.16, bf16[2048,2048]{1,0:T(8,128)(2,1)} %get-tuple-element.42.refs_4_, bf16[2048,2048]{1,0:T(8,128)(2,1)} %get-tuple-element.41.refs_2_), kind=kOutput, calls=%fused_computation.23 | convolution fusion | flops 8631877632 | bytes 37756928 | tf_op jit(solution)/shard_map/dot_general | solution.py:24
  345.5 19.8 %convert_reduce_fusion = (f32[2048]{0:T(1024)S(1)}, bf16[1024,2048]{1,0:T(8,128)(2,1)}) fusion(f32[1024,2048]{1,0:T(8,128)} %fusion.16, f32[2048]{0:T(1024)S(1)} %bitcast.119, bf16[2048,2048]{1,0:T(8,128)(2,1)S(1)} %bitcast.138, bf16[2048,2048]{1,0:T(8,128)(2,1)} %get-tuple-element.45.refs_3_), kind=kOutput, calls=%fused_computation.20 | convolution fusion | flops 8636069888 | bytes 25182208 | tf_op jit(solution)/shard_map/dot_general | solution.py:24
  365.3 18.3 %convert_reduce_fusion.1 = (f32[2048]{0:T(1024)S(1)}, bf16[1024,2048]{1,0:T(8,128)(2,1)}) fusion(f32[1024,2048]{1,0:T(8,128)} %get-tuple-element.130, f32[2048]{0:T(1024)S(1)} %bitcast.120, bf16[2048,2048]{1,0:T(8,128)(2,1)S(1)} %bitcast.138, bf16[2048,2048]{1,0:T(8,128)(2,1)} %get-tuple-element.45.refs_3_), kind=kOutput, calls=%fused_computation.21 | convolution fusion | flops 8636069888 | bytes 25182208 | tf_op jit(solution)/shard_map/dot_general | solution.py:24
  383.7 0.6 copy-done.18
  384.3 0.6 slice.183
  384.9 62.8 %collective-permute-start.18 = (f32[1024]{0:T(1024)}, f32[1024]{0:T(1024)}, u32[]{:S(2)}, u32[]{:S(2)}) collective-permute-start(f32[1024]{0:T(1024)} %slice.183), channel_id=1, source_target_pairs={{0,4},{4,0},{1,5},{5,1},{2,6},{6,2},{3,7},{7,3},{8,12},{12,8},{9,1... | collective-permute-start | bytes 12296 | tf_op jit(solution)/shard_map/ppermute | solution.py:60
  447.7 6.2 convolution_convert_fusion
  454.0 8.4 pad_maximum_fusion.1.refs_1_
  462.4 8.3 pad_maximum_fusion.refs_0_
  470.7 171.5 %shard_map.255 = (f32[2,256,2048]{2,1,0:T(8,128)}, bf16[2048,2048]{1,0:T(8,128)(2,1)}, f32[1024,512]{1,0:T(8,128)}, bf16[8,512,1024]{2,1,0:T(8,128)(2,1)}, f32[4...) custom-call(bf16[2048,2048]{1,0:T(8,128)(2,1)} %pad_maximum_fusion.r, ...), custom_call_target="tpu_custom_call" | custom-call | flops 99999997952 | bytes 100000000 | tf_op jit(solution)/shard_map/pallas_call | solution.py:1186
  642.3 241.5 %shard_map.256 = (f32[512,768]{1,0:T(8,128)}, f32[256,512]{1,0:T(8,128)}, f32[512,1024]{1,0:T(8,128)}, bf16[2,256,2048]{2,1,0:T(8,128)(2,1)}, bf16[3,256,2048]{2...) custom-call(bf16[2048,1536]{1,0:T(8,128)(2,1)} %get-tuple-element.47, ...), custom_call_target="tpu_custom_call" | custom-call | flops 99999997952 | bytes 100000000 | tf_op jit(solution)/shard_map/pallas_call | solution.py:1238
  883.8 0.8 reshape.195
  884.7 2.9 collective-permute-start.9
  887.7 1.6 fusion.41
  889.3 3.4 fusion.40
  892.8 4.2 fusion.66
  897.1 1.3 copy-done.4
  898.4 1.0 fusion.26
  899.5 10.0 convolution_convert_fusion.1
  909.5 0.8 fusion.33
  910.4 1.6 maximum_select_fusion.1
  912.0 1.9 copy.33
  913.9 1.6 copy.34
  916.1 6.9 collective-permute-start.5
  923.0 1.7 collective-permute-done.5
  925.3 2.9 collective-permute-start.6
  928.2 2.1 collective-permute-start.14
  930.3 0.7 slice_add_fusion.2
  931.0 1.6 collective-permute-start.19
  932.5 1.2 collective-permute-start.7
  933.8 1.3 collective-permute-start.15
  935.0 1.9 collective-permute-start.12
  936.9 0.6 collective-permute-start.20
  937.5 1.1 collective-permute-done.15
  938.6 1.0 collective-permute-start.8
  939.6 1.2 collective-permute-start.16
  940.8 9.6 convert_add_fusion
  950.6 2.3 collective-permute-start.3
  953.0 4.8 convert_add_fusion.1
  958.0 0.6 fusion.84
  958.6 0.6 add.242
  959.8 0.6 fusion.73
  960.4 2.8 collective-permute-done.17
  963.2 0.6 fusion.71
  963.9 13.2 %collective-permute-done.3 = bf16[256,2048]{1,0:T(8,128)(2,1)S(1)} collective-permute-done((bf16[256,2048]{1,0:T(8,128)(2,1)S(1)}, bf16[256,2048]{1,0:T(8,128)(2,1)S(1)}, u32[]{:S(2)}, u32[]{:S(2)}) %collective-permute-start.3) | collective-permute-done | bytes 1048608 | tf_op jit(solution)/shard_map/ppermute | solution.py:44
  977.0 17.5 %collective-permute-done.1 = bf16[256,2048]{1,0:T(8,128)(2,1)S(1)} collective-permute-done((bf16[256,2048]{1,0:T(8,128)(2,1)S(1)}, bf16[256,2048]{1,0:T(8,128)(2,1)S(1)}, u32[]{:S(2)}, u32[]{:S(2)}) %collective-permute-start.1) | collective-permute-done | bytes 1048608 | tf_op jit(solution)/shard_map/ppermute | solution.py:44
  994.5 1.2 fusion.67
  995.8 1.6 maximum_select_fusion
  997.5 0.8 copy.38
  998.3 1.3 copy.39
  999.6 1.3 copy.40
  (120 shorter events, 2.9 us)
Async XLA Ops:
  0.6 5.4 copy-start.10
  6.1 1.6 copy-start.11
  8.6 3.1 copy-start
  8.6 3.1 copy-start.2
  8.6 3.1 copy-start.27
  8.6 3.1 copy-start.15
  8.6 3.1 copy-start.20
  8.6 3.1 copy-start.21
  8.6 3.1 copy-start.22
  8.6 3.1 copy-start.23
  309.3 36.3 %slice-start = ((s8[8388608]{0:T(1024)(128)(4,1)}), s8[4194304]{0:T(1024)(128)(4,1)S(1)}, s32[]{:S(2)}) async-start(s8[8388608]{0:T(1024)(128)(4,1)} %bitcast.137), calls=%async_computation | async-start | bytes 8388608
  323.9 21.6 %slice-start.1 = ((s8[8388608]{0:T(1024)(128)(4,1)}), s8[4194304]{0:T(1024)(128)(4,1)S(1)}, s32[]{:S(2)}) async-start(s8[8388608]{0:T(1024)(128)(4,1)} %bitcast.137), calls=%async_computation.1 | async-start | bytes 8388608
  345.5 102.2 %copy-start.9 = (bf16[1024,2048]{1,0:T(8,128)(2,1)}, bf16[1024,2048]{1,0:T(8,128)(2,1)S(1)}, u32[]{:S(2)}) copy-start(bf16[1024,2048]{1,0:T(8,128)(2,1)S(1)} %get-tuple-element.125) | copy-start | bytes 12582916
  383.7 0.6 copy-start.18
  384.9 543.3 %collective-permute-start.18 = (f32[1024]{0:T(1024)}, f32[1024]{0:T(1024)}, u32[]{:S(2)}, u32[]{:S(2)}) collective-permute-start(f32[1024]{0:T(1024)} %slice.183), channel_id=1, source_target_pairs={{0,4},{4,0},{1,5},{5,1},{2,6},{6,2},{3,7},{7,3},{8,12},{12,8},{9,1... | collective-permute-start | bytes 12296 | tf_op jit(solution)/shard_map/ppermute | solution.py:60
  453.9 485.8 %collective-permute-start.2 = (bf16[512,2048]{1,0:T(8,128)(2,1)}, bf16[512,2048]{1,0:T(8,128)(2,1)}, u32[]{:S(2)}, u32[]{:S(2)}) collective-permute-start(bf16[512,2048]{1,0:T(8,128)(2,1)} %convolution_convert_fusion), channel_id=1, source_target_pairs={{0,1},{1,0},{2,3},{3,2},{4,5},{5,4},{6,7},{7,6},{8,9},{9,8},{10,11... | collective-permute-start | bytes 6291464 | tf_op jit(solution)/shard_map/ppermute | solution.py:44
  642.2 245.4 %copy-start.26 = (f32[256]{0:T(256)S(1)}, f32[256]{0:T(256)}, u32[]{:S(2)}) copy-start(f32[256]{0:T(256)} %get-tuple-element.102) | copy-start | bytes 3076
  642.3 245.4 %copy-start.25 = (f32[256]{0:T(256)S(1)}, f32[256]{0:T(256)}, u32[]{:S(2)}) copy-start(f32[256]{0:T(256)} %get-tuple-element.114) | copy-start | bytes 3076
  642.3 247.0 %copy-start.16 = (f32[2048]{0:T(1024)S(1)}, f32[2048]{0:T(1024)}, u32[]{:S(2)}) copy-start(f32[2048]{0:T(1024)} %param.17) | copy-start | bytes 24580
  883.8 9.0 copy-start.1
  884.6 30.9 %collective-permute-start.10 = (f32[256]{0:T(256)S(1)}, f32[256]{0:T(256)S(1)}, u32[]{:S(2)}, u32[]{:S(2)}) collective-permute-start(f32[256]{0:T(256)S(1)} %bitcast.136), channel_id=1, source_target_pairs={{0,4},{4,0},{1,5},{5,1},{2,6},{6,2},{3,7},{7,3},{8,12},{12,8},{9,1... | collective-permute-start | bytes 3080 | tf_op jit(solution)/shard_map/ppermute | solution.py:60
  884.7 31.2 %collective-permute-start.9 = (f32[256]{0:T(256)S(1)}, f32[256]{0:T(256)S(1)}, u32[]{:S(2)}, u32[]{:S(2)}) collective-permute-start(f32[256]{0:T(256)S(1)} %bitcast.135), channel_id=1, source_target_pairs={{0,4},{4,0},{1,5},{5,1},{2,6},{6,2},{3,7},{7,3},{8,12},{12,8},{9,1... | collective-permute-start | bytes 3080 | tf_op jit(solution)/shard_map/ppermute | solution.py:60
  892.8 5.6 copy-start.3
  897.1 1.3 copy-start.4
  899.4 16.7 %collective-permute-start.4 = (f32[2,2048]{1,0:T(2,128)S(1)}, f32[2,2048]{1,0:T(2,128)S(1)}, u32[]{:S(2)}, u32[]{:S(2)}) collective-permute-start(f32[2,2048]{1,0:T(2,128)S(1)} %maximum_add_fusion), channel_id=1, source_target_pairs={{0,1},{1,0},{2,3},{3,2},{4,5},{5,4},{6,7},{7,6},{8,9},{9,8},{10,11... | collective-permute-start | bytes 49160 | tf_op jit(solution)/shard_map/ppermute | solution.py:44
  899.5 10.0 copy-start.5
  899.5 10.0 copy-start.6
  912.0 4.0 copy-start.17
  912.0 18.3 %copy-start.19 = (f32[2048]{0:T(1024)S(1)}, f32[2048]{0:T(1024)}, u32[]{:S(2)}) copy-start(f32[2048]{0:T(1024)} %copy-done.18) | copy-start | bytes 24580
  915.5 35.1 %collective-permute-start = (bf16[512,2048]{1,0:T(8,128)(2,1)}, bf16[512,2048]{1,0:T(8,128)(2,1)S(1)}, u32[]{:S(2)}, u32[]{:S(2)}) collective-permute-start(bf16[512,2048]{1,0:T(8,128)(2,1)} %convolution_convert_fusion.1), channel_id=1, source_target_pairs={{0,1},{1,0},{2,3},{3,2},{4,5},{5,4},{6,7},{7,6},{8,9},{9,8},{10,11... | collective-permute-start | bytes 6291464 | tf_op jit(solution)/shard_map/ppermute | solution.py:44
  916.0 9.3 collective-permute-start.13
  916.1 8.6 collective-permute-start.5
  924.7 9.0 collective-permute-start.11
  925.3 5.7 collective-permute-start.6
  928.2 4.3 collective-permute-start.14
  931.0 4.1 collective-permute-start.19
  932.5 4.4 collective-permute-start.7
  933.8 4.9 collective-permute-start.15
  935.0 22.9 %collective-permute-start.12 = (f32[2,256]{1,0:T(2,128)S(1)}, f32[2,256]{1,0:T(2,128)S(1)}, u32[]{:S(2)}, u32[]{:S(2)}) collective-permute-start(f32[2,256]{1,0:T(2,128)S(1)} %fusion.69), channel_id=1, source_target_pairs={{0,8},{8,0},{1,9},{9,1},{2,10},{10,2},{3,11},{11,3},{4,12},{12,4},... | collective-permute-start | bytes 6152 | tf_op jit(solution)/shard_map/ppermute | solution.py:44
  936.9 21.7 %collective-permute-start.20 = (f32[1024]{0:T(1024)S(1)}, f32[1024]{0:T(1024)S(1)}, u32[]{:S(2)}, u32[]{:S(2)}) collective-permute-start(f32[1024]{0:T(1024)S(1)} %add.241), channel_id=1, source_target_pairs={{0,8},{8,0},{1,9},{9,1},{2,10},{10,2},{3,11},{11,3},{4,12},{12,4},... | collective-permute-start | bytes 12296 | tf_op jit(solution)/shard_map/ppermute | solution.py:44
  938.6 20.6 %collective-permute-start.8 = (f32[2,2048]{1,0:T(2,128)S(1)}, f32[2,2048]{1,0:T(2,128)S(1)}, u32[]{:S(2)}, u32[]{:S(2)}) collective-permute-start(f32[2,2048]{1,0:T(2,128)S(1)} %add.227), channel_id=1, source_target_pairs={{0,8},{8,0},{1,9},{9,1},{2,10},{10,2},{3,11},{11,3},{4,12},{12,4},... | collective-permute-start | bytes 49160 | tf_op jit(solution)/shard_map/ppermute | solution.py:44
  939.6 13.3 %slice-start.2 = ((s8[8388608]{0:T(1024)(128)(4,1)}), s8[4194304]{0:T(1024)(128)(4,1)S(1)}, s32[]{:S(2)}) async-start(s8[8388608]{0:T(1024)(128)(4,1)} %bitcast.139), calls=%async_computation.2 | async-start | bytes 8388608
  939.6 13.3 %copy-start.8 = (bf16[1024,2048]{1,0:T(8,128)(2,1)S(1)}, bf16[1024,2048]{1,0:T(8,128)(2,1)}, u32[]{:S(2)}) copy-start(bf16[1024,2048]{1,0:T(8,128)(2,1)} %get-tuple-element.124) | copy-start | bytes 12582916
  939.6 13.3 %slice-start.3 = ((s8[8388608]{0:T(1024)(128)(4,1)}), s8[4194304]{0:T(1024)(128)(4,1)S(1)}, s32[]{:S(2)}) async-start(s8[8388608]{0:T(1024)(128)(4,1)} %bitcast.139), calls=%async_computation.3 | async-start | bytes 8388608
  939.6 19.6 %collective-permute-start.16 = (f32[4,2048]{1,0:T(4,128)S(1)}, f32[4,2048]{1,0:T(4,128)S(1)}, u32[]{:S(2)}, u32[]{:S(2)}) collective-permute-start(f32[4,2048]{1,0:T(4,128)S(1)} %add.236), channel_id=1, source_target_pairs={{0,16},{16,0},{1,17},{17,1},{2,18},{18,2},{3,19},{19,3},{4,20},{20... | collective-permute-start | bytes 98312 | tf_op jit(solution)/shard_map/ppermute | solution.py:44
  950.6 43.9 %copy-start.24 = (f32[2048]{0:T(1024)S(1)}, f32[2048]{0:T(1024)}, u32[]{:S(2)}) copy-start(f32[2048]{0:T(1024)} %param.28) | copy-start | bytes 24580
  950.6 26.4 %collective-permute-start.3 = (bf16[256,2048]{1,0:T(8,128)(2,1)S(1)}, bf16[256,2048]{1,0:T(8,128)(2,1)S(1)}, u32[]{:S(2)}, u32[]{:S(2)}) collective-permute-start(bf16[256,2048]{1,0:T(8,128)(2,1)S(1)} %slice.248), channel_id=1, source_target_pairs={{0,2},{2,0},{1,3},{3,1},{4,6},{6,4},{5,7},{7,5},{8,10},{10,8},{9,1... | collective-permute-start | bytes 3145736 | tf_op jit(solution)/shard_map/ppermute | solution.py:44
  952.9 41.6 %copy-start.7 = (f32[2,256,2048]{2,1,0:T(8,128)S(1)}, f32[2,256,2048]{2,1,0:T(8,128)}, u32[]{:S(2)}) copy-start(f32[2,256,2048]{2,1,0:T(8,128)} %get-tuple-element.40.refs_6_) | copy-start | bytes 12582916
  957.9 36.6 %collective-permute-start.1 = (bf16[256,2048]{1,0:T(8,128)(2,1)S(1)}, bf16[256,2048]{1,0:T(8,128)(2,1)S(1)}, u32[]{:S(2)}, u32[]{:S(2)}) collective-permute-start(bf16[256,2048]{1,0:T(8,128)(2,1)S(1)} %slice.249), channel_id=1, source_target_pairs={{0,2},{2,0},{1,3},{3,1},{4,6},{6,4},{5,7},{7,5},{8,10},{10,8},{9,1... | collective-permute-start | bytes 3145736 | tf_op jit(solution)/shard_map/ppermute | solution.py:44
  959.2 4.0 collective-permute-start.17
  995.8 1.7 copy-start.14
  995.8 2.5 copy-start.13
  995.8 3.8 copy-start.12

commit v3 on v2

--- a/solution.py
+++ b/solution.py
@@ -42,13 +42,6 @@
 
 def flip(x, axis):
     return lax.ppermute(x, axis, [(0, 1), (1, 0)])
-
-
-def scatter4(product):
-    away = product(1).astype(BF16)
-    kept = product(0) + flip(away, "c").astype(F32)
-    local = kept.shape[0] // 2
-    return kept[:local] + flip(kept[local:].astype(BF16), "h").astype(F32)
 
 
 def turn(x, groups, by, axes=("e", "g")):
@@ -397,107 +390,102 @@
     bias_here[0] = bias_ref[...]
     first_norm(0)
     spread = [spread_to(norm_here.at[pl.ds(0, size), :], norm_here, 0), None]
-    before = []
-    for k in range(1, groups):
-        copy = copies.remote(
-            norm_here.at[pl.ds(0, size), :],
-            prefix_here.at[pl.ds((k - 1) * length, size), :],
-            places.further((0, k)),
-            tracked=False,
-        )
-        pl.when(places.g + k < groups)(copy.start)
-        before.append(copy)
     first_norm(1)
     spread[1] = spread_to(norm_here.at[pl.ds(length, size), :], norm_here, length)
     w_in.second(False)
     w_out.own()
     w_out.turn()
     spread[0].forward()
+    w_out.second(False)
     w_in.turned()
-    w_out.second(False)
+
+    before, later = [], []
+    for k in range(1, groups):
+        row = (k - 1) * length
+        slot = [prefix_here.at[pl.ds(row + n * size, size), :] for n in range(4)]
+        copy = copies.remote(
+            norm_here.at[pl.ds(0, size), :], slot[0], places.further((0, k)), tracked=False
+        )
+        pl.when(places.g + k < groups)(copy.start)
+        before.append(copy)
+        far = copies.remote(slot[0], slot[1], places.to_h, tracked=False)
+        core = copies.remote(slot[0], slot[2], places.to_c, tracked=False)
+        last = copies.remote(slot[1], slot[3], places.to_c, tracked=False)
+        later.append((far, core, last))
+
+    def for_prefix(action):
+        for k in range(1, groups):
+            pl.when(places.g >= k)(functools.partial(action, k - 1))
+
+    def prefix_came(k):
+        before[k].wait_recv()
+        later[k][0].start()
+        later[k][1].start()
+
+    def prefix_forward(k):
+        later[k][0].wait_recv()
+        later[k][2].start()
+
+    def prefix_finish(k):
+        later[k][1].wait_recv()
+        later[k][2].wait_recv()
+
+    for k in range(1, groups):
+
+        @pl.when(places.g < k)
+        def _():
+            in_tiles(length, size, lambda t: clear((k - 1) * length + t))
+
     spread[1].forward()
     w_in.second(True)
+    w_in.finish(False)
+    w_in.finish(True)
     w_up.own()
-    w_up.turn()
+    w_out.turned()
+    copies.local(in_here, in_all)
+    for copy in bias_steps:
+        copy.wait_recv()
     spread_cot = []
     for r in range(2):
         copies.local(cots_ref.at[r], full_cot.at[pl.ds(r * length, size), :])
         spread_cot.append(spread_to(cots_ref.at[r], full_cot, r * length))
-
-    later = []
-    for k in range(1, groups):
-        row = (k - 1) * length
-        slot = [prefix_here.at[pl.ds(row + n * size, size), :] for n in range(4)]
-        far = copies.remote(slot[0], slot[1], places.to_h, tracked=False)
-        core = copies.remote(slot[0], slot[2], places.to_c, tracked=False)
-        last = copies.remote(slot[1], slot[3], places.to_c, tracked=False)
-        later.append((far, core, last))
-
-        @pl.when(places.g >= k)
-        def _():
-            before[k - 1].wait_recv()
-            far.start()
-            core.start()
-
-        @pl.when(places.g < k)
-        def _():
-            in_tiles(length, size, lambda t: clear(row + t))
-
-    w_in.finish(False)
-    w_in.finish(True)
-    copies.local(in_here, in_all)
-    for copy in bias_steps:
-        copy.wait_recv()
     spread[1].finish()
     project(norm_here, length, proj, length, 0)
-    w_out.turned()
+    w_out.second(True)
     attention(1, quarter)
-    w_out.second(True)
-    w_up.second(False)
-    for k in range(1, groups):
-        far, core, last = later[k - 1]
-
-        @pl.when(places.g >= k)
-        def _():
-            far.wait_recv()
-            last.start()
-
     spread[0].finish()
     copies.local(norm_here, full1)
-    project(norm_here, 0, proj, 0, 0)
+    w_up.second(False)
     w_out.finish(False)
     w_out.finish(True)
     copies.local(out_here, out_all)
     out_product(1)
     w_down.own()
-    for k in range(1, groups):
-        far, core, last = later[k - 1]
-
-        @pl.when(places.g >= k)
-        def _():
-            core.wait_recv()
-            last.wait_recv()
-
+    for_prefix(prefix_came)
+    w_up.turn()
+    project(norm_here, 0, proj, 0, 0)
+    copies.local(proj, proj_out)
+    out_sum(1)
+    for_prefix(prefix_forward)
+    w_down.second(False)
+    spread_cot[0].forward()
+    spread_cot[1].forward()
+    for_prefix(prefix_finish)
     for k in range(1, groups):
         project(prefix_here, (k - 1) * length, prefix_proj, (k - 1) * length, 1)
     copies.local(prefix_here, prefix1)
     copies.local(prefix_proj, prefix_out)
-    copies.local(proj, proj_out)
-    out_sum(1)
-    w_up.turned()
+    spread2 = [None, second_norm(1)]
     w_down.turn()
-    spread_cot[0].forward()
-    spread_cot[1].forward()
     attention(0, None)
     copies.local(att, att_out)
     copies.local(lse, lse_out)
     out_product(0)
-    w_down.second(False)
-    spread2 = [None, second_norm(1)]
+    w_up.turned()
     out_sum(0)
+    spread2[1].forward()
     w_up.second(True)
     spread2[0] = second_norm(0)
-    spread2[1].forward()
     w_down.turned()
     spread2[0].forward()
     w_up.finish(False)
@@ -731,60 +719,102 @@
 
 def middle_kernel(extra, groups, *refs):
     (
-        dup, act, full2, full_cot, up_all, cots, resid, wide,
-        dres, full_dres, grad_down, up_parts, sums, down_parts, land, turned,
-        big, narrow, tiles, c_send, c_recv, h_send, h_recv, low, stage_down, stage_up, work, own,
+        full2, full_cot, up_all, down_all, resid, wide, bias_up,
+        mixed, full_dres, grad_down, up_parts, sums, up_sums, act, dup, down_parts, land, turned,
+        big, down, narrow, tiles, cots, c_send, c_recv, h_send, h_recv, low, stage_down, work, own,
         fetched, send_sem, recv_sem, near_sem, free,
     ) = refs
-    size, width = cots.shape[1:]
+    size, width = mixed.shape[1:]
     length = 4 * size
     hidden, depth = grad_down.shape
     shares = extra * 4
     chunk = min(64, size)
+    strip = min(512, hidden)
     places = Places(extra, groups)
     copies = Copies(send_sem, recv_sem, near_sem)
     sources = len(places.offsets)
-    down = GradScatter(
+    scatter = GradScatter(
         copies, places, down_parts, land, turned, work, own, fetched, grad_down
     )
     fold = Fold(copies, places, c_send, c_recv, h_send, free, size)
-    folded = []
+    folded = {}
+
+    def load(source, target):
+        return copies.local(source, target, tracked=False)
 
     def load_big(source):
-        return copies.local(source, big.at[: source.shape[0]], tracked=False)
-
-    loading = load_big(up_all)
+        return load(source, big.at[: source.shape[0]])
+
+    loading = [load_big(up_all), load(down_all, down)]
+    tile_slots = [tiles.at[0], tiles.at[1]]
+    cot_slots = [cots.at[0], cots.at[1]]
+    narrow_slots = [narrow.at[0], narrow.at[1]]
     order = [(r, slot) for r in range(2) for slot in (2, 3, 1, 0)]
-    tile_slots = [tiles.at[0], tiles.at[1]]
-    narrow_slots = [narrow.at[0], narrow.at[1]]
+    where = [pl.ds(r * length + s * size, size) for r, s in order]
     stream = Stream(
-        copies, [tile_slots], [[dup.at[pl.ds(r * length + s * size, size), :]] for r, s in order]
+        copies, [tile_slots, cot_slots], [[full2.at[w, :], full_cot.at[w, :]] for w in where]
     )
     places.barrier()
     sums[...] = jnp.zeros_like(sums)
-    loading.wait()
-
-    def block_of(r):
+    up_sums[...] = jnp.zeros_like(up_sums)
+    for copy in loading:
+        copy.wait()
+
+    stored = {}
+    for n, (r, slot) in enumerate(order):
+        at = stream.take(n)
+        if n >= 2:
+            for copy in stored.pop(n - 2):
+                copy.wait()
+        act_at, dup_at = c_send.at[pl.ds(at * size, size), :], low.at[at]
+
+        def body(g, _):
+            columns = pl.ds(pl.multiple_of(g * strip, HDIM), strip)
+            value = dot(tiles[at], big[:width, columns]) + bias_up[:1, columns]
+            square = value * value
+            tanh = jnp.tanh(0.7978845608028654 * value * (1.0 + 0.044715 * square))
+            half = 0.5 * (1.0 + tanh)
+            act_at[:, columns] = (value * half).astype(BF16)
+            slope = half + 0.5 * value * (1.0 - tanh * tanh) * 0.7978845608028654 * (
+                1.0 + 3 * 0.044715 * square
+            )
+            back = (dot(cots[at], down[columns, :], ((1,), (1,))) * slope).astype(BF16)
+            dup_at[:, columns] = back
+            up_sums[:, columns] += jnp.sum(back.astype(F32), axis=0, keepdims=True)
+            return 0
+
+        lax.fori_loop(0, groups * hidden // strip, body, 0)
+        stored[n] = [
+            load(act_at, act.at[where[n], :]),
+            load(dup_at, dup.at[where[n], :]),
+        ]
+    for n in list(stored):
+        for copy in stored.pop(n):
+            copy.wait()
+
+    own_cots = [load(full_cot.at[pl.ds(r * length, size), :], cots.at[r]) for r in range(2)]
+    stream_dup = Stream(copies, [tile_slots], [[dup.at[w, :]] for w in where])
+
+    def dup_block(r):
         def block(slot):
-            at = stream.take(order.index((r, slot)))
+            at = stream_dup.take(order.index((r, slot)))
             return dot(tiles[at], big[:width], ((1,), (1,)))
 
         return block
 
     for r in range(2):
-        fold.away(block_of(r))
-        folded.append(fold.kept(block_of(r), dres.at[r], h_recv.at[r], r == 0))
+        fold.away(dup_block(r))
+        folded[r] = fold.kept(dup_block(r), low.at[r], h_recv.at[r], True)
 
     def norm_back_rows(r):
         folded[r].wait_recv()
 
         def body(t):
             rows = pl.ds(t, chunk)
-            grad = dres[r, rows, :] + h_recv[r, rows, :].astype(F32)
+            grad = low[r, rows, :].astype(F32) + h_recv[r, rows, :].astype(F32)
             scaled, inverse = stats(resid[r, rows, :])
             cot = cots[r, rows, :].astype(F32)
             value = cot + norm_back(grad, scaled, inverse, wide[3:4])
-            dres[r, rows, :] = value
             low[r, rows, :] = value.astype(BF16)
             for n, term in enumerate((value, grad * scaled, grad, cot)):
                 sums[n : n + 1, :] += jnp.sum(term, axis=0, keepdims=True)
@@ -793,15 +823,17 @@
         copies.local(low.at[r], full_dres.at[pl.ds(r * length, size), :])
         return Spread(copies, places, low.at[r], full_dres, r * length, size)
 
-    def columns(source):
+    def columns_of(source):
         return [
             [source.at[:, pl.ds(d * depth, depth)]] for g in range(groups) for d in range(shares)
         ]
 
     turn_order = list(range(groups))[::-1]
     loading = load_big(act)
-    stream_cot = Stream(copies, [narrow_slots], columns(full_cot))
+    stream_cot = Stream(copies, [narrow_slots], columns_of(full_cot))
     loading.wait()
+    for copy in own_cots:
+        copy.wait()
     put = {}
     count = 0
     spread = [None, None]
@@ -821,65 +853,80 @@
                 ).astype(BF16)
 
             in_tiles(hidden, hidden // 2, body)
-            put[count] = copies.local(
-                stage_down.at[slot], down_parts.at[g * shares + d], tracked=False
-            )
+            put[count] = load(stage_down.at[slot], down_parts.at[g * shares + d])
             count += 1
 
     def of_group(g):
         return [n for n in range(sources) if places.offsets[n][1] == g][::-1]
 
-    def flush():
-        for n in range(max(count - 2, 0), count):
-            if n in put:
-                put.pop(n).wait()
-
     for step, g in enumerate(turn_order):
         down_grad(g)
-        flush()
+        for n in list(put):
+            put.pop(n).wait()
         for n in of_group(g):
-            down.start(n)
+            scatter.start(n)
         if step == 0:
             spread[0] = norm_back_rows(0)
     spread[1] = norm_back_rows(1)
+    for n in of_group(turn_order[0]):
+        scatter.middle(n)
+
+    def act_block(r):
+        def block(slot):
+            return dot(big[r * length + slot * size : r * length + (slot + 1) * size, :], down[...])
+
+        return block
+
+    for r in range(2):
+        fold.away(act_block(r))
+        folded[2 + r] = fold.kept(act_block(r), mixed.at[r], h_recv.at[2 + r], r == 0)
+        spread[r].forward()
+        if r == 0:
+            for g in turn_order[1:]:
+                for n in of_group(g):
+                    scatter.middle(n)
+    for n in of_group(turn_order[0]):
+        if n:
+            scatter.last(n)
+
     loading = load_big(dup)
-    stream_two = Stream(copies, [narrow_slots], columns(full2))
-    for n in of_group(turn_order[0]):
-        down.middle(n)
-    spread[0].forward()
+    stream_two = Stream(copies, [narrow_slots], columns_of(full2))
+    stage_up = [down.at[pl.ds(n * depth, depth), pl.ds(0, hidden)] for n in range(2)]
     loading.wait()
     put_up = {}
     done = 0
-    for step, g in enumerate(turn_order):
+    for g in turn_order:
         for d in range(shares):
             at = stream_two.take(done)
-            slot = done % 2
             if done >= 2:
                 put_up.pop(done - 2).wait()
-            stage_up[slot] = dot(
+            stage_up[done % 2][...] = dot(
                 narrow[at], big[: 2 * length, g * hidden : (g + 1) * hidden], ((0,), (0,))
             ).astype(BF16)
-            put_up[done] = copies.local(
-                stage_up.at[slot], up_parts.at[g * shares + d], tracked=False
-            )
+            put_up[done] = load(stage_up[done % 2], up_parts.at[g * shares + d])
             done += 1
-        if step == 0:
-            for n in of_group(turn_order[0]):
-                if n:
-                    down.last(n)
-            spread[1].forward()
-            for g_next in turn_order[1:]:
-                for n in of_group(g_next):
-                    down.middle(n)
+    for r in range(2):
+        folded[2 + r].wait_recv()
+
+        def add(t):
+            rows = pl.ds(t, chunk)
+            mixed[r, rows, :] = (
+                resid[r, rows, :]
+                + mixed[r, rows, :].astype(F32)
+                + h_recv[2 + r, rows, :].astype(F32)
+                + wide[5:6]
+            ).astype(BF16)
+
+        in_tiles(size, chunk, add)
     for copy in put_up.values():
         copy.wait()
     spread[0].finish()
     spread[1].finish()
     for g in turn_order:
         for n in of_group(g):
-            if (n, "t") not in down.steps:
-                down.last(n)
-    down.total()
+            if (n, "t") not in scatter.steps:
+                scatter.last(n)
+    scatter.total()
     copies.finish()
 
 
@@ -1174,51 +1221,56 @@
     )
 
 
-def run_middle(split, dup, act, full2, full_cot, up_all, cots, resid, wide, hidden, depth):
+def run_middle(split, full2, full_cot, up_all, down_all, resid, wide, bias_up, hidden, depth):
     extra, groups = split
     sources = extra * groups
-    size, width = cots.shape[1:]
+    size, width = resid.shape[1:]
     length = 4 * size
+    all_hidden = groups * hidden
     shape = jax.ShapeDtypeStruct
     anywhere = pl.BlockSpec(memory_space=pl.ANY)
     inside = pl.BlockSpec(memory_space=pltpu.VMEM)
     shares = sources * 4
     return pl.pallas_call(
         functools.partial(middle_kernel, extra, groups),
-        in_specs=[anywhere] * 5 + [inside] * 3,
-        out_specs=[inside, anywhere, inside, anywhere, inside] + [anywhere] * 3,
+        in_specs=[anywhere] * 4 + [inside] * 3,
+        out_specs=[inside, anywhere, inside, anywhere, inside, inside] + [anywhere] * 5,
         out_shape=[
-            shape((2, size, width), F32),
+            shape((2, size, width), BF16),
             shape((2 * length, width), BF16),
             shape((hidden, depth), F32),
             shape((shares, depth, hidden), BF16),
             shape((4, width), F32),
+            shape((1, all_hidden), F32),
+            shape((2 * length, all_hidden), BF16),
+            shape((2 * length, all_hidden), BF16),
             shape((shares, hidden, depth), BF16),
         ]
         + GradScatter.landing(sources, hidden, depth),
         scratch_shapes=[
-            pltpu.VMEM((max(width, 2 * length), groups * hidden), BF16),
+            pltpu.VMEM((max(width, 2 * length), all_hidden), BF16),
+            pltpu.VMEM((all_hidden, width), BF16),
             pltpu.VMEM((2, 2 * length, depth), BF16),
-            pltpu.VMEM((2, size, groups * hidden), BF16),
+            pltpu.VMEM((2, size, width), BF16),
+            pltpu.VMEM((2, size, width), BF16),
             pltpu.VMEM((2 * size, width), BF16),
             pltpu.VMEM((2 * size, width), BF16),
             pltpu.VMEM((size, width), BF16),
-            pltpu.VMEM((2, size, width), BF16),
+            pltpu.VMEM((4, size, width), BF16),
             pltpu.VMEM((2, size, width), BF16),
             pltpu.VMEM((2, hidden, depth), BF16),
-            pltpu.VMEM((2, depth, hidden), BF16),
         ]
         + GradScatter.working(sources, hidden, depth)
         + [
             pltpu.VMEM((3, hidden // 2, depth), BF16),
             pltpu.SemaphoreType.DMA((sources * 8 + 16,)),
             pltpu.SemaphoreType.DMA((sources * 8 + 16,)),
-            pltpu.SemaphoreType.DMA((sources * 16 + 6 * shares + 24,)),
+            pltpu.SemaphoreType.DMA((sources * 16 + 6 * shares + 80,)),
             pltpu.SemaphoreType.REGULAR,
         ],
         compiler_params=kernel_params(1),
         cost_estimate=pl.CostEstimate(flops=10**11, bytes_accessed=10**8, transcendentals=10**6),
-    )(dup, act, full2, full_cot, up_all, cots, resid, wide)
+    )(full2, full_cot, up_all, down_all, resid, wide, bias_up)
 
 
 def run_last(split, quarter, proj, prefix_proj, att, full_dres, out_all, in_all, full1, prefix1, up_parts, lse):
@@ -1326,7 +1378,7 @@
     no_bias = jnp.zeros_like(in_bias[0])
     biases = jnp.concatenate([in_bias[0], no_bias, in_bias[1], up_bias])
     biases = jnp.broadcast_to(biases, (8, biases.shape[0]))
-    wide = jnp.stack([first_gain, first_shift, out_bias, second_gain, second_shift])
+    wide = jnp.stack([first_gain, first_shift, out_bias, second_gain, second_shift, down_bias])
     (
         in_all, out_all, up_all, down_all, biases, full1, prefix1, proj, proj_prefix, attended, lse,
         resid, full2, full_cot,
@@ -1342,43 +1394,14 @@
         biases,
         jnp.stack(cots),
     )
-    bias_up = biases[:, 0, 3 * cols :].reshape(-1)
+    bias_up = biases[:, 0, 3 * cols :].reshape(1, -1)
     length = 4 * size
-    both = (slice(0, length), slice(length, 2 * length))
-
-    def halves(x):
-        middle = x.shape[0] // 2
-        return lambda i: x[i * middle : (i + 1) * middle]
-
-    def product_of(x, weight, contract):
-        part = halves(x)
-        return lambda i: dot(part(i), weight, contract)
-
     scaled1, inverse1 = zip(*[stats(x) for x in rows])
 
-    active, dup = [None] * 2, [None] * 2
-    for r in (1, 0):
-        upward = dot(full2[both[r]], up_all) + bias_up
-        tanh = jnp.tanh(0.7978845608028654 * (upward + 0.044715 * upward * upward * upward))
-        active[r] = (0.5 * upward * (1.0 + tanh)).astype(BF16)
-        slope = (
-            0.5 * (1.0 + tanh)
-            + 0.5
-            * upward
-            * (1.0 - tanh * tanh)
-            * 0.7978845608028654
-            * (1.0 + 3 * 0.044715 * upward * upward)
-        )
-        dup[r] = (dot(full_cot[both[r]], down_all, ((1,), (1,))) * slope).astype(BF16)
-    grad_up_bias = jnp.sum(dup[0], 0, dtype=F32) + jnp.sum(dup[1], 0, dtype=F32)
-    dup, act = jnp.concatenate(dup, 0), jnp.concatenate(active, 0)
-    dres, full_dres, grad_down, up_parts, sums2 = run_middle(
-        split, dup, act, full2, full_cot, up_all, jnp.stack(cots), resid, wide, hidden, depth
-    )[:5]
-    mixed = [None] * 2
-    for r in (1, 0):
-        summed = scatter4(product_of(active[r], down_all, ((1,), (0,))))
-        mixed[r] = (resid[r] + summed + down_bias).astype(BF16)
+    mixed, full_dres, grad_down, up_parts, sums2, grad_up_bias = run_middle(
+        split, full2, full_cot, up_all, down_all, resid, wide, bias_up, hidden, depth
+    )[:6]
+    dres = [full_dres[r * length : r * length + size].astype(F32) for r in range(2)]
 
     grad_in, grad_out, grad_up, kept, halves_far, returned, dproj_sums = run_last(
         split, quarter, proj, proj_prefix, attended, full_dres, out_all, in_all, full1, prefix1, up_parts, lse

time: 1010 us -> 910 us (0.901)
  matrix products: 105 us -> 0 us
  Pallas kernels: 708 us -> 808 us
  starting transfers between devices: 90.5 us -> 43.9 us
  waiting for transfers between devices: 36.3 us -> 5.03 us
  other arithmetic: 38.5 us -> 23.8 us
    dot_general x8 -> x0, matrix products: 105 us -> none  [dot(): lax.dot_general(x, y, (contract, ((), ())), preferred_element_type=F32)]
    pallas_call x1, Pallas kernels: 172 us -> 265 us  [run_middle(): pl.pallas_call(functools.partial(middle_kernel, extra, groups), in_specs=...]
    ppermute x3, starting transfers between devices: 65.8 us -> 8.88 us  [turn(): return lax.ppermute(x, axes, pairs)]
    ppermute x18 -> x14, waiting for transfers between devices: 36.3 us -> 5.02 us  [flip(): return lax.ppermute(x, axis, [(0, 1), (1, 0)])]
    concatenate x2 -> x0, other arithmetic: 16.7 us -> none  [local(): dup, act = (jnp.concatenate(dup, 0), jnp.concatenate(active, 0))]
    ppermute x18 -> x14, starting transfers between devices: 24.7 us -> 35 us  [flip(): return lax.ppermute(x, axis, [(0, 1), (1, 0)])]
  transfers between devices with their start and end apart: 21 -> 17, of which waited for: 5 -> 4; matrix products, arithmetic and copies ran while one was open for 7% -> 3% of each run, Pallas kernels for 41% -> 27%
where the time goes in v3:
time: 910 us; the launch traced here: 906 us
  Pallas kernels  808 us (89%)
  starting transfers between devices  43.9 us (5%)
  other arithmetic  23.8 us (3%)
  local copies, waits for them, and re-layouts  23.4 us (3%)
    pallas_call x1, Pallas kernels, run_forward(): pl.pallas_call(functools.partial(layer_forward, extra, groups, quarter),...  295 us
    pallas_call x1, Pallas kernels, run_middle(): pl.pallas_call(functools.partial(middle_kernel, extra, groups), in_specs=...  265 us
    pallas_call x1, Pallas kernels, run_last(): pl.pallas_call(functools.partial(last_kernel, extra, groups, quarter), in...  247 us
    ppermute x14, starting transfers between devices, flip(): return lax.ppermute(x, axis, [(0, 1), (1, 0)])  35 us
  transfers between devices with their start and end apart: 17, of which 4 were waited for; matrix products, arithmetic and copies ran while one was open for 3% of the time, Pallas kernels for 27%

profile of v3, /device:TPU:0, one launch (start us, length us, event | category | flops | bytes accessed | tf_op | source)
XLA Modules:
  0.0 905.8 jit_solution(12655394062626401593)
XLA Ops:
  0.6 1.3 slice.82
  2.6 0.0 copy-start.9
  2.6 2.6 convert_reduce_fusion.1
  5.2 1.3 constant_dynamic-slice_fusion.1
  6.5 2.3 copy.31
  8.8 2.3 copy.32.refs_1_
  11.1 0.0 copy-start.17
  11.1 0.0 copy-start.18
  11.1 0.0 copy-start.19
  11.1 0.0 copy-start.20
  11.1 0.0 copy-start.21
  11.2 3.7 pad_maximum_fusion
  14.9 0.7 stack.83.refs_5_
  15.6 0.6 broadcast_in_dim.9.refs_6_
  16.2 295.3 %shard_map.254 = (bf16[2048,1536]{1,0:T(8,128)(2,1)}, bf16[512,2048]{1,0:T(8,128)(2,1)}, bf16[2048,2048]{1,0:T(8,128)(2,1)}, bf16[2048,2048]{1,0:T(8,128)(2,1)},...) custom-call(bf16[2,256,2048]{2,1,0:T(8,128)(2,1)} %get-tuple-element, ...), custom_call_target="tpu_custom_call" | custom-call | flops 99999997952 | bytes 100000000 | tf_op jit(solution)/shard_map/pallas_call | solution.py:541
  311.5 1.4 slice.85
  313.0 265.4 %shard_map.255 = (bf16[2,256,2048]{2,1,0:T(8,128)(2,1)}, bf16[2048,2048]{1,0:T(8,128)(2,1)}, f32[1024,512]{1,0:T(8,128)}, bf16[8,512,1024]{2,1,0:T(8,128)(2,1)},...) custom-call(bf16[2048,2048]{1,0:T(8,128)(2,1)} %get-tuple-element.41, ...), custom_call_target="tpu_custom_call" | custom-call | flops 99999997952 | bytes 100000000 | tf_op jit(solution)/shard_map/pallas_call | solution.py:1234
  578.4 0.7 fusion.37
  579.1 5.8 collective-permute-start.14
  585.0 13.7 %collective-permute-start.9 = (f32[4,2048]{1,0:T(4,128)}, f32[4,2048]{1,0:T(4,128)S(1)}, u32[]{:S(2)}, u32[]{:S(2)}) collective-permute-start(f32[4,2048]{1,0:T(4,128)} %get-tuple-element.64), channel_id=1, source_target_pairs={{0,1},{1,0},{2,3},{3,2},{4,5},{5,4},{6,7},{7,6},{8,9},{9,8},{10,11... | collective-permute-start | bytes 98312 | tf_op jit(solution)/shard_map/ppermute | solution.py:44
  598.6 246.9 %shard_map.256 = (f32[512,768]{1,0:T(8,128)}, f32[256,512]{1,0:T(8,128)}, f32[512,1024]{1,0:T(8,128)}, bf16[2,256,2048]{2,1,0:T(8,128)(2,1)}, bf16[3,256,2048]{2...) custom-call(bf16[2048,1536]{1,0:T(8,128)(2,1)} %get-tuple-element.49, ...), custom_call_target="tpu_custom_call" | custom-call | flops 99999997952 | bytes 100000000 | tf_op jit(solution)/shard_map/pallas_call | solution.py:1290
  845.6 0.8 reshape.112
  846.4 0.1 collective-permute-start.5
  846.5 3.0 collective-permute-start.6
  849.5 2.2 fusion.12
  851.7 0.0 copy-start.1
  851.8 3.2 fusion.32
  855.1 0.2 copy-done.7
  855.3 3.4 fusion.11
  858.7 0.1 collective-permute-start
  858.8 0.0 copy-start.5
  858.8 1.8 fusion.33
  860.7 0.4 copy-done.5
  861.0 0.6 copy-done.8
  861.7 4.0 fusion.29
  865.7 1.6 maximum_select_fusion
  867.3 7.2 collective-permute-start.1
  874.5 1.5 collective-permute-start.7
  876.1 0.2 collective-permute-start.10
  876.2 0.0 collective-permute-done.1
  876.3 2.9 collective-permute-start.2
  879.3 1.6 collective-permute-start.8
  880.8 0.5 collective-permute-start.15
  881.4 1.6 collective-permute-start.3
  882.9 2.6 collective-permute-start.11
  885.5 1.6 maximum_select_fusion.1
  887.2 0.1 copy-done.11
  887.3 0.5 copy.33
  887.8 1.6 copy.34
  889.4 0.5 collective-permute-start.16
  889.9 1.6 collective-permute-start.4
  891.5 0.6 collective-permute-start.12
  892.1 0.6 fusion.40
  892.7 0.3 collective-permute-done.16
  893.0 0.6 add.138
  893.6 0.1 collective-permute-done.4
  893.7 1.7 collective-permute-done.12
  895.5 0.6 collective-permute-start.13
  896.1 0.6 fusion.36
  896.7 2.8 collective-permute-done.13
  899.5 0.6 fusion.34
  900.1 0.8 copy.38
  900.9 3.3 copy.39
  904.2 1.3 copy.40
  (83 shorter events, 0.4 us)
Async XLA Ops:
  2.6 2.6 copy-start.9
  5.2 5.9 copy-start
  5.2 5.9 copy-start.2
  5.2 1.3 copy-start.25
  11.1 3.7 copy-start.24
  11.1 3.7 copy-start.14
  11.1 3.7 copy-start.17
  11.1 3.7 copy-start.18
  11.1 3.7 copy-start.19
  11.1 3.7 copy-start.20
  11.1 3.7 copy-start.21
  579.1 301.7 %collective-permute-start.14 = (f32[1024]{0:T(1024)S(1)}, f32[1024]{0:T(1024)S(1)}, u32[]{:S(2)}, u32[]{:S(2)}) collective-permute-start(f32[1024]{0:T(1024)S(1)} %bitcast.152), channel_id=1, source_target_pairs={{0,4},{4,0},{1,5},{5,1},{2,6},{6,2},{3,7},{7,3},{8,12},{12,8},{9,1... | collective-permute-start | bytes 12296 | tf_op jit(solution)/shard_map/ppermute | solution.py:53
  585.0 291.1 %collective-permute-start.9 = (f32[4,2048]{1,0:T(4,128)}, f32[4,2048]{1,0:T(4,128)S(1)}, u32[]{:S(2)}, u32[]{:S(2)}) collective-permute-start(f32[4,2048]{1,0:T(4,128)} %get-tuple-element.64), channel_id=1, source_target_pairs={{0,1},{1,0},{2,3},{3,2},{4,5},{5,4},{6,7},{7,6},{8,9},{9,8},{10,11... | collective-permute-start | bytes 98312 | tf_op jit(solution)/shard_map/ppermute | solution.py:44
  598.6 250.8 %copy-start.23 = (f32[256]{0:T(256)S(1)}, f32[256]{0:T(256)}, u32[]{:S(2)}) copy-start(f32[256]{0:T(256)} %get-tuple-element.115) | copy-start | bytes 3076
  598.6 250.8 %copy-start.22 = (f32[256]{0:T(256)S(1)}, f32[256]{0:T(256)}, u32[]{:S(2)}) copy-start(f32[256]{0:T(256)} %get-tuple-element.104) | copy-start | bytes 3076
  845.6 6.2 copy-start.12
  846.4 20.9 %collective-permute-start.5 = (f32[256]{0:T(256)S(1)}, f32[256]{0:T(256)S(1)}, u32[]{:S(2)}, u32[]{:S(2)}) collective-permute-start(f32[256]{0:T(256)S(1)} %bitcast.155), channel_id=1, source_target_pairs={{0,4},{4,0},{1,5},{5,1},{2,6},{6,2},{3,7},{7,3},{8,12},{12,8},{9,1... | collective-permute-start | bytes 3080 | tf_op jit(solution)/shard_map/ppermute | solution.py:53
  846.5 20.8 %collective-permute-start.6 = (f32[256]{0:T(256)S(1)}, f32[256]{0:T(256)S(1)}, u32[]{:S(2)}, u32[]{:S(2)}) collective-permute-start(f32[256]{0:T(256)S(1)} %bitcast.156), channel_id=1, source_target_pairs={{0,4},{4,0},{1,5},{5,1},{2,6},{6,2},{3,7},{7,3},{8,12},{12,8},{9,1... | collective-permute-start | bytes 3080 | tf_op jit(solution)/shard_map/ppermute | solution.py:53
  851.7 3.3 copy-start.1
  851.8 3.3 copy-start.3
  851.8 3.5 copy-start.7
  851.8 3.5 copy-start.15
  855.0 3.6 copy-start.4
  858.7 8.6 collective-permute-start
  858.8 2.2 copy-start.5
  858.8 2.8 copy-start.8
  861.7 4.0 copy-start.6
  865.7 10.4 %copy-start.16 = (f32[4,2048]{1,0:T(4,128)S(1)}, f32[4,2048]{1,0:T(4,128)}, u32[]{:S(2)}) copy-start(f32[4,2048]{1,0:T(4,128)} %get-tuple-element.64) | copy-start | bytes 98308
  867.3 8.9 collective-permute-start.1
  874.5 4.7 collective-permute-start.7
  876.1 6.9 collective-permute-start.10
  876.3 5.1 collective-permute-start.2
  879.3 12.9 %collective-permute-start.8 = (f32[2,256]{1,0:T(2,128)S(1)}, f32[2,256]{1,0:T(2,128)S(1)}, u32[]{:S(2)}, u32[]{:S(2)}) collective-permute-start(f32[2,256]{1,0:T(2,128)S(1)} %fusion.31), channel_id=1, source_target_pairs={{0,8},{8,0},{1,9},{9,1},{2,10},{10,2},{3,11},{11,3},{4,12},{12,4},... | collective-permute-start | bytes 6152 | tf_op jit(solution)/shard_map/ppermute | solution.py:44
  880.8 8.6 collective-permute-start.15
  881.4 8.5 collective-permute-start.3
  882.9 8.5 collective-permute-start.11
  885.5 1.7 copy-start.11
  887.8 12.4 %copy-start.13 = (f32[256,512]{1,0:T(8,128)S(1)}, f32[256,512]{1,0:T(8,128)}, u32[]{:S(2)}) copy-start(f32[256,512]{1,0:T(8,128)} %get-tuple-element.158) | copy-start | bytes 1572868
  889.4 3.6 collective-permute-start.16
  889.9 3.8 collective-permute-start.4
  891.5 4.0 collective-permute-start.12
  895.5 4.0 collective-permute-start.13
  900.9 3.3 copy-start.10

commit v4 on v3

--- a/solution.py
+++ b/solution.py
@@ -40,27 +40,6 @@
     )
 
 
-def flip(x, axis):
-    return lax.ppermute(x, axis, [(0, 1), (1, 0)])
-
-
-def turn(x, groups, by, axes=("e", "g")):
-    extra, count = groups
-    pairs = []
-    for e in range(extra):
-        for g in range(count):
-            pairs.append((e * count + g, (e + by[0]) % extra * count + (g + by[1]) % count))
-    return lax.ppermute(x, axes, pairs)
-
-
-def sum_axis(x, axis):
-    if lax.axis_size(axis) == 1:
-        return x
-    if lax.axis_size(axis) == 2:
-        return x + flip(x, axis)
-    return jnp.sum(lax.all_gather(x, axis), 0)
-
-
 def row_blocks(place, count, size):
     found = []
     for j in range(count):
@@ -80,6 +59,31 @@
     return 0 if segment is None else block * size // segment * segment
 
 
+class Remote:
+    def __init__(self, copies, number, source, target, device):
+        self.copies, self.number, self.source, self.target = copies, number, source, target
+        self.device = device
+
+    def _copy(self):
+        return pltpu.make_async_remote_copy(
+            src_ref=self.source,
+            dst_ref=self.target,
+            send_sem=self.copies.send.at[self.number],
+            recv_sem=self.copies.recv.at[self.number],
+            device_id=self.device,
+            device_id_type=pl.DeviceIdType.MESH,
+        )
+
+    def start(self):
+        self._copy().start()
+
+    def wait_send(self):
+        self._copy().wait_send()
+
+    def wait_recv(self):
+        self._copy().wait_recv()
+
+
 class Copies:
     def __init__(self, send, recv, near):
         self.send, self.recv, self.near = send, recv, near
@@ -87,14 +91,7 @@
         self.open_sends, self.open_locals = [], []
 
     def remote(self, source, target, device, tracked=True):
-        copy = pltpu.make_async_remote_copy(
-            src_ref=source,
-            dst_ref=target,
-            send_sem=self.send.at[self.remotes],
-            recv_sem=self.recv.at[self.remotes],
-            device_id=device,
-            device_id_type=pl.DeviceIdType.MESH,
-        )
+        copy = Remote(self, self.remotes, source, target, device)
         self.remotes += 1
         if tracked:
             copy.start()
@@ -212,9 +209,9 @@
 
 def layer_forward(extra, groups, quarter, *refs):
     (
-        rows_ref, in_ref, out_ref, up_ref, down_ref, wide_ref, bias_ref, cots_ref,
+        rows_ref, in_ref, out_ref, up_ref, down_ref, wide_ref, bias_ref,
         in_all, out_all, up_all, down_all, bias_all, full1, prefix1, proj_out, prefix_out, att_out,
-        lse_out, resid_out, full2, full_cot,
+        lse_out, resid_out, full2,
         in_here, out_here, norm_here, prefix_here, proj, prefix_proj, att, lse, c_send, c_recv, h_send,
         h_recv, resid, normed2, k_own, v_own, send_sem, recv_sem, near_sem,
     ) = refs
@@ -388,16 +385,13 @@
         if n and o[0] == 0
     ]
     bias_here[0] = bias_ref[...]
+    first_norm(1)
+    spread = [None, spread_to(norm_here.at[pl.ds(length, size), :], norm_here, length)]
     first_norm(0)
-    spread = [spread_to(norm_here.at[pl.ds(0, size), :], norm_here, 0), None]
-    first_norm(1)
-    spread[1] = spread_to(norm_here.at[pl.ds(length, size), :], norm_here, length)
     w_in.second(False)
     w_out.own()
+    w_in.turned()
     w_out.turn()
-    spread[0].forward()
-    w_out.second(False)
-    w_in.turned()
 
     before, later = [], []
     for k in range(1, groups):
@@ -436,52 +430,49 @@
         def _():
             in_tiles(length, size, lambda t: clear((k - 1) * length + t))
 
+    w_out.second(False)
     spread[1].forward()
+    spread[0] = spread_to(norm_here.at[pl.ds(0, size), :], norm_here, 0)
     w_in.second(True)
     w_in.finish(False)
     w_in.finish(True)
     w_up.own()
-    w_out.turned()
     copies.local(in_here, in_all)
     for copy in bias_steps:
         copy.wait_recv()
-    spread_cot = []
-    for r in range(2):
-        copies.local(cots_ref.at[r], full_cot.at[pl.ds(r * length, size), :])
-        spread_cot.append(spread_to(cots_ref.at[r], full_cot, r * length))
     spread[1].finish()
     project(norm_here, length, proj, length, 0)
+    w_out.turned()
+    spread[0].forward()
+    attention(1, quarter)
     w_out.second(True)
-    attention(1, quarter)
+    w_up.second(False)
     spread[0].finish()
     copies.local(norm_here, full1)
-    w_up.second(False)
+    project(norm_here, 0, proj, 0, 0)
+    copies.local(proj, proj_out)
+    for_prefix(prefix_came)
+    w_up.turn()
     w_out.finish(False)
     w_out.finish(True)
     copies.local(out_here, out_all)
+    w_down.own()
     out_product(1)
-    w_down.own()
-    for_prefix(prefix_came)
-    w_up.turn()
-    project(norm_here, 0, proj, 0, 0)
-    copies.local(proj, proj_out)
     out_sum(1)
     for_prefix(prefix_forward)
     w_down.second(False)
-    spread_cot[0].forward()
-    spread_cot[1].forward()
     for_prefix(prefix_finish)
     for k in range(1, groups):
         project(prefix_here, (k - 1) * length, prefix_proj, (k - 1) * length, 1)
     copies.local(prefix_here, prefix1)
     copies.local(prefix_proj, prefix_out)
+    w_down.turn()
     spread2 = [None, second_norm(1)]
-    w_down.turn()
     attention(0, None)
+    w_up.turned()
     copies.local(att, att_out)
     copies.local(lse, lse_out)
     out_product(0)
-    w_up.turned()
     out_sum(0)
     spread2[1].forward()
     w_up.second(True)
@@ -494,8 +485,6 @@
     w_down.finish(False)
     spread2[1].finish()
     spread2[0].finish()
-    spread_cot[0].finish()
-    spread_cot[1].finish()
     w_down.finish(True)
 
     for k in range(1, groups):
@@ -511,7 +500,7 @@
     copies.finish()
 
 
-def run_forward(split, quarter, rows, in_w, out_w, up_w, down_w, wide, bias, cots):
+def run_forward(split, quarter, rows, in_w, out_w, up_w, down_w, wide, bias):
     extra, groups = split
     size, width = rows.shape[1:]
     length = 4 * size
@@ -536,11 +525,10 @@
         shape((2 * heads, 1, length), F32),
         shape((2, size, width), F32),
         shape((2 * length, width), BF16),
-        shape((2 * length, width), BF16),
     ]
     return pl.pallas_call(
         functools.partial(layer_forward, extra, groups, quarter),
-        in_specs=[inside] + [anywhere] * 4 + [inside] * 2 + [anywhere],
+        in_specs=[inside] + [anywhere] * 4 + [inside] * 2,
         out_specs=[inside if n == 4 else anywhere for n in range(len(out_shape))],
         out_shape=out_shape,
         scratch_shapes=[
@@ -566,7 +554,7 @@
         ],
         compiler_params=kernel_params(0),
         cost_estimate=pl.CostEstimate(flops=10**11, bytes_accessed=10**8, transcendentals=10**7),
-    )(rows, in_w, out_w, up_w, down_w, wide, bias, cots)
+    )(rows, in_w, out_w, up_w, down_w, wide, bias)
 
 
 class GradScatter:
@@ -576,6 +564,9 @@
         self.fetched, self.out = fetched, out
         self.half, self.cols = land.shape[2:]
         self.steps = {}
+        numbers = range(len(places.offsets))
+        self.land_at = {(n, k): land.at[n, k] for n in numbers for k in range(6)}
+        self.work_at = {(n, k): work.at[n, k] for n in numbers for k in range(2)}
 
     def piece(self, n, i, j, part):
         places = self.places
@@ -584,54 +575,108 @@
         return self.parts.at[index, pl.ds(part * self.half, self.half), :]
 
     def _send(self, n, key, source, partner):
-        self.steps[n, key] = self.copies.remote(source, self.land.at[n, key], partner)
+        self.steps[n, key] = self.copies.remote(source, self.land_at[n, key], partner)
+
+    ORDER = ((1, 1), (0, 1), (1, 0), (0, 0))
+
+    def index(self, n, i, j):
+        places = self.places
+        return places.offsets[n][1] * places.extra * 4 + places.share(places.offsets[n], i, j)
+
+    def send(self, n, i, j):
+        to_a, to_b = self.places.to_a, self.places.to_b
+        if (i, j) == (1, 1):
+            self._send(n, 0, self.piece(n, 1, 1, 0), to_a)
+            self._send(n, 1, self.piece(n, 1, 1, 1), to_b)
+        elif (i, j) == (0, 1):
+            self._send(n, 2, self.piece(n, 0, 1, 0), to_a)
+        elif (i, j) == (1, 0):
+            self._send(n, 3, self.piece(n, 1, 0, 1), to_b)
 
     def start(self, n):
-        to_a, to_b = self.places.to_a, self.places.to_b
-        self._send(n, 0, self.piece(n, 1, 1, 0), to_a)
-        self._send(n, 1, self.piece(n, 1, 1, 1), to_b)
-        self._send(n, 2, self.piece(n, 0, 1, 0), to_a)
-        self._send(n, 3, self.piece(n, 1, 0, 1), to_b)
-
-    def _fetch(self, sources):
-        got = [self.fetched.at[m, : self.half, : self.cols] for m in range(len(sources))]
-        loads = [self.copies.local(s, t, tracked=False) for s, t in zip(sources, got)]
-        for load in loads:
-            load.wait()
-        return functools.reduce(jnp.add, [t[...].astype(F32) for t in got])
-
-    def middle(self, n):
-        self.steps[n, 0].wait_recv()
-        self.work[n, 0] = self._fetch([self.land.at[n, 0], self.piece(n, 1, 0, 0)]).astype(BF16)
-        self._send(n, 5, self.work.at[n, 0], self.places.to_b)
-        self.steps[n, 1].wait_recv()
-        self.work[n, 1] = self._fetch([self.land.at[n, 1], self.piece(n, 0, 1, 1)]).astype(BF16)
-        self._send(n, 4, self.work.at[n, 1], self.places.to_a)
-
-    def last(self, n):
-        for part, keys in ((0, (2, 5)), (1, (3, 4))):
-            for key in keys:
-                self.steps[n, key].wait_recv()
-            summed = self._fetch([self.piece(n, 0, 0, part)] + [self.land.at[n, k] for k in keys])
-            rows = slice(part * self.half, (part + 1) * self.half)
-            if n == 0:
-                self.out[rows, :] = summed
-            else:
-                self.own[n - 1, rows, :] = summed.astype(BF16)
-        if n:
-            e, g = self.places.offsets[n]
-            self.steps[n, "t"] = self.copies.remote(
-                self.own.at[n - 1], self.turned.at[n - 1], self.places.further((-e, -g))
-            )
+        for i, j in self.ORDER:
+            self.send(n, i, j)
+
+    def _run(self, jobs):
+        before = None
+        for m, (waits, sources, finish) in enumerate(jobs):
+            for copy in waits:
+                copy.wait_recv()
+            slots = [
+                self.fetched.at[m % 2, k, : self.half, : self.cols] for k in range(len(sources))
+            ]
+            loads = [self.copies.local(s, t, tracked=False) for s, t in zip(sources, slots)]
+            if before is not None:
+                before()
+
+            def after(loads=loads, slots=slots, finish=finish):
+                for load in loads:
+                    load.wait()
+                finish(functools.reduce(jnp.add, [t[...].astype(F32) for t in slots]))
+
+            before = after
+        if before is not None:
+            before()
+
+    def middle(self, *numbers):
+        jobs = []
+        for n in numbers:
+            for key, target, partner, arrived, piece in (
+                (5, 0, self.places.to_b, 0, self.piece(n, 1, 0, 0)),
+                (4, 1, self.places.to_a, 1, self.piece(n, 0, 1, 1)),
+            ):
+
+                def finish(summed, n=n, key=key, target=target, partner=partner):
+                    self.work[n, target] = summed.astype(BF16)
+                    self._send(n, key, self.work_at[n, target], partner)
+
+                jobs.append(([self.steps[n, arrived]], [self.land.at[n, arrived], piece], finish))
+        self._run(jobs)
+
+    def last(self, *numbers):
+        jobs = []
+        for n in numbers:
+            for part, keys in ((0, (2, 5)), (1, (3, 4))):
+
+                def finish(summed, n=n, part=part):
+                    rows = slice(part * self.half, (part + 1) * self.half)
+                    if n == 0:
+                        self.out[rows, :] = summed
+                        return
+                    self.own[n - 1, rows, :] = summed.astype(BF16)
+                    if part == 1:
+                        e, g = self.places.offsets[n]
+                        self.steps[n, "t"] = self.copies.remote(
+                            self.own.at[n - 1],
+                            self.turned.at[n - 1],
+                            self.places.further((-e, -g)),
+                        )
+
+                jobs.append(
+                    (
+                        [self.steps[n, k] for k in keys],
+                        [self.piece(n, 0, 0, part)] + [self.land.at[n, k] for k in keys],
+                        finish,
+                    )
+                )
+        self._run(jobs)
 
     def total(self):
+        jobs = []
         for n in range(1, len(self.places.offsets)):
-            self.steps[n, "t"].wait_recv()
             for part in range(2):
-                rows = slice(part * self.half, (part + 1) * self.half)
-                self.out[rows, :] += self._fetch(
-                    [self.turned.at[n - 1, pl.ds(part * self.half, self.half), :]]
+
+                def finish(summed, part=part):
+                    self.out[part * self.half : (part + 1) * self.half, :] += summed
+
+                jobs.append(
+                    (
+                        [] if part else [self.steps[n, "t"]],
+                        [self.turned.at[n - 1, pl.ds(part * self.half, self.half), :]],
+                        finish,
+                    )
                 )
+        self._run(jobs)
 
     @staticmethod
     def landing(sources, rows, cols):
@@ -652,7 +697,7 @@
     def __init__(self, copies, places, c_send, c_recv, h_send, free, size):
         self.copies, self.places, self.size = copies, places, size
         self.c_send, self.c_recv, self.h_send, self.free = c_send, c_recv, h_send, free
-        self.core = self.far = None
+        self.core, self.count, self.far = None, 0, {}
 
     def away(self, block):
         if self.core is not None:
@@ -663,31 +708,47 @@
             pl.semaphore_wait(self.free, 1)
         self.core = self.copies.remote(self.c_send, self.c_recv, self.places.to_c)
 
-    def kept(self, block, target, h_recv, more):
-        size = self.size
-        far = block(1)
+    def kept(self, block, target, more, h_recv=None, far_out=None):
+        size, turn = self.size, self.count % len(self.h_send)
+        self.count += 1
+        h_send = self.h_send[turn]
+        if turn in self.far:
+            self.far.pop(turn)()
+        h_send[...] = block(1).astype(BF16)
+        target[...] = block(0).astype(BF16)
         self.core.wait_recv()
-        if self.far is not None:
-            self.copies.sent(self.far)
-        self.h_send[...] = (far + self.c_recv[size:, :].astype(F32)).astype(BF16)
-        self.far = self.copies.remote(self.h_send, h_recv, self.places.to_h)
-        target[...] = (block(0) + self.c_recv[:size, :].astype(F32)).astype(target.dtype)
+        h_send[...] = (h_send[...].astype(F32) + self.c_recv[size:, :].astype(F32)).astype(BF16)
+        if far_out is None:
+            copy = self.copies.remote(h_send, h_recv, self.places.to_h)
+            self.far[turn] = functools.partial(self.copies.sent, copy)
+        else:
+            copy = self.copies.local(h_send, far_out, tracked=False)
+            self.far[turn] = copy.wait
+        target[...] = (target[...].astype(F32) + self.c_recv[:size, :].astype(F32)).astype(BF16)
         if more:
             pl.semaphore_signal(
                 self.free, inc=1, device_id=self.places.to_c, device_id_type=pl.DeviceIdType.MESH
             )
-        return self.far
+        return copy
+
+    def finish(self):
+        for wait in self.far.values():
+            wait()
+        self.copies.sent(self.core)
 
 
 class Stream:
-    def __init__(self, copies, slots, blocks):
+    def __init__(self, copies, slots, blocks, ready=None):
         self.copies, self.slots, self.blocks = copies, slots, blocks
+        self.ready = ready
         self.loads = {}
         self._load(0)
 
     def _load(self, n):
         if n < len(self.blocks):
             targets = [s[n % 2] for s in self.slots]
+            if self.ready is not None:
+                self.ready(n)
             self.loads[n] = [
                 self.copies.local(s, t, tracked=False) for s, t in zip(self.blocks[n], targets)
             ]
@@ -719,8 +780,9 @@
 
 def middle_kernel(extra, groups, *refs):
     (
-        full2, full_cot, up_all, down_all, resid, wide, bias_up,
-        mixed, full_dres, grad_down, up_parts, sums, up_sums, act, dup, down_parts, land, turned,
+        full2, own_cots, up_all, down_all, resid, wide, bias_up,
+        mixed, full_dres, grad_down, up_parts, sums, up_sums, mixed_far, full_cot, act, dup, down_parts,
+        land, turned,
         big, down, narrow, tiles, cots, c_send, c_recv, h_send, h_recv, low, stage_down, work, own,
         fetched, send_sem, recv_sem, near_sem, free,
     ) = refs
@@ -736,7 +798,7 @@
     scatter = GradScatter(
         copies, places, down_parts, land, turned, work, own, fetched, grad_down
     )
-    fold = Fold(copies, places, c_send, c_recv, h_send, free, size)
+    fold = Fold(copies, places, c_send, c_recv, [h_send.at[0], h_send.at[1]], free, size)
     folded = {}
 
     def load(source, target):
@@ -749,12 +811,29 @@
     tile_slots = [tiles.at[0], tiles.at[1]]
     cot_slots = [cots.at[0], cots.at[1]]
     narrow_slots = [narrow.at[0], narrow.at[1]]
-    order = [(r, slot) for r in range(2) for slot in (2, 3, 1, 0)]
+    order = [(r, slot) for slot in (0, 2, 1, 3) for r in range(2)]
     where = [pl.ds(r * length + s * size, size) for r, s in order]
+    places.barrier()
+    spread_cot = []
+    for r in range(2):
+        copies.local(own_cots.at[r], full_cot.at[pl.ds(r * length, size), :], tracked=False).wait()
+        spread_cot.append(Spread(copies, places, own_cots.at[r], full_cot, r * length, size))
+
+    def cot_ready(n):
+        r, slot = order[n]
+        if slot == 1:
+            spread_cot[r].forward()
+        elif slot == 2:
+            spread_cot[r].core.wait_recv()
+        elif slot == 3:
+            spread_cot[r].last.wait_recv()
+
     stream = Stream(
-        copies, [tile_slots, cot_slots], [[full2.at[w, :], full_cot.at[w, :]] for w in where]
+        copies,
+        [tile_slots, cot_slots],
+        [[full2.at[w, :], full_cot.at[w, :]] for w in where],
+        cot_ready,
     )
-    places.barrier()
     sums[...] = jnp.zeros_like(sums)
     up_sums[...] = jnp.zeros_like(up_sums)
     for copy in loading:
@@ -792,19 +871,24 @@
         for copy in stored.pop(n):
             copy.wait()
 
-    own_cots = [load(full_cot.at[pl.ds(r * length, size), :], cots.at[r]) for r in range(2)]
-    stream_dup = Stream(copies, [tile_slots], [[dup.at[w, :]] for w in where])
+    here_cots = [load(own_cots.at[r], cots.at[r]) for r in range(2)]
+    dup_order = [(r, slot) for r in range(2) for slot in (2, 3, 1, 0)]
+    stream_dup = Stream(
+        copies,
+        [tile_slots],
+        [[dup.at[pl.ds(r * length + s * size, size), :]] for r, s in dup_order],
+    )
 
     def dup_block(r):
         def block(slot):
-            at = stream_dup.take(order.index((r, slot)))
+            at = stream_dup.take(dup_order.index((r, slot)))
             return dot(tiles[at], big[:width], ((1,), (1,)))
 
         return block
 
     for r in range(2):
         fold.away(dup_block(r))
-        folded[r] = fold.kept(dup_block(r), low.at[r], h_recv.at[r], True)
+        folded[r] = fold.kept(dup_block(r), low.at[r], True, h_recv.at[r])
 
     def norm_back_rows(r):
         folded[r].wait_recv()
@@ -829,47 +913,53 @@
         ]
 
     turn_order = list(range(groups))[::-1]
+
+    def of_group(g):
+        return [n for n in range(sources) if places.offsets[n][1] == g][::-1]
+
+    wanted = [(n, i, j) for g in turn_order for n in of_group(g) for i, j in GradScatter.ORDER]
+
+    def wanted_columns(source):
+        found = []
+        for n, i, j in wanted:
+            share = places.share(places.offsets[n], i, j)
+            found.append([source.at[:, pl.ds(pl.multiple_of(share * depth, depth), depth)]])
+        return found
+
     loading = load_big(act)
-    stream_cot = Stream(copies, [narrow_slots], columns_of(full_cot))
+    stream_cot = Stream(copies, [narrow_slots], wanted_columns(full_cot))
     loading.wait()
-    for copy in own_cots:
+    for copy in here_cots:
         copy.wait()
     put = {}
-    count = 0
     spread = [None, None]
 
-    def down_grad(g):
-        nonlocal count
-        for d in range(shares):
-            at = stream_cot.take(count)
-            slot = count % 2
-            if count - 2 in put:
-                put.pop(count - 2).wait()
-
-            def body(t):
-                left = big[: 2 * length, pl.ds(pl.multiple_of(g * hidden + t, HDIM), hidden // 2)]
-                stage_down[slot, pl.ds(t, hidden // 2), :] = dot(
-                    left, narrow[at], ((0,), (0,))
-                ).astype(BF16)
-
-            in_tiles(hidden, hidden // 2, body)
-            put[count] = load(stage_down.at[slot], down_parts.at[g * shares + d])
-            count += 1
-
-    def of_group(g):
-        return [n for n in range(sources) if places.offsets[n][1] == g][::-1]
-
-    for step, g in enumerate(turn_order):
-        down_grad(g)
-        for n in list(put):
-            put.pop(n).wait()
-        for n in of_group(g):
-            scatter.start(n)
-        if step == 0:
+    def settle(number):
+        if number in put:
+            put.pop(number).wait()
+            scatter.send(*wanted[number])
+
+    for number, (n, i, j) in enumerate(wanted):
+        at = stream_cot.take(number)
+        slot = number % 2
+        first = places.offsets[n][1] * hidden
+
+        def body(t):
+            left = big[: 2 * length, pl.ds(pl.multiple_of(first + t, HDIM), hidden // 2)]
+            stage_down[slot, pl.ds(t, hidden // 2), :] = dot(
+                left, narrow[at], ((0,), (0,))
+            ).astype(BF16)
+
+        in_tiles(hidden, hidden // 2, body)
+        put[number] = load(stage_down.at[slot], down_parts.at[scatter.index(n, i, j)])
+        settle(number - 1)
+        if number == 4 * extra - 1:
+            settle(number)
             spread[0] = norm_back_rows(0)
+            scatter.middle(*of_group(turn_order[0]))
+    settle(len(wanted) - 1)
     spread[1] = norm_back_rows(1)
-    for n in of_group(turn_order[0]):
-        scatter.middle(n)
+    scatter.last(*[n for n in of_group(turn_order[0]) if n])
 
     def act_block(r):
         def block(slot):
@@ -879,15 +969,10 @@
 
     for r in range(2):
         fold.away(act_block(r))
-        folded[2 + r] = fold.kept(act_block(r), mixed.at[r], h_recv.at[2 + r], r == 0)
+        fold.kept(act_block(r), mixed.at[r], r == 0, far_out=mixed_far.at[r])
         spread[r].forward()
         if r == 0:
-            for g in turn_order[1:]:
-                for n in of_group(g):
-                    scatter.middle(n)
-    for n in of_group(turn_order[0]):
-        if n:
-            scatter.last(n)
+            scatter.middle(*[n for g in turn_order[1:] for n in of_group(g)])
 
     loading = load_big(dup)
     stream_two = Stream(copies, [narrow_slots], columns_of(full2))
@@ -905,32 +990,17 @@
             ).astype(BF16)
             put_up[done] = load(stage_up[done % 2], up_parts.at[g * shares + d])
             done += 1
-    for r in range(2):
-        folded[2 + r].wait_recv()
-
-        def add(t):
-            rows = pl.ds(t, chunk)
-            mixed[r, rows, :] = (
-                resid[r, rows, :]
-                + mixed[r, rows, :].astype(F32)
-                + h_recv[2 + r, rows, :].astype(F32)
-                + wide[5:6]
-            ).astype(BF16)
-
-        in_tiles(size, chunk, add)
     for copy in put_up.values():
         copy.wait()
     spread[0].finish()
     spread[1].finish()
-    for g in turn_order:
-        for n in of_group(g):
-            if (n, "t") not in scatter.steps:
-                scatter.last(n)
+    scatter.last(*[n for g in turn_order for n in of_group(g) if (n, "t") not in scatter.steps])
     scatter.total()
+    fold.finish()
     copies.finish()
 
 
-def attention_back_rows(places, row, length, size, heads, per, segment, refs, column):
+def attention_back_rows(places, row, length, size, heads, per, segment, refs, column, pump=None):
     (
         proj, prefix_proj, att, datt, lse, dproj, dprefix,
         k_own, v_own, dk_own, dv_own, dk_pre, dv_pre,
@@ -1004,6 +1074,8 @@
             there = pl.ds(base + at[j], size)
             dproj[there, k_at] = (dk_own[rows] * factor).astype(BF16)
             dproj[there, v_at] = dv_own[rows].astype(BF16)
+        if pump is not None:
+            pl.when(n == heads // 2 - 1)(pump)
         return 0
 
     lax.fori_loop(0, heads, head, 0)
@@ -1011,12 +1083,14 @@
 
 def last_kernel(extra, groups, quarter, *refs):
     (
-        proj_in, prefix_in, att_in, full_dres, out_all, in_all, full1, prefix1, up_parts, lse,
-        grad_in, grad_out, grad_up, dnormed1, h_recv, returned, dproj_sums,
+        proj_in, prefix_in, att_in, full_dres, out_all, in_all, full1, prefix1, up_parts, mixed_far, rows_in,
+        lse, wide_ref, sums2, up_sums,
+        grad_in, grad_out, grad_up, dnormed1, all_sums, bias_sums, mixed_recv,
         in_parts, out_parts, land_in, turned_in, land_out, turned_out, land_up, turned_up,
         proj, prefix_proj, att, datt, dprefix, w_in, w_out, spare,
         k_own, v_own, dk_own, dv_own, dk_pre, dv_pre,
-        c_send, c_recv, h_send, back, stage_in, stage_out,
+        c_send, c_recv, h_send, h_recv, back, returned, dproj_sums, sum_send, sum_recv, bias_send, bias_recv,
+        bias_out, bias_turn, stage_in, stage_out,
         work_in, own_in, work_out, own_out, work_up, own_up, fetched, send_sem, recv_sem, near_sem, free,
     ) = refs
     size, width = dnormed1.shape[1:]
@@ -1041,7 +1115,7 @@
         copies, places, in_parts, land_in, turned_in, work_in, own_in, fetched, grad_in
     )
     dproj = proj
-    folds = Fold(copies, places, c_send, c_recv, h_send, free, size)
+    folds = Fold(copies, places, c_send, c_recv, [h_send.at[0], h_send.at[1]], free, size)
     folded = {}
 
     def column(n, parts, m):
@@ -1061,6 +1135,9 @@
     places.barrier()
     for n in far_first:
         up.start(n)
+    mixed_steps = [
+        copies.remote(mixed_far.at[r], mixed_recv.at[r], places.to_h) for r in range(2)
+    ]
     for copy in here:
         copy.wait()
 
@@ -1071,7 +1148,7 @@
                 tiles[at][...], w_out[...], ((1,), (1,))
             ).astype(BF16)
 
-    def attention_back(r, segment):
+    def attention_back(r, segment, pump=None):
         attention_back_rows(
             places, r, length, size, heads, per, segment,
             (
@@ -1079,6 +1156,7 @@
                 k_own, v_own, dk_own, dv_own, dk_pre, dv_pre,
             ),
             column,
+            pump,
         )
 
     def block_of(source, row):
@@ -1090,18 +1168,15 @@
 
     def fold(number, source, row, target, more=True):
         folds.away(block_of(source, row))
-        folded[number] = folds.kept(block_of(source, row), target, h_recv.at[number], more)
+        folded[number] = folds.kept(block_of(source, row), target, more, h_recv.at[number])
 
     attended_grad(0)
     attended_grad(1)
-    attention_back(0, None)
-    for n in far_first:
-        up.middle(n)
+    attention_back(0, None, lambda: up.middle(*far_first))
+    up.last(*far_first[:-1])
     for k in range(1, groups):
         fold(1 + k, dprefix, (k - 1) * length, back.at[k - 1])
     attention_back(1, quarter)
-    for n in far_first:
-        up.last(n)
 
     home = []
     for k in range(1, groups):
@@ -1117,17 +1192,19 @@
     prefix_rows = prefix1.shape[0]
     slots_pre = [prefix_proj.at[:, pl.ds(n * depth, depth)] for n in range(2)]
 
+    def share_of(n, i, j):
+        return places.share(places.offsets[n], i, j)
+
     class Columns:
-        def __init__(self, sources_and_slots, count):
-            self.pairs, self.count, self.loads = sources_and_slots, count, {}
+        def __init__(self, pairs, shares_at):
+            self.pairs, self.shares_at, self.loads = pairs, shares_at, {}
             self._load(0)
 
         def _load(self, n):
-            if n < self.count:
-                d = n % shares
+            if n < len(self.shares_at):
+                at = pl.ds(pl.multiple_of(self.shares_at[n] * depth, depth), depth)
                 self.loads[n] = [
-                    copies.local(s.at[:, pl.ds(d * depth, depth)], slot[n % 2], tracked=False)
-                    for s, slot in self.pairs
+                    copies.local(s.at[:, at], slot[n % 2], tracked=False) for s, slot in self.pairs
                 ]
 
         def take(self, n):
@@ -1136,58 +1213,69 @@
             self._load(n + 1)
             return n % 2
 
-    put = []
-
-    def store(stage, target):
-        put.append(copies.local(stage, target, tracked=False))
-
-    def drain(left):
-        while len(put) > left:
-            put.pop(0).wait()
-
-    stream_in = Columns([(full1, slots), (prefix1, slots_pre)], groups * shares)
-    count = 0
-    for g in range(groups)[::-1]:
-        for d in range(shares):
-            at = stream_in.take(count)
-            drain(1)
-            which = pl.ds(g * wide, wide)
+    groups_first = [
+        n for g in range(groups)[::-1] for n in far_first if places.offsets[n][1] == g
+    ]
+    wanted = [(n, i, j) for n in groups_first for i, j in GradScatter.ORDER]
+    stream_in = Columns([(full1, slots), (prefix1, slots_pre)], [share_of(*w) for w in wanted])
+    put = {}
+
+    def settle(scatter, todo, number):
+        if number in put:
+            put.pop(number).wait()
+            scatter.send(*todo[number])
+
+    def in_pieces(numbers):
+        for number in numbers:
+            n, i, j = wanted[number]
+            at = stream_in.take(number)
+            which = pl.ds(places.offsets[n][1] * wide, wide)
             value = dot(slots[at][...], dproj[:, which], ((0,), (0,)))
             if prefix_rows:
                 value = value + dot(slots_pre[at][...], dprefix[:, which], ((0,), (0,)))
-            stage_in[count % 2] = value.astype(BF16)
-            store(stage_in.at[count % 2], in_parts.at[g * shares + d])
-            count += 1
-        drain(0)
-        for n in far_first:
-            if places.offsets[n][1] == g:
-                into.start(n)
-    stream_out = Columns([(full_dres, slots)], shares)
-    for d in range(shares):
-        at = stream_out.take(d)
-        for g in range(groups):
-            drain(1)
-            slot = (d * groups + g) % 2
-            stage_out[slot] = dot(
-                att[:, g * cols : (g + 1) * cols], slots[at][...], ((0,), (0,))
-            ).astype(BF16)
-            store(stage_out.at[slot], out_parts.at[g * shares + d])
-    drain(0)
-    for n in far_first:
-        out.start(n)
+            stage_in[number % 2] = value.astype(BF16)
+            put[number] = copies.local(
+                stage_in.at[number % 2], in_parts.at[into.index(n, i, j)], tracked=False
+            )
+            settle(into, wanted, number - 1)
+        settle(into, wanted, numbers[-1])
+
+    hidden = up_parts.shape[2]
+    far_ones = [n for n in far_first if places.offsets[n][1] == groups - 1]
+    near_ones = [n for n in far_first if places.offsets[n][1] != groups - 1]
+    in_pieces(range(4 * len(far_ones)))
     fold(0, dproj, 0, dnormed1.at[0])
-    for n in far_first:
-        if places.offsets[n][1] == groups - 1:
-            into.middle(n)
+    into.middle(*far_ones)
+    if near_ones:
+        in_pieces(range(4 * len(far_ones), len(wanted)))
+    into.last(*[n for n in far_ones if n])
     fold(1, dproj, length, dnormed1.at[1], False)
-    for n in far_first:
-        if places.offsets[n][1] != groups - 1:
-            into.middle(n)
-    for n in far_first:
-        if n and places.offsets[n][1] == groups - 1:
-            into.last(n)
-    for n in far_first:
-        out.middle(n)
+    todo = [(n, i, j) for i, j in GradScatter.ORDER for n in groups_first]
+    stream_out = Columns([(full_dres, slots)], [share_of(*w) for w in todo])
+    put.clear()
+    for number, (n, i, j) in enumerate(todo):
+        at = stream_out.take(number)
+        first = places.offsets[n][1] * cols
+        stage_out[number % 2] = dot(
+            att[:, first : first + cols], slots[at][...], ((0,), (0,))
+        ).astype(BF16)
+        put[number] = copies.local(
+            stage_out.at[number % 2], out_parts.at[out.index(n, i, j)], tracked=False
+        )
+        settle(out, todo, number - 1)
+    settle(out, todo, len(todo) - 1)
+    folds.finish()
+    here = [
+        copies.local(rows_in, c_send, tracked=False),
+        copies.local(
+            full_dres.at[pl.ds(0, size), :], c_recv.at[pl.ds(0, size), :], tracked=False
+        ),
+        copies.local(
+            full_dres.at[pl.ds(length, size), :], c_recv.at[pl.ds(size, size), :], tracked=False
+        ),
+    ]
+    into.middle(*near_ones)
+    into.last(*[n for n in near_ones if n])
     dproj_sums[...] = jnp.zeros_like(dproj_sums)
 
     def add_rows(t):
@@ -1199,19 +1287,94 @@
         dproj_sums[1:2, :] += jnp.sum(dprefix[pl.ds(t, size), :].astype(F32), axis=0, keepdims=True)
 
     in_tiles(prefix_rows, size, add_prefix)
-    up.total()
-    for n in far_first:
-        if (n, "t") not in into.steps:
-            into.last(n)
-    for n in far_first:
-        out.last(n)
-    for r in range(2):
+    bias_send[...] = jnp.zeros_like(bias_send)
+    for g in range(groups):
+        base = g * wide
+        bias_send[g, 0:1, :cols] = dproj_sums[0:1, base : base + cols]
+        bias_send[g, 0:1, cols : 2 * cols] = (
+            dproj_sums[0:1, base + 2 * cols : base + wide] + dproj_sums[1:2, base + 2 * cols : base + wide]
+        )
+        bias_send[g, 0:1, 2 * cols :] = up_sums[0:1, g * hidden : (g + 1) * hidden]
+    bias_steps = [
+        copies.remote(bias_send.at[g], bias_turn.at[g - 1], places.further((0, -g)))
+        for g in range(1, groups)
+    ]
+    out.middle(*far_first)
+    up.last(0)
+
+    all_sums[...] = jnp.zeros_like(all_sums)
+    all_sums[0:4, :] = sums2[...]
+    chunk = min(64, size)
+    for copy in here:
+        copy.wait()
+    for r in (1, 0):
+        if r == 0:
+            out.last(*far_first[:-1])
+            for k in range(1, groups):
+
+                @pl.when(places.g + k < groups)
+                def _():
+                    home[k - 1].wait_recv()
+                    dnormed1[0] = (
+                        dnormed1[0].astype(F32) + returned[k - 1].astype(F32)
+                    ).astype(BF16)
+
+                pl.when(places.g >= k)(home[k - 1].wait_send)
         folded[r].wait_recv()
+
+        def norm_rows(t):
+            at = pl.ds(t, chunk)
+            grad = dnormed1[r, at, :].astype(F32) + h_recv[r, at, :].astype(F32)
+            scaled, inverse = stats(c_send[pl.ds(r * size + t, chunk), :].astype(F32))
+            value = c_recv[pl.ds(r * size + t, chunk), :].astype(F32) + norm_back(
+                grad, scaled, inverse, wide_ref[0:1]
+            )
+            dnormed1[r, at, :] = value.astype(BF16)
+            all_sums[4:5, :] += jnp.sum(grad * scaled, axis=0, keepdims=True)
+            all_sums[5:6, :] += jnp.sum(grad, axis=0, keepdims=True)
+
+        in_tiles(size, chunk, norm_rows)
+
+    for copy in bias_steps:
+        copy.wait_recv()
+    bias_sums[...] = functools.reduce(
+        jnp.add, [bias_send[0]] + [bias_turn[g - 1] for g in range(1, groups)]
+    )
+    waiting = [up.total, lambda: into.last(0), lambda: out.last(0)]
+    stages = [("c", 2), ("h", 2), ("g", groups), ("b", 2), ("a", 2), ("e", extra)]
+    for number, (axis, count) in enumerate(stages):
+        if count == 1:
+            continue
+        pairs = [(all_sums, sum_send.at[number], sum_recv.at[number])]
+        if axis in DP:
+            pairs.append((bias_sums, bias_out.at[number], bias_recv.at[number]))
+        me = lax.axis_index(axis)
+        steps = []
+        for values, sending, coming in pairs:
+            sending[...] = values[...]
+            for k in range(1, count):
+                partner = {axis: lax.rem(me + k, count)}
+                steps.append(copies.remote(sending, coming.at[k - 1], partner))
+        if waiting:
+            waiting.pop(0)()
+        for copy in steps:
+            copy.wait_recv()
+        for values, sending, coming in pairs:
+            if count == 2:
+                values[...] = sending[...] + coming[0]
+            else:
+                total = jnp.zeros(values.shape, F32)
+                for device in range(count):
+                    back_by = lax.rem(me - device + count, count)
+                    other = coming[jnp.maximum(back_by - 1, 0)]
+                    total = total + jnp.where(back_by == 0, sending[...], other)
+                values[...] = total
+    for job in waiting:
+        job()
+    for copy in mixed_steps:
+        copy.wait_recv()
     out.total()
     into.total()
-    for k in range(1, groups):
-        pl.when(places.g + k < groups)(home[k - 1].wait_recv)
-        pl.when(places.g >= k)(home[k - 1].wait_send)
     copies.finish()
 
 
@@ -1221,7 +1384,7 @@
     )
 
 
-def run_middle(split, full2, full_cot, up_all, down_all, resid, wide, bias_up, hidden, depth):
+def run_middle(split, full2, cots, up_all, down_all, resid, wide, bias_up, hidden, depth):
     extra, groups = split
     sources = extra * groups
     size, width = resid.shape[1:]
@@ -1234,7 +1397,7 @@
     return pl.pallas_call(
         functools.partial(middle_kernel, extra, groups),
         in_specs=[anywhere] * 4 + [inside] * 3,
-        out_specs=[inside, anywhere, inside, anywhere, inside, inside] + [anywhere] * 5,
+        out_specs=[inside, anywhere, inside, anywhere, inside, inside] + [anywhere] * 7,
         out_shape=[
             shape((2, size, width), BF16),
             shape((2 * length, width), BF16),
@@ -1242,6 +1405,8 @@
             shape((shares, depth, hidden), BF16),
             shape((4, width), F32),
             shape((1, all_hidden), F32),
+            shape((2, size, width), BF16),
+            shape((2 * length, width), BF16),
             shape((2 * length, all_hidden), BF16),
             shape((2 * length, all_hidden), BF16),
             shape((shares, hidden, depth), BF16),
@@ -1255,14 +1420,14 @@
             pltpu.VMEM((2, size, width), BF16),
             pltpu.VMEM((2 * size, width), BF16),
             pltpu.VMEM((2 * size, width), BF16),
-            pltpu.VMEM((size, width), BF16),
-            pltpu.VMEM((4, size, width), BF16),
+            pltpu.VMEM((2, size, width), BF16),
+            pltpu.VMEM((2, size, width), BF16),
             pltpu.VMEM((2, size, width), BF16),
             pltpu.VMEM((2, hidden, depth), BF16),
         ]
         + GradScatter.working(sources, hidden, depth)
         + [
-            pltpu.VMEM((3, hidden // 2, depth), BF16),
+            pltpu.VMEM((2, 3, hidden // 2, depth), BF16),
             pltpu.SemaphoreType.DMA((sources * 8 + 16,)),
             pltpu.SemaphoreType.DMA((sources * 8 + 16,)),
             pltpu.SemaphoreType.DMA((sources * 16 + 6 * shares + 80,)),
@@ -1270,10 +1435,10 @@
         ],
         compiler_params=kernel_params(1),
         cost_estimate=pl.CostEstimate(flops=10**11, bytes_accessed=10**8, transcendentals=10**6),
-    )(full2, full_cot, up_all, down_all, resid, wide, bias_up)
-
-
-def run_last(split, quarter, proj, prefix_proj, att, full_dres, out_all, in_all, full1, prefix1, up_parts, lse):
+    )(full2, cots, up_all, down_all, resid, wide, bias_up)
+
+
+def run_last(split, quarter, proj, prefix_proj, att, full_dres, out_all, in_all, full1, prefix1, up_parts, mixed_far, rows, lse, norms, sums2, up_sums):
     extra, groups = split
     sources = extra * groups
     shares = sources * 4
@@ -1283,22 +1448,23 @@
     depth, hidden = up_parts.shape[1:]
     wide, all_wide = 3 * cols, 3 * cols * groups
     prefix_rows = prefix1.shape[0]
+    most = max(extra, groups, 2) - 1
     shape = jax.ShapeDtypeStruct
     anywhere = pl.BlockSpec(memory_space=pl.ANY)
     inside = pl.BlockSpec(memory_space=pltpu.VMEM)
     heads_rows = [pltpu.VMEM((length, HDIM), BF16)] * 2 + [pltpu.VMEM((length, HDIM), F32)] * 2
     return pl.pallas_call(
         functools.partial(last_kernel, extra, groups, quarter),
-        in_specs=[anywhere] * 9 + [inside],
-        out_specs=[inside] * 7 + [anywhere] * 8,
+        in_specs=[anywhere] * 11 + [inside] * 4,
+        out_specs=[inside] * 6 + [anywhere] * 9,
         out_shape=[
             shape((depth, wide), F32),
             shape((cols, depth), F32),
             shape((depth, hidden), F32),
             shape((2, size, width), BF16),
-            shape((1 + groups, size, width), BF16),
-            shape((max(groups - 1, 1), size, width), BF16),
-            shape((2, all_wide), F32),
+            shape((8, width), F32),
+            shape((8, 2 * cols + hidden), F32),
+            shape((2, size, width), BF16),
             shape((shares, depth, wide), BF16),
             shape((shares, cols, depth), BF16),
         ]
@@ -1320,8 +1486,17 @@
         + [
             pltpu.VMEM((2 * size, width), BF16),
             pltpu.VMEM((2 * size, width), BF16),
-            pltpu.VMEM((size, width), BF16),
+            pltpu.VMEM((2, size, width), BF16),
+            pltpu.VMEM((1 + groups, size, width), BF16),
             pltpu.VMEM((max(groups - 1, 1), size, width), BF16),
+            pltpu.VMEM((max(groups - 1, 1), size, width), BF16),
+            pltpu.VMEM((2, all_wide), F32),
+            pltpu.VMEM((6, 8, width), F32),
+            pltpu.VMEM((6, most, 8, width), F32),
+            pltpu.VMEM((groups, 8, 2 * cols + hidden), F32),
+            pltpu.VMEM((6, most, 8, 2 * cols + hidden), F32),
+            pltpu.VMEM((6, 8, 2 * cols + hidden), F32),
+            pltpu.VMEM((max(groups - 1, 1), 8, 2 * cols + hidden), F32),
             pltpu.VMEM((2, depth, wide), BF16),
             pltpu.VMEM((2, cols, depth), BF16),
         ]
@@ -1329,15 +1504,15 @@
         + GradScatter.working(sources, cols, depth)
         + GradScatter.working(sources, depth, hidden)
         + [
-            pltpu.VMEM((3, depth // 2, max(wide, hidden, depth)), BF16),
-            pltpu.SemaphoreType.DMA((sources * 24 + 4 * groups + 16,)),
-            pltpu.SemaphoreType.DMA((sources * 24 + 4 * groups + 16,)),
+            pltpu.VMEM((2, 3, depth // 2, max(wide, hidden, depth)), BF16),
+            pltpu.SemaphoreType.DMA((sources * 24 + 12 * groups + 48,)),
+            pltpu.SemaphoreType.DMA((sources * 24 + 12 * groups + 48,)),
             pltpu.SemaphoreType.DMA((sources * 48 + 10 * shares + 32,)),
             pltpu.SemaphoreType.REGULAR,
         ],
         compiler_params=kernel_params(2),
         cost_estimate=pl.CostEstimate(flops=10**11, bytes_accessed=10**8, transcendentals=10**7),
-    )(proj, prefix_proj, att, full_dres, out_all, in_all, full1, prefix1, up_parts, lse)
+    )(proj, prefix_proj, att, full_dres, out_all, in_all, full1, prefix1, up_parts, mixed_far, rows, lse, norms, sums2, up_sums)
 
 
 def local(
@@ -1372,7 +1547,7 @@
     def unpick(first, second):
         return jnp.where(single == 0, jnp.stack([first, second]), jnp.stack([second, first]))
 
-    rows = [r.astype(F32) for r in pick(tokens)]
+    picked = jnp.stack(pick(tokens))
     cots = pick(cotangent)
 
     no_bias = jnp.zeros_like(in_bias[0])
@@ -1381,78 +1556,44 @@
     wide = jnp.stack([first_gain, first_shift, out_bias, second_gain, second_shift, down_bias])
     (
         in_all, out_all, up_all, down_all, biases, full1, prefix1, proj, proj_prefix, attended, lse,
-        resid, full2, full_cot,
+        resid, full2,
     ) = run_forward(
         split,
         quarter,
-        jnp.stack(pick(tokens)),
+        picked,
         in_weight.reshape(depth, 3 * cols),
         out_weight,
         up_weight,
         down_weight,
         wide,
         biases,
-        jnp.stack(cots),
     )
     bias_up = biases[:, 0, 3 * cols :].reshape(1, -1)
     length = 4 * size
-    scaled1, inverse1 = zip(*[stats(x) for x in rows])
-
-    mixed, full_dres, grad_down, up_parts, sums2, grad_up_bias = run_middle(
-        split, full2, full_cot, up_all, down_all, resid, wide, bias_up, hidden, depth
-    )[:6]
-    dres = [full_dres[r * length : r * length + size].astype(F32) for r in range(2)]
-
-    grad_in, grad_out, grad_up, kept, halves_far, returned, dproj_sums = run_last(
-        split, quarter, proj, proj_prefix, attended, full_dres, out_all, in_all, full1, prefix1, up_parts, lse
+
+    mixed, full_dres, grad_down, up_parts, sums2, up_sums, mixed_far = run_middle(
+        split, full2, jnp.stack(cots), up_all, down_all, resid, wide, bias_up, hidden, depth
     )[:7]
-    dnormed1 = [kept[r].astype(F32) + halves_far[r].astype(F32) for r in range(2)]
-    at_g = lax.axis_index("g")
-    for k in range(1, groups):
-        dnormed1[0] += jnp.where(at_g + k < groups, returned[k - 1].astype(F32), 0.0)
-    grad_in = grad_in.reshape(in_weight.shape)
-    tokens_grad, sums1 = [], []
-    for r in range(2):
-        tokens_grad.append(
-            (dres[r] + norm_back(dnormed1[r], scaled1[r], inverse1[r], first_gain)).astype(BF16)
-        )
-        sums1.append(jnp.stack([jnp.sum(dnormed1[r] * scaled1[r], 0), jnp.sum(dnormed1[r], 0)]))
-
-    sums = dproj_sums.reshape(2, groups, 3, cols)
-    grad_q_bias = sums[0, :, 0]
-    grad_v_bias = sums[0, :, 2] + sums[1, :, 2]
-
-    def to_owner(x):
-        share = x.reshape(groups, -1)
-        return functools.reduce(
-            jnp.add,
-            [share[0]] + [turn(share[g], split, (0, (-g) % groups)) for g in range(1, groups)],
-        )
-
-    def sum_over(x, axes):
-        for axis in axes:
-            x = sum_axis(x, axis)
-        return x
-
-    early = sum_over(sums2, ("c", "h", "g") + DP)
-    grad_up_bias = sum_over(to_owner(grad_up_bias), DP)
-    late = sum_over(sums1[0] + sums1[1], ("c", "h", "g") + DP)
-    grad_in_bias = sum_over(jnp.stack([to_owner(grad_q_bias), to_owner(grad_v_bias)]), DP)
+    grad_in, grad_out, grad_up, tokens_grad, all_sums, bias_sums, mixed_recv = run_last(
+        split, quarter, proj, proj_prefix, attended, full_dres, out_all, in_all, full1, prefix1, up_parts,
+        mixed_far, picked.reshape(2 * size, width), lse, wide, sums2, up_sums,
+    )[:7]
+    mixed = (resid + mixed.astype(F32) + mixed_recv.astype(F32) + down_bias).astype(BF16)
     return (
         unpick(*mixed),
         unpick(*tokens_grad),
-        late[0],
-        late[1],
-        grad_in,
-        grad_in_bias,
+        all_sums[4],
+        all_sums[5],
+        grad_in.reshape(in_weight.shape),
+        bias_sums[0, : 2 * cols].reshape(2, cols),
         grad_out,
-        early[0],
-        early[1],
-        early[2],
+        all_sums[0],
+        all_sums[1],
+        all_sums[2],
         grad_up,
-        grad_up_bias,
+        bias_sums[0, 2 * cols :],
         grad_down,
-        early[3],
+        all_sums[3],
     )
 
 

time: 910 us -> 872 us (0.958)
  starting transfers between devices: 43.9 us -> 0 us
  Pallas kernels: 808 us -> 822 us
  other arithmetic: 23.8 us -> 11.4 us
    ppermute x17 -> x0, starting transfers between devices: 43.9 us -> none  [the longest x14 35 us: flip(): return lax.ppermute(x, axis, [(0, 1), (1, 0)])]
    pallas_call x1, Pallas kernels: 295 us -> 259 us  [run_forward(): pl.pallas_call(functools.partial(layer_forward, extra, groups, quarter),...]
    pallas_call x1, Pallas kernels: 265 us -> 299 us  [run_middle(): pl.pallas_call(functools.partial(middle_kernel, extra, groups), in_specs=...]
    pallas_call x1, Pallas kernels: 247 us -> 264 us  [run_last(): pl.pallas_call(functools.partial(last_kernel, extra, groups, quarter), in...]
    reduce_sum x4 -> x0, other arithmetic: 11.5 us -> none  [the longest x1 3.39 us: local(): jnp.sum(dnormed1[r] * scaled1[r], 0)]
  transfers between devices with their start and end apart: 17 -> 0, of which waited for: 4 -> 0; matrix products, arithmetic and copies ran while one was open for 3% -> 0% of each run, Pallas kernels for 27% -> 0%
where the time goes in v4:
time: 872 us; the launch traced here: 860 us
  Pallas kernels  822 us (94%)
  local copies, waits for them, and re-layouts  25.4 us (3%)
  other arithmetic  11.4 us (1%)
    pallas_call x1, Pallas kernels, run_middle(): pl.pallas_call(functools.partial(middle_kernel, extra, groups), in_specs=...  299 us
    pallas_call x1, Pallas kernels, run_last(): pl.pallas_call(functools.partial(last_kernel, extra, groups, quarter), in...  264 us
    pallas_call x1, Pallas kernels, run_forward(): pl.pallas_call(functools.partial(layer_forward, extra, groups, quarter),...  259 us

profile of v4, /device:TPU:0, one launch (start us, length us, event | category | flops | bytes accessed | tf_op | source)
XLA Modules:
  0.0 860.4 jit_solution(10668909328776817309)
XLA Ops:
  0.6 0.0 copy-start.1
  0.7 1.4 slice.38
  2.7 0.8 fusion.3
  3.5 0.7 pad_maximum_fusion.2
  4.2 0.6 broadcast_in_dim.8.refs_6_
  4.8 1.5 stack.46.refs_5_.refs_12_
  6.3 1.4 copy.31
  7.7 1.2 copy.32.refs_1_
  8.9 0.0 copy-done.1
  8.9 2.0 constant_dynamic-slice_fusion.1
  10.8 1.5 pad_maximum_fusion.1.refs_1_
  12.3 1.5 pad_maximum_fusion.refs_0_
  13.8 258.7 %shard_map.254 = (bf16[2048,1536]{1,0:T(8,128)(2,1)}, bf16[512,2048]{1,0:T(8,128)(2,1)}, bf16[2048,2048]{1,0:T(8,128)(2,1)}, bf16[2048,2048]{1,0:T(8,128)(2,1)},...) custom-call(bf16[2,256,2048]{2,1,0:T(8,128)(2,1)} %pad_maximum_fusio, ...), custom_call_target="tpu_custom_call" | custom-call | flops 99999997952 | bytes 100000000 | tf_op jit(solution)/shard_map/pallas_call | solution.py:529
  272.6 1.4 slice.41
  274.0 298.9 %shard_map.255 = (bf16[2,256,2048]{2,1,0:T(8,128)(2,1)}, bf16[2048,2048]{1,0:T(8,128)(2,1)}, f32[1024,512]{1,0:T(8,128)}, bf16[8,512,1024]{2,1,0:T(8,128)(2,1)},...) custom-call(bf16[2048,2048]{1,0:T(8,128)(2,1)} %get-tuple-element.42, ...), custom_call_target="tpu_custom_call" | custom-call | flops 99999997952 | bytes 100000000 | tf_op jit(solution)/shard_map/pallas_call | solution.py:1397
  573.0 0.0 copy-start.6
  573.0 264.2 %shard_map.256 = (f32[512,768]{1,0:T(8,128)}, f32[256,512]{1,0:T(8,128)}, f32[512,1024]{1,0:T(8,128)}, bf16[2,256,2048]{2,1,0:T(8,128)(2,1)}, f32[8,2048]{1,0:T(...) custom-call(bf16[2048,1536]{1,0:T(8,128)(2,1)} %get-tuple-element.47, ...), custom_call_target="tpu_custom_call" | custom-call | flops 99999997952 | bytes 100000000 | tf_op jit(solution)/shard_map/pallas_call | solution.py:1456
  837.2 0.0 copy-done.6
  837.2 0.0 copy-start.5
  837.2 4.5 add_convert_fusion
  841.8 0.7 slice_reduce_fusion
  842.5 1.4 slice.48
  843.9 0.6 reshape_squeeze.7
  844.4 0.0 copy-done.5
  844.4 0.6 fusion.2
  845.1 3.0 copy.33
  848.1 3.0 copy.34
  851.1 0.2 fusion.1
  851.4 0.0 copy-start
  851.4 1.6 maximum_select_fusion
  853.0 0.8 copy-done
  853.7 0.2 fusion
  854.0 0.0 copy-start.4
  854.0 0.0 copy-start.3
  854.0 1.6 maximum_select_fusion.1
  855.6 0.0 copy-done.4
  855.6 0.8 copy.38
  856.4 0.1 copy-done.3
  856.5 0.0 copy-start.2
  856.5 1.3 copy.39
  857.8 1.0 copy-done.2
  858.8 1.3 copy.40
  (1 shorter events, 0.0 us)
Async XLA Ops:
  0.6 8.2 copy-start.1
  573.0 264.2 %copy-start.6 = (f32[2048]{0:T(1024)S(1)}, f32[2048]{0:T(1024)}, u32[]{:S(2)}) copy-start(f32[2048]{0:T(1024)} %param.28) | copy-start | bytes 24580
  837.2 7.2 copy-start.5
  851.4 2.4 copy-start
  854.0 1.6 copy-start.4
  854.0 2.5 copy-start.3
  856.5 2.3 copy-start.2

commit v5 on v4

--- a/solution.py
+++ b/solution.py
@@ -815,9 +815,12 @@
     where = [pl.ds(r * length + s * size, size) for r, s in order]
     places.barrier()
     spread_cot = []
+    placed = []
     for r in range(2):
-        copies.local(own_cots.at[r], full_cot.at[pl.ds(r * length, size), :], tracked=False).wait()
         spread_cot.append(Spread(copies, places, own_cots.at[r], full_cot, r * length, size))
+        placed.append(load(own_cots.at[r], full_cot.at[pl.ds(r * length, size), :]))
+    for copy in placed:
+        copy.wait()
 
     def cot_ready(n):
         r, slot = order[n]
@@ -1138,8 +1141,7 @@
     mixed_steps = [
         copies.remote(mixed_far.at[r], mixed_recv.at[r], places.to_h) for r in range(2)
     ]
-    for copy in here:
-        copy.wait()
+    here[0].wait()
 
     def attended_grad(r):
         for slot in range(4):
@@ -1172,6 +1174,8 @@
 
     attended_grad(0)
     attended_grad(1)
+    for copy in here[1:]:
+        copy.wait()
     attention_back(0, None, lambda: up.middle(*far_first))
     up.last(*far_first[:-1])
     for k in range(1, groups):

time: 872 us -> 872 us (level)
  no operation moved by 1% of the time
where the time goes in v5:
time: 872 us; the launch traced here: 859 us
  Pallas kernels  821 us (94%)
  local copies, waits for them, and re-layouts  25.4 us (3%)
  other arithmetic  11.4 us (1%)
    pallas_call x1, Pallas kernels, run_middle(): pl.pallas_call(functools.partial(middle_kernel, extra, groups), in_specs=...  298 us
    pallas_call x1, Pallas kernels, run_last(): pl.pallas_call(functools.partial(last_kernel, extra, groups, quarter), in...  264 us
    pallas_call x1, Pallas kernels, run_forward(): pl.pallas_call(functools.partial(layer_forward, extra, groups, quarter),...  259 us

profile of v5, /device:TPU:0, one launch (start us, length us, event | category | flops | bytes accessed | tf_op | source)
XLA Modules:
  0.0 859.5 jit_solution(9826162262177672982)
XLA Ops:
  0.6 0.0 copy-start.1
  0.7 1.4 slice.38
  2.7 0.8 fusion.3
  3.5 0.7 pad_maximum_fusion.2
  4.2 0.6 broadcast_in_dim.8.refs_6_
  4.8 1.5 stack.46.refs_5_.refs_12_
  6.3 1.4 copy.31
  7.7 1.2 copy.32.refs_1_
  8.9 0.0 copy-done.1
  8.9 2.0 constant_dynamic-slice_fusion.1
  10.8 1.5 pad_maximum_fusion.1.refs_1_
  12.3 1.5 pad_maximum_fusion.refs_0_
  13.8 258.7 %shard_map.254 = (bf16[2048,1536]{1,0:T(8,128)(2,1)}, bf16[512,2048]{1,0:T(8,128)(2,1)}, bf16[2048,2048]{1,0:T(8,128)(2,1)}, bf16[2048,2048]{1,0:T(8,128)(2,1)},...) custom-call(bf16[2,256,2048]{2,1,0:T(8,128)(2,1)} %pad_maximum_fusio, ...), custom_call_target="tpu_custom_call" | custom-call | flops 99999997952 | bytes 100000000 | tf_op jit(solution)/shard_map/pallas_call | solution.py:529
  272.6 1.4 slice.41
  274.0 297.8 %shard_map.255 = (bf16[2,256,2048]{2,1,0:T(8,128)(2,1)}, bf16[2048,2048]{1,0:T(8,128)(2,1)}, f32[1024,512]{1,0:T(8,128)}, bf16[8,512,1024]{2,1,0:T(8,128)(2,1)},...) custom-call(bf16[2048,2048]{1,0:T(8,128)(2,1)} %get-tuple-element.42, ...), custom_call_target="tpu_custom_call" | custom-call | flops 99999997952 | bytes 100000000 | tf_op jit(solution)/shard_map/pallas_call | solution.py:1401
  571.9 0.0 copy-start.6
  571.9 264.4 %shard_map.256 = (f32[512,768]{1,0:T(8,128)}, f32[256,512]{1,0:T(8,128)}, f32[512,1024]{1,0:T(8,128)}, bf16[2,256,2048]{2,1,0:T(8,128)(2,1)}, f32[8,2048]{1,0:T(...) custom-call(bf16[2048,1536]{1,0:T(8,128)(2,1)} %get-tuple-element.47, ...), custom_call_target="tpu_custom_call" | custom-call | flops 99999997952 | bytes 100000000 | tf_op jit(solution)/shard_map/pallas_call | solution.py:1460
  836.3 0.0 copy-done.6
  836.3 0.0 copy-start.5
  836.3 4.5 add_convert_fusion
  840.8 0.7 slice_reduce_fusion
  841.6 1.4 slice.48
  842.9 0.6 reshape_squeeze.7
  843.5 0.0 copy-done.5
  843.5 0.6 fusion.2
  844.1 3.0 copy.33
  847.2 3.0 copy.34
  850.2 0.2 fusion.1
  850.4 0.0 copy-start
  850.4 1.6 maximum_select_fusion
  852.0 0.8 copy-done
  852.8 0.2 fusion
  853.0 0.0 copy-start.4
  853.0 0.0 copy-start.3
  853.0 1.6 maximum_select_fusion.1
  854.6 0.0 copy-done.4
  854.6 0.8 copy.38
  855.4 0.1 copy-done.3
  855.6 0.0 copy-start.2
  855.6 1.3 copy.39
  856.9 1.0 copy-done.2
  857.9 1.3 copy.40
  (1 shorter events, 0.0 us)
Async XLA Ops:
  0.6 8.2 copy-start.1
  571.9 264.4 %copy-start.6 = (f32[2048]{0:T(1024)S(1)}, f32[2048]{0:T(1024)}, u32[]{:S(2)}) copy-start(f32[2048]{0:T(1024)} %param.28) | copy-start | bytes 24580
  836.3 7.2 copy-start.5
  850.4 2.4 copy-start
  853.0 1.6 copy-start.4
  853.0 2.5 copy-start.3
  855.6 2.3 copy-start.2
